TPU v7x, 32 devices: a whole 2x2x4 slice. The times are simulated.
32 devices in a mesh: dp: 4 (over x, core), tm: 8 (over z, y).
Axes of the slice: x: 2, y: 2, z: 4, core: 2. Of those that a mesh axis runs over, the one named last changes fastest.
Arguments:
- queries: bfloat16 [4, 2048, 1152], P('dp', 'tm'), may hold values from -96 to 96
- keys: bfloat16 [4, 2048, 1152], P('dp', 'tm'), may hold values from -6 to 6
- values: bfloat16 [4, 2048, 1152], P('dp', 'tm'), may hold values from -6 to 6
- out_grad: bfloat16 [4, 2048, 1152], P('dp', 'tm'), may hold values from -6 to 6
- lengths: int32 [4], P('dp'), may hold values from 512 to 2048, as said below
- rel_bias: float32 [12, 768], replicated, may hold values from -4 to 4
Outputs:
- query_grad: bfloat16 [4, 2048, 1152], P('dp', 'tm')
- key_grad: bfloat16 [4, 2048, 1152], P('dp', 'tm')
- value_grad: bfloat16 [4, 2048, 1152], P('dp', 'tm')
- bias_grad: float32 [12, 768], replicated
Inputs may be any that keep to these rules, and one draw needn't show every extreme that they name: Every recording's valid frames are its first lengths[r] frames; some recording is valid to its end.
All inputs are finite; a program needn't handle non-finite values.
Results may differ from a plain program's by a relative error of at most 0.007.
Values may be sent and summed in bfloat16 or wider, within the bound.
No kernel may reach another device: no remote copies, remote signals or barrier semaphores. Data moves between devices by JAX's collectives and lax.ppermute only.
A program may use at most 128 MiB of HBM per device.

v0:
```python
import functools

import jax
import jax.numpy as jnp
import numpy as np
from jax import lax
from jax.experimental import pallas as pl
from jax.experimental.pallas import tpu as pltpu
from jax.sharding import PartitionSpec as P

BLOCK = 256
HALF = jnp.bfloat16
LOG2E = float(np.log2(np.e))
MASKED = -(2.0**30)
GROUP_HEADS = 4
GROUP_LANES = 384
WINDOWS = ((0, 128), (0, 256), (128, 256), (256, 128))

NT = (((1,), (1,)), ((), ()))
NN = (((1,), (0,)), ((), ()))
TN = (((0,), (0,)), ((), ()))


def dot(a, b, dims):
    return lax.dot_general(a, b, dims, preferred_element_type=jnp.float32)


def shifted(x, axis, by):
    count = lax.axis_size(axis)
    pairs = [(i, i + by) for i in range(count) if 0 <= i + by < count]
    return lax.ppermute(x, axis, pairs)


def head_mask(j, head_width, dtype):
    lo, width = WINDOWS[j]
    lane = lax.broadcasted_iota(jnp.int32, (1, width), 1) + lo
    inside = (lane >= j * head_width) & (lane < (j + 1) * head_width)
    return jnp.where(inside, 1.0, 0.0).astype(dtype)


def live_rows(count, width, dtype):
    row = lax.broadcasted_iota(jnp.int32, (BLOCK, width), 0)
    return jnp.where(row < count, 1.0, 0.0).astype(dtype)


def skew(row):
    base = pltpu.roll(jnp.broadcast_to(row, (8, 2 * BLOCK)), 0, 1, stride=1, stride_axis=0)
    turns = [pltpu.roll(base, 8 * a, 1) if a else base for a in range(16)]
    near = [turn[:, BLOCK:] for turn in turns]
    far = [turn[:, BLOCK - 128 : 2 * BLOCK - 128] for turn in turns]
    return jnp.concatenate(near + far, axis=0)


def unskew(matrix):
    zeros = jnp.zeros((8, 128), jnp.float32)
    total = None
    for a in range(16):
        upper = matrix[8 * a : 8 * a + 8]
        lower = matrix[128 + 8 * a : 136 + 8 * a]
        part = jnp.concatenate(
            [zeros, lower[:, :128], upper[:, :128] + lower[:, 128:], upper[:, 128:]], axis=1
        )
        if a:
            part = pltpu.roll(part, 2 * BLOCK - 8 * a, 1)
        total = part if total is None else total + part
    return total


def flipped(rows):
    tiles = rows.shape[1] // 128
    a = lax.broadcasted_iota(jnp.int32, (128, 128), 0)
    b = lax.broadcasted_iota(jnp.int32, (128, 128), 1)
    swap = jnp.where(a + b == 127, 1.0, 0.0).astype(jnp.bfloat16)
    total = None
    for _ in range(3):
        piece = rows.astype(jnp.bfloat16)
        rows = rows - piece.astype(jnp.float32)
        moved = jnp.concatenate(
            [dot(piece[:, 128 * t : 128 * t + 128], swap, NN) for t in reversed(range(tiles))], axis=1
        )
        total = moved if total is None else total + moved
    return total


def window(ref, j):
    lo, width = WINDOWS[j]
    return ref[:BLOCK, lo : lo + width]


def add_window(ref, j, value):
    lo, width = WINDOWS[j]
    for tile in range(0, width, 128):
        at = slice(lo + tile, lo + tile + 128)
        piece = value[:, tile : tile + 128]
        if (lo + tile) // 128 == j:
            ref[:, at] = piece
        else:
            ref[:, at] += piece


def live_tiles(count):
    rows = live_rows(count, 128, jnp.bfloat16)
    return {128: rows, 256: jnp.concatenate([rows, rows], axis=1)}


def put_lines(ref, j, lines):
    for tile in range(4):
        ref[0, tile, 8 * j : 8 * j + 8, :] = lines[:, 128 * tile : 128 * tile + 128]


def get_lines(ref, group, r):
    rows = pl.ds(r, GROUP_HEADS, stride=8)
    return jnp.concatenate([ref[group, tile, rows, :] for tile in range(4)], axis=1)


def lined(ref, group):
    total = get_lines(ref, group, 0)
    for r in range(1, 8):
        total = total + pltpu.roll(get_lines(ref, group, r), 2 * BLOCK - r, 1)
    return total


def pack_rows(ref, rows):
    high = rows.astype(HALF).astype(jnp.float32)
    low = rows - high
    main = jnp.concatenate([high[:12], low[4:8]], axis=0)
    side = jnp.concatenate([low[8:12, :128], low[8:12, 128:], jnp.zeros((8, 128), jnp.float32)], axis=0)
    ref[...] = jnp.concatenate([main, side], axis=1).astype(HALF)


def unpack_rows(ref):
    strip = ref[...].astype(jnp.float32)
    m = strip[:4, :BLOCK]
    total = strip[4:8, :BLOCK] + strip[12:16, :BLOCK]
    mixed = strip[8:12, :BLOCK] + jnp.concatenate([strip[:4, BLOCK:], strip[4:8, BLOCK:]], axis=1)
    return m, total, mixed


def reference_value(x):
    return jnp.max(x, axis=0, keepdims=True).astype(HALF).astype(jnp.float32)


def add_products(j, qm, gm, km, p, ds, dq_acc, dk_acc, dv_acc):
    pb = p.astype(HALF)
    dsb = ds.astype(HALF)
    add_window(dv_acc, j, dot(pb, gm, NN))
    add_window(dk_acc, j, dot(dsb, qm, NN))
    add_window(dq_acc, j, dot(dsb, km, TN))


def own_stats_kernel(
    head_width, group, live_ref, q_ref, g_ref, k_ref, v_ref, bias_ref, *refs
):
    if group == 0:
        stats_ref, e_ref, dp_ref, chunk_ref, flip_ref = refs
        flip_ref[...] = flipped(bias_ref[...]) * LOG2E
    else:
        stats_ref, e_ref, dp_ref, chunk_ref = refs[-4:]
        flip_ref = bias_ref

    scale = head_width**-0.5 * LOG2E
    live = live_ref[0]
    key_live = lax.broadcasted_iota(jnp.int32, (BLOCK, BLOCK), 0) < live
    rows = live_tiles(live)
    for j in range(GROUP_HEADS):
        mask = head_mask(j, head_width, HALF)
        head = group * GROUP_HEADS + j
        qm = window(q_ref, j) * mask
        gm = window(g_ref, j) * mask * rows[WINDOWS[j][1]]
        x = dot(window(k_ref, j), qm, NT) * scale + skew(flip_ref[head : head + 1, : 2 * BLOCK])
        x = jnp.where(key_live, x, MASKED)
        m = reference_value(x)
        e = jnp.exp2(x - m)
        dp = dot(window(v_ref, j), gm, NT)
        e_ref[j] = e
        dp_ref[j] = dp
        stats_ref[0, j : j + 1, :] = m
        stats_ref[0, 4 + j : 5 + j, :] = jnp.sum(e, axis=0, keepdims=True)
        stats_ref[0, 8 + j : 9 + j, :] = jnp.sum(e * dp, axis=0, keepdims=True)
    stats_ref[0, 12:16, :] = jnp.zeros((4, BLOCK), jnp.float32)
    chunk_ref[:BLOCK, :] = g_ref[...]
    pack_rows(chunk_ref.at[BLOCK:PACKED, :], stats_ref[0])


def cross_kernel(
    head_width, group, live_ref, q_ref, g_ref, k_ref, v_ref, w_ref, *refs
):
    out_ref, dq_ref, dk_ref, dv_ref, lines_ref, rows_ref, dq_acc, dk_acc, dv_acc = refs[-9:]
    scale = head_width**-0.5 * LOG2E
    live = live_tiles(live_ref[0])
    far_m, far_total, far_mixed = unpack_rows(g_ref.at[BLOCK:PACKED, :])
    for j in range(GROUP_HEADS):
        mask = head_mask(j, head_width, HALF)
        qm = window(q_ref, j) * mask
        gm = window(g_ref, j) * mask * live[WINDOWS[j][1]]
        km = window(k_ref, j) * mask
        x = dot(km, qm, NT) * scale + skew(w_ref[group * GROUP_HEADS + j : group * GROUP_HEADS + j + 1, BLOCK:])
        m_far = far_m[j : j + 1]
        m = jnp.maximum(reference_value(x), m_far)
        e = jnp.exp2(x - m)
        dp = dot(window(v_ref, j), gm, NT)
        shrink = jnp.exp2(m_far - m)
        total = jnp.sum(e, axis=0, keepdims=True) + far_total[j : j + 1] * shrink
        mixed = jnp.sum(e * dp, axis=0, keepdims=True) + far_mixed[j : j + 1] * shrink
        inverse = 1.0 / total
        delta = mixed * inverse
        rows_ref[j : j + 1, :] = m
        rows_ref[4 + j : 5 + j, :] = inverse
        rows_ref[8 + j : 9 + j, :] = delta
        p = e * inverse
        ds = p * (dp - delta)
        put_lines(lines_ref, j, unskew(ds))
        add_products(j, qm, gm, km, p, ds, dq_acc, dk_acc, dv_acc)
    rows_ref[12:16, :] = jnp.zeros((4, BLOCK), jnp.float32)
    pack_rows(out_ref, rows_ref[...])
    scaling = head_width**-0.5
    dq_ref[...] = (dq_acc[...] * scaling).astype(HALF)
    dk_ref[...] = (dk_acc[...] * scaling).astype(HALF)
    dv_ref[...] = dv_acc[...].astype(HALF)


ROW_TILES = 3 * BLOCK // 128


def place(row, tile, parts):
    each = parts[2] // 128
    at = row * ROW_TILES + tile
    return at // each, slice(128 * (at % each), 128 * (at % each) + 128)


def spread_kernel(terms_ref, out_ref):
    total = terms_ref[0]
    for part in range(1, terms_ref.shape[0]):
        total = total + terms_ref[part]
    for part in range(out_ref.shape[0]):
        out_ref[part] = total


def gather_kernel(parts_ref, _, out_ref):
    for row in range(out_ref.shape[0]):
        for tile in range(ROW_TILES):
            part, lanes = place(row, tile, parts_ref.shape)
            out_ref[row : row + 1, 128 * tile : 128 * tile + 128] = parts_ref[part, :, lanes]


def own_kernel(
    groups, head_width, live_ref, q_ref, g_ref, k_ref, e_ref, dp_ref, near_ref, given_ref, dkc_ref, dvc_ref,
    cross_ref, dq_ref, dk_ref, dv_ref, table_ref, dq_acc, dk_acc, dv_acc, lines_ref,
):
    step = pl.program_id(0)
    live = live_tiles(live_ref[0])
    given_m, given_inverse, given_delta = unpack_rows(given_ref)
    for j in range(GROUP_HEADS):
        mask = head_mask(j, head_width, HALF)
        qm = window(q_ref, j) * mask
        gm = window(g_ref, j) * mask * live[WINDOWS[j][1]]
        km = window(k_ref, j) * mask
        m_near = near_ref[0, j : j + 1, :]
        inverse_near = 1.0 / near_ref[0, 4 + j : 5 + j, :]
        inverse = given_inverse[j : j + 1]
        there = inverse > 0.0
        m = jnp.where(there, given_m[j : j + 1], m_near)
        ratio = jnp.exp2(m_near - m) * jnp.where(there, inverse, inverse_near)
        delta = jnp.where(there, given_delta[j : j + 1], near_ref[0, 8 + j : 9 + j, :] * inverse_near)
        p = e_ref[j] * ratio
        ds = p * (dp_ref[j] - delta)
        put_lines(lines_ref.at[pl.ds(step, 1)], j, unskew(ds))
        add_products(j, qm, gm, km, p, ds, dq_acc, dk_acc, dv_acc)
    scaling = head_width**-0.5
    f32 = jnp.float32
    dq_ref[...] = dq_acc[...] * scaling
    dk_ref[...] = (dk_acc[...] * scaling + dkc_ref[...].astype(f32)).astype(HALF)
    dv_ref[...] = (dv_acc[...] + dvc_ref[...].astype(f32)).astype(HALF)

    @pl.when(step == groups - 1)
    def _():
        table_ref[...] = jnp.zeros_like(table_ref)
        for i in range(groups):
            a, b = lined(lines_ref, i), lined(cross_ref, i)
            row = jnp.concatenate([a[:, :BLOCK], a[:, BLOCK:] + b[:, :BLOCK], b[:, BLOCK:]], axis=1)
            row = flipped(row)
            for j in range(GROUP_HEADS):
                for tile in range(ROW_TILES):
                    part, lanes = place(i * GROUP_HEADS + j, tile, table_ref.shape)
                    table_ref[part, :, lanes] = row[j : j + 1, 128 * tile : 128 * tile + 128]


def params(mebibytes=32):
    return pltpu.CompilerParams(vmem_limit_bytes=mebibytes * 1024 * 1024)


COST = pl.CostEstimate(flops=1024, bytes_accessed=1024, transcendentals=0)
LONG = pl.CostEstimate(flops=10**11, bytes_accessed=1024, transcendentals=0)


def shape(s, t=jnp.float32):
    return jax.ShapeDtypeStruct(s, t)


SMEM = pl.BlockSpec(memory_space=pltpu.SMEM)
ANY = pl.BlockSpec(memory_space=pl.ANY)
ACCS = [pltpu.VMEM((BLOCK, GROUP_LANES), jnp.float32)] * 3
PACKED = BLOCK + 16
LINES = (1, 4, 8 * GROUP_HEADS, 128)


def whole_spec(s):
    return pl.BlockSpec(s, lambda i: (0,) * len(s))


def columns(first=0):
    return pl.BlockSpec((BLOCK, GROUP_LANES), lambda i: (0, first + i))


def stack(size, *rest, first=0):
    return pl.BlockSpec((size,) + rest, lambda i: (first + i,) + (0,) * len(rest))


def columns(first=0, rows=BLOCK):
    return pl.BlockSpec((rows, GROUP_LANES), lambda i: (0, first + i))


def stack(size, *rest, first=0):
    return pl.BlockSpec((size,) + rest, lambda i: (first + i,) + (0,) * len(rest))


def own_stats(head_width, group, live, q, g, k, v, bias, before):
    heads = bias.shape[0]
    groups = heads // GROUP_HEADS
    squares = stack(GROUP_HEADS, BLOCK, BLOCK, first=group)
    outs = [
        shape((groups, 16, BLOCK)),
        shape((heads, BLOCK, BLOCK)),
        shape((heads, BLOCK, BLOCK)),
        shape((PACKED, GROUP_LANES), HALF),
    ]
    out_specs = [stack(1, 16, BLOCK, first=group), squares, squares, whole_spec((PACKED, GROUP_LANES))]
    if not before:
        outs.append(shape(bias.shape))
        out_specs.append(whole_spec(bias.shape))
    return pl.pallas_call(
        functools.partial(own_stats_kernel, head_width, group),
        grid=(1,),
        in_specs=[SMEM] + [columns(group)] * 4 + [whole_spec(bias.shape)] + [ANY] * len(before),
        out_specs=out_specs,
        out_shape=outs,
        input_output_aliases={6 + i: i for i in range(len(before))},
        compiler_params=params(60),
        cost_estimate=COST,
        name=f"own_stats_{group}",
    )(live, q, g, k, v, bias, *before)


def cross(head_width, group, live, q, g, k, v, w, before):
    half = shape(q.shape, HALF)
    groups = q.shape[1] // GROUP_LANES
    return pl.pallas_call(
        functools.partial(cross_kernel, head_width, group),
        grid=(1,),
        in_specs=[
            SMEM, columns(group), columns(rows=PACKED), columns(group), columns(group), whole_spec(w.shape),
        ] + [ANY] * len(before),
        out_specs=[columns(group, 16), columns(group), columns(group), columns(group), stack(*LINES, first=group)],
        out_shape=[shape((16, q.shape[1]), HALF), half, half, half, shape((groups,) + LINES[1:])],
        scratch_shapes=[pltpu.VMEM((16, BLOCK), jnp.float32)] + ACCS,
        input_output_aliases={6 + i: i for i in range(len(before))},
        compiler_params=params(),
        cost_estimate=COST,
        name=f"cross_{group}",
    )(live, q, g, k, v, w, *before)


def own(head_width, live, q, g, k, e, dp, near, given, dkc, dvc, lines, parts):
    groups = near.shape[0]
    table = shape((parts, 1, -(-groups * GROUP_HEADS * ROW_TILES // parts) * 128))
    return pl.pallas_call(
        functools.partial(own_kernel, groups, head_width),
        grid=(groups,),
        in_specs=[
            SMEM, columns(), columns(), columns(),
            stack(GROUP_HEADS, BLOCK, BLOCK), stack(GROUP_HEADS, BLOCK, BLOCK),
            stack(1, 16, BLOCK), columns(rows=16), columns(), columns(), whole_spec(lines.shape),
        ],
        out_specs=[columns()] * 3 + [whole_spec(table.shape)],
        out_shape=[shape(q.shape), shape(q.shape, HALF), shape(q.shape, HALF), table],
        scratch_shapes=ACCS + [pltpu.VMEM(lines.shape, jnp.float32)],
        compiler_params=params(),
        cost_estimate=LONG,
        name="own",
    )(live, q, g, k, e, dp, near, given, dkc, dvc, lines)


def spread(terms, count):
    return pl.pallas_call(
        spread_kernel,
        out_shape=shape((count,) + terms.shape[1:]),
        compiler_params=params(),
        cost_estimate=COST,
        name="spread",
    )(terms)


def sum_over_devices(parts, axes, heads, after):
    terms = lax.all_to_all(parts, axes, 0, 0)
    every = lax.all_to_all(spread(terms, parts.shape[0]), axes, 0, 0)
    return pl.pallas_call(
        gather_kernel,
        in_specs=[pl.BlockSpec(memory_space=pltpu.VMEM), ANY],
        out_shape=shape((heads, 3 * BLOCK)),
        compiler_params=params(),
        cost_estimate=COST,
        name="gather",
    )(every, after)


def per_device(queries, keys, values, out_grad, lengths, rel_bias):
    frame_count, feature_width = queries.shape[1:]
    head_count = rel_bias.shape[0]
    head_width = feature_width // head_count
    groups = head_count // GROUP_HEADS
    live_own = lengths - lax.axis_index("tm") * BLOCK
    live_next = live_own - BLOCK
    q, k, v, g = (a.reshape(frame_count, feature_width) for a in (queries, keys, values, out_grad))

    q_next = shifted(q, "tm", -1)
    *before, chunk, w = own_stats(head_width, 0, live_own, q, g, k, v, rel_bias, ())
    chunks = [shifted(chunk, "tm", -1)]
    for group in range(1, groups):
        *before, chunk = own_stats(head_width, group, live_own, q, g, k, v, w, before)
        chunks.append(shifted(chunk, "tm", -1))
    near, e, dp = before
    results = ()
    for group in range(groups):
        results = cross(head_width, group, live_next, q_next, chunks[group], k, v, w, results)
    given, dq_cross, dkc, dvc, lines = results
    given = shifted(given, "tm", 1)
    dq_cross = shifted(dq_cross, "tm", 1)
    parts = lax.axis_size("dp") * lax.axis_size("tm")
    dq_own, dk, dv, table = own(head_width, live_own, q, g, k, e, dp, near, given, dkc, dvc, lines, parts)
    dq = (dq_own + dq_cross.astype(jnp.float32)).astype(HALF)
    bias_grad = sum_over_devices(table, ("dp", "tm"), head_count, dq)
    return tuple(a[None] for a in (dq, dk, dv)) + (bias_grad,)


def solution(mesh):
    block = P("dp", "tm", None)
    return jax.shard_map(
        per_device,
        mesh=mesh,
        in_specs=(block, block, block, block, P("dp"), P()),
        out_specs=(block, block, block, P()),
        check_vma=False,
    )
```

profile of v0, /device:TPU:0, one launch (start us, length us, event | category | flops | bytes accessed | tf_op | source)
XLA Modules:
  0.0 69.9 jit_solution(8997146950078171838)
XLA Ops:
  0.6 1.3 %collective-permute-start = (bf16[256,1152]{1,0:T(8,128)(2,1)}, bf16[256,1152]{1,0:T(8,128)(2,1)S(1)}, u32[]{:S(2)}, u32[]{:S(2)}) collective-permute-start(bf16[256,1152]{1,0:T(8,128)(2,1)} %bitcast.21), channel_id=1, source_target_pairs={{1,0},{2,1},{3,2},{4,3},{5,4},{6,5},{7,6},{9,8},{10,9},{11,10},{12... | collective-permute-start | bytes 1769480 | tf_op jit(solution)/shard_map/ppermute | solution.py:31
  2.6 3.5 %own_stats_0.1 = (f32[3,16,256]{2,1,0:T(8,128)}, f32[12,256,256]{2,1,0:T(8,128)}, f32[12,256,256]{2,1,0:T(8,128)}, bf16[272,384]{1,0:T(8,128)(2,1)}, f32[12,768]{1,0:T(8,128)}) custom-call(s32[1]{0:T(128)S(6)} %sub.10.live_ref, bf16[256,1152]{1,0:T(8,128)(2,1)} %bitcast.22, bf16[256,1152]{1,0:T(8,128)(2,1)} %bitcast.26, bf16[256,1152]{1,0:T(8,128)(2,1)} %bitcast.14, ...), custom_call_target="tpu_custom_call" | custom-call | flops 1024 | bytes 1024 | tf_op jit(solution)/shard_map/own_stats_0/pallas_call | solution.py:341
  6.0 1.3 %collective-permute-start.3 = (bf16[272,384]{1,0:T(8,128)(2,1)}, bf16[272,384]{1,0:T(8,128)(2,1)S(1)}, u32[]{:S(2)}, u32[]{:S(2)}) collective-permute-start(bf16[272,384]{1,0:T(8,128)(2,1)} %get-tuple-element.48), channel_id=1, source_target_pairs={{1,0},{2,1},{3,2},{4,3},{5,4},{6,5},{7,6},{9,8},{10,9},{11,10},{12... | collective-permute-start | bytes 626696 | tf_op jit(solution)/shard_map/ppermute | solution.py:31
  7.3 3.2 %own_stats_1.1 = (f32[3,16,256]{2,1,0:T(8,128)}, f32[12,256,256]{2,1,0:T(8,128)}, f32[12,256,256]{2,1,0:T(8,128)}, bf16[272,384]{1,0:T(8,128)(2,1)}) custom-call(s32[1]{0:T(128)S(6)} %sub.10.live_ref, bf16[256,1152]{1,0:T(8,128)(2,1)} %bitcast.23, bf16[256,1152]{1,0:T(8,128)(2,1)} %bitcast.27, ...), custom_call_target="tpu_custom_call", output_to_operand_aliasing={{0}: (6, {}), {1}: (7, {}), {2}: (8, {})} | custom-call | flops 1024 | bytes 1024 | tf_op jit(solution)/shard_map/own_stats_1/pallas_call | solution.py:341
  10.6 1.3 %collective-permute-start.2 = (bf16[272,384]{1,0:T(8,128)(2,1)}, bf16[272,384]{1,0:T(8,128)(2,1)S(1)}, u32[]{:S(2)}, u32[]{:S(2)}) collective-permute-start(bf16[272,384]{1,0:T(8,128)(2,1)} %get-tuple-element.47), channel_id=1, source_target_pairs={{1,0},{2,1},{3,2},{4,3},{5,4},{6,5},{7,6},{9,8},{10,9},{11,10},{12... | collective-permute-start | bytes 626696 | tf_op jit(solution)/shard_map/ppermute | solution.py:31
  11.9 0.0 copy-start
  11.9 0.0 copy-start.1
  11.9 0.0 copy-start.7
  11.9 3.3 %own_stats_2.1 = (f32[3,16,256]{2,1,0:T(8,128)}, f32[12,256,256]{2,1,0:T(8,128)}, f32[12,256,256]{2,1,0:T(8,128)}, bf16[272,384]{1,0:T(8,128)(2,1)}) custom-call(s32[1]{0:T(128)S(6)} %sub.10.live_ref, bf16[256,1152]{1,0:T(8,128)(2,1)} %bitcast.24, bf16[256,1152]{1,0:T(8,128)(2,1)} %bitcast.28, ...), custom_call_target="tpu_custom_call", output_to_operand_aliasing={{0}: (6, {}), {1}: (7, {}), {2}: (8, {})} | custom-call | flops 1024 | bytes 1024 | tf_op jit(solution)/shard_map/own_stats_2/pallas_call | solution.py:341
  15.2 1.3 %collective-permute-start.1 = (bf16[272,384]{1,0:T(8,128)(2,1)}, bf16[272,384]{1,0:T(8,128)(2,1)S(1)}, u32[]{:S(2)}, u32[]{:S(2)}) collective-permute-start(bf16[272,384]{1,0:T(8,128)(2,1)} %get-tuple-element.46), channel_id=1, source_target_pairs={{1,0},{2,1},{3,2},{4,3},{5,4},{6,5},{7,6},{9,8},{10,9},{11,10},{12... | collective-permute-start | bytes 626696 | tf_op jit(solution)/shard_map/ppermute | solution.py:31
  16.5 7.8 %collective-permute-done.3.g_ref = bf16[272,384]{1,0:T(8,128)(2,1)S(1)} collective-permute-done((bf16[272,384]{1,0:T(8,128)(2,1)}, bf16[272,384]{1,0:T(8,128)(2,1)S(1)}, u32[]{:S(2)}, u32[]{:S(2)}) %collective-permute-start.3) | collective-permute-done | bytes 208928 | tf_op jit(solution)/shard_map/ppermute | solution.py:31
  24.3 0.0 collective-permute-done.q_ref
  24.3 0.0 copy-done
  24.4 0.0 copy-done.7
  24.4 1.8 %cross_0.1 = (bf16[16,1152]{1,0:T(8,128)(2,1)S(1)}, bf16[256,1152]{1,0:T(8,128)(2,1)S(1)}, bf16[256,1152]{1,0:T(8,128)(2,1)S(1)}, bf16[256,1152]{1,0:T(8,128)(2,1)S(1)}, f32[3,4,32,128]{3,2,1,0:T(8,128)S(1)}) custom-call(s32[1]{0:T(128)S(6)} %sub.11.live_ref, bf16[256,1152]{1,0:T(8,128)(2,1)S(1)} %collective-permute-done.q_ref, ...), custom_call_target="tpu_custom_call" | custom-call | flops 1024 | bytes 1024 | tf_op jit(solution)/shard_map/cross_0/pallas_call | solution.py:357
  26.2 2.6 %collective-permute-done.2.g_ref = bf16[272,384]{1,0:T(8,128)(2,1)S(1)} collective-permute-done((bf16[272,384]{1,0:T(8,128)(2,1)}, bf16[272,384]{1,0:T(8,128)(2,1)S(1)}, u32[]{:S(2)}, u32[]{:S(2)}) %collective-permute-start.2) | collective-permute-done | bytes 208928 | tf_op jit(solution)/shard_map/ppermute | solution.py:31
  28.8 0.0 copy-start.8
  28.8 1.8 %cross_1.1 = (bf16[16,1152]{1,0:T(8,128)(2,1)S(1)}, bf16[256,1152]{1,0:T(8,128)(2,1)S(1)}, bf16[256,1152]{1,0:T(8,128)(2,1)S(1)}, bf16[256,1152]{1,0:T(8,128)(2,1)S(1)}, f32[3,4,32,128]{3,2,1,0:T(8,128)S(1)}) custom-call(s32[1]{0:T(128)S(6)} %sub.11.live_ref, ...), custom_call_target="tpu_custom_call", output_to_operand_aliasing={{0}: (6, {}), {1}: (7, {}), {2}: (8, {}), {3}: (9, {}), {4}... | custom-call | flops 1024 | bytes 1024 | tf_op jit(solution)/shard_map/cross_1/pallas_call | solution.py:357
  30.7 1.8 %collective-permute-done.1.g_ref = bf16[272,384]{1,0:T(8,128)(2,1)S(1)} collective-permute-done((bf16[272,384]{1,0:T(8,128)(2,1)}, bf16[272,384]{1,0:T(8,128)(2,1)S(1)}, u32[]{:S(2)}, u32[]{:S(2)}) %collective-permute-start.1) | collective-permute-done | bytes 208928 | tf_op jit(solution)/shard_map/ppermute | solution.py:31
  32.5 1.8 %cross_2.1 = (bf16[16,1152]{1,0:T(8,128)(2,1)S(1)}, bf16[256,1152]{1,0:T(8,128)(2,1)S(1)}, bf16[256,1152]{1,0:T(8,128)(2,1)S(1)}, bf16[256,1152]{1,0:T(8,128)(2,1)S(1)}, f32[3,4,32,128]{3,2,1,0:T(8,128)S(1)}) custom-call(s32[1]{0:T(128)S(6)} %sub.11.live_ref, ...), custom_call_target="tpu_custom_call", output_to_operand_aliasing={{0}: (6, {}), {1}: (7, {}), {2}: (8, {}), {3}: (9, {}), {4}... | custom-call | flops 1024 | bytes 1024 | tf_op jit(solution)/shard_map/cross_2/pallas_call | solution.py:357
  34.3 4.5 %collective-permute-start.4 = (bf16[16,1152]{1,0:T(8,128)(2,1)S(1)}, bf16[16,1152]{1,0:T(8,128)(2,1)S(1)}, u32[]{:S(2)}, u32[]{:S(2)}) collective-permute-start(bf16[16,1152]{1,0:T(8,128)(2,1)S(1)} %get-tuple-element.59), channel_id=1, source_target_pairs={{0,1},{1,2},{2,3},{3,4},{4,5},{5,6},{6,7},{8,9},{9,10},{10,11},{11... | collective-permute-start | bytes 110600 | tf_op jit(solution)/shard_map/ppermute | solution.py:31
  38.8 2.6 %collective-permute-start.5 = (bf16[256,1152]{1,0:T(8,128)(2,1)S(1)}, bf16[256,1152]{1,0:T(8,128)(2,1)S(1)}, u32[]{:S(2)}, u32[]{:S(2)}) collective-permute-start(bf16[256,1152]{1,0:T(8,128)(2,1)S(1)} %get-tuple-element.64), channel_id=1, source_target_pairs={{0,1},{1,2},{2,3},{3,4},{4,5},{5,6},{6,7},{8,9},{9,10},{10,11},{11... | collective-permute-start | bytes 1769480 | tf_op jit(solution)/shard_map/ppermute | solution.py:31
  41.4 0.0 collective-permute-done.4.given_ref
  41.5 4.4 %own.1 = (f32[256,1152]{1,0:T(8,128)S(1)}, bf16[256,1152]{1,0:T(8,128)(2,1)}, bf16[256,1152]{1,0:T(8,128)(2,1)}, f32[32,1,384]{2,1,0:T(1,128)S(1)}) custom-call(s32[1]{0:T(128)S(6)} %sub.10.live_ref, bf16[256,1152]{1,0:T(8,128)(2,1)S(1)} %bitcast.25, bf16[256,1152]{1,0:T(8,128)(2,1)S(1)} %bitcast.29, bf16[256,1152]{1,0:T(8,128)(2,1)S(1)} %bitcast.20, ...), custom_call_target="tpu_custom_call" | custom-call | flops 99999997952 | bytes 1024 | tf_op jit(solution)/shard_map/own/pallas_call | solution.py:376
  45.9 12.1 %all_to_all.10.terms_ref = f32[32,1,384]{2,1,0:T(1,128)S(1)} all-to-all(f32[32,1,384]{2,1,0:T(1,128)S(1)} %get-tuple-element.67), channel_id=1, replica_groups=mesh['dp'=4,'tm'=8] {'dp','tm'}, dimensions={0} | all-to-all | bytes 98304 | tf_op jit(solution)/shard_map/all_to_all | solution.py:404
  58.0 0.7 spread.1
  58.6 3.4 %all-to-all-start.1 = ((f32[32,1,384]{2,1,0:T(1,128)}), f32[32,1,384]{2,1,0:T(1,128)S(1)}, u32[]{:S(2)}, u32[]{:S(2)}) async-start(f32[32,1,384]{2,1,0:T(1,128)} %spread.1), calls=%async_computation.1 | async-start | bytes 98304 | tf_op jit(solution)/shard_map/all_to_all | solution.py:405
  62.1 0.0 collective-permute-done.5
  62.1 0.1 add_convert_fusion._
  62.2 0.0 copy-start.6
  62.2 7.1 %all-to-all-done.1.parts_ref = f32[32,1,384]{2,1,0:T(1,128)S(1)} async-done(((f32[32,1,384]{2,1,0:T(1,128)}), f32[32,1,384]{2,1,0:T(1,128)S(1)}, u32[]{:S(2)}, u32[]{:S(2)}) %all-to-all-start.1) | async-done | bytes 49184 | tf_op jit(solution)/shard_map/all_to_all | solution.py:405
  69.3 0.6 gather.1
  (11 shorter events, 0.0 us)
Async XLA Ops:
  0.6 23.7 %collective-permute-start = (bf16[256,1152]{1,0:T(8,128)(2,1)}, bf16[256,1152]{1,0:T(8,128)(2,1)S(1)}, u32[]{:S(2)}, u32[]{:S(2)}) collective-permute-start(bf16[256,1152]{1,0:T(8,128)(2,1)} %bitcast.21), channel_id=1, source_target_pairs={{1,0},{2,1},{3,2},{4,3},{5,4},{6,5},{7,6},{9,8},{10,9},{11,10},{12... | collective-permute-start | bytes 1769480 | tf_op jit(solution)/shard_map/ppermute | solution.py:31
  6.0 18.3 %collective-permute-start.3 = (bf16[272,384]{1,0:T(8,128)(2,1)}, bf16[272,384]{1,0:T(8,128)(2,1)S(1)}, u32[]{:S(2)}, u32[]{:S(2)}) collective-permute-start(bf16[272,384]{1,0:T(8,128)(2,1)} %get-tuple-element.48), channel_id=1, source_target_pairs={{1,0},{2,1},{3,2},{4,3},{5,4},{6,5},{7,6},{9,8},{10,9},{11,10},{12... | collective-permute-start | bytes 626696 | tf_op jit(solution)/shard_map/ppermute | solution.py:31
  10.6 18.2 %collective-permute-start.2 = (bf16[272,384]{1,0:T(8,128)(2,1)}, bf16[272,384]{1,0:T(8,128)(2,1)S(1)}, u32[]{:S(2)}, u32[]{:S(2)}) collective-permute-start(bf16[272,384]{1,0:T(8,128)(2,1)} %get-tuple-element.47), channel_id=1, source_target_pairs={{1,0},{2,1},{3,2},{4,3},{5,4},{6,5},{7,6},{9,8},{10,9},{11,10},{12... | collective-permute-start | bytes 626696 | tf_op jit(solution)/shard_map/ppermute | solution.py:31
  11.9 12.5 %copy-start = (bf16[1,256,1152]{2,1,0:T(8,128)(2,1)S(1)}, bf16[1,256,1152]{2,1,0:T(8,128)(2,1)}, u32[]{:S(2)}) copy-start(bf16[1,256,1152]{2,1,0:T(8,128)(2,1)} %param.8) | copy-start | bytes 1769476
  11.9 12.5 %copy-start.1 = (bf16[1,256,1152]{2,1,0:T(8,128)(2,1)S(1)}, bf16[1,256,1152]{2,1,0:T(8,128)(2,1)}, u32[]{:S(2)}) copy-start(bf16[1,256,1152]{2,1,0:T(8,128)(2,1)} %param.7) | copy-start | bytes 1769476
  11.9 12.5 %copy-start.7 = (f32[12,768]{1,0:T(8,128)S(1)}, f32[12,768]{1,0:T(8,128)}, u32[]{:S(2)}) copy-start(f32[12,768]{1,0:T(8,128)} %get-tuple-element.36.bias_ref.w_ref) | copy-start | bytes 110596
  15.2 17.3 %collective-permute-start.1 = (bf16[272,384]{1,0:T(8,128)(2,1)}, bf16[272,384]{1,0:T(8,128)(2,1)S(1)}, u32[]{:S(2)}, u32[]{:S(2)}) collective-permute-start(bf16[272,384]{1,0:T(8,128)(2,1)} %get-tuple-element.46), channel_id=1, source_target_pairs={{1,0},{2,1},{3,2},{4,3},{5,4},{6,5},{7,6},{9,8},{10,9},{11,10},{12... | collective-permute-start | bytes 626696 | tf_op jit(solution)/shard_map/ppermute | solution.py:31
  28.8 12.6 %copy-start.2 = (f32[12,256,256]{2,1,0:T(8,128)S(1)}, f32[12,256,256]{2,1,0:T(8,128)}, u32[]{:S(2)}) copy-start(f32[12,256,256]{2,1,0:T(8,128)} %get-tuple-element.43.e_ref) | copy-start | bytes 9437188
  28.8 12.6 %copy-start.3 = (f32[12,256,256]{2,1,0:T(8,128)S(1)}, f32[12,256,256]{2,1,0:T(8,128)}, u32[]{:S(2)}) copy-start(f32[12,256,256]{2,1,0:T(8,128)} %get-tuple-element.44.dp_ref) | copy-start | bytes 9437188
  28.8 12.6 %copy-start.4 = (bf16[1,256,1152]{2,1,0:T(8,128)(2,1)S(1)}, bf16[1,256,1152]{2,1,0:T(8,128)(2,1)}, u32[]{:S(2)}) copy-start(bf16[1,256,1152]{2,1,0:T(8,128)(2,1)} %param.6) | copy-start | bytes 1769476
  28.8 12.6 %copy-start.5 = (bf16[1,256,1152]{2,1,0:T(8,128)(2,1)S(1)}, bf16[1,256,1152]{2,1,0:T(8,128)(2,1)}, u32[]{:S(2)}) copy-start(bf16[1,256,1152]{2,1,0:T(8,128)(2,1)} %param.9) | copy-start | bytes 1769476
  28.8 12.6 %copy-start.8 = (f32[3,16,256]{2,1,0:T(8,128)S(1)}, f32[3,16,256]{2,1,0:T(8,128)}, u32[]{:S(2)}) copy-start(f32[3,16,256]{2,1,0:T(8,128)} %get-tuple-element.45.near_ref) | copy-start | bytes 147460
  34.3 7.1 %collective-permute-start.4 = (bf16[16,1152]{1,0:T(8,128)(2,1)S(1)}, bf16[16,1152]{1,0:T(8,128)(2,1)S(1)}, u32[]{:S(2)}, u32[]{:S(2)}) collective-permute-start(bf16[16,1152]{1,0:T(8,128)(2,1)S(1)} %get-tuple-element.59), channel_id=1, source_target_pairs={{0,1},{1,2},{2,3},{3,4},{4,5},{5,6},{6,7},{8,9},{9,10},{10,11},{11... | collective-permute-start | bytes 110600 | tf_op jit(solution)/shard_map/ppermute | solution.py:31
  38.8 23.2 %collective-permute-start.5 = (bf16[256,1152]{1,0:T(8,128)(2,1)S(1)}, bf16[256,1152]{1,0:T(8,128)(2,1)S(1)}, u32[]{:S(2)}, u32[]{:S(2)}) collective-permute-start(bf16[256,1152]{1,0:T(8,128)(2,1)S(1)} %get-tuple-element.64), channel_id=1, source_target_pairs={{0,1},{1,2},{2,3},{3,4},{4,5},{5,6},{6,7},{8,9},{9,10},{10,11},{11... | collective-permute-start | bytes 1769480 | tf_op jit(solution)/shard_map/ppermute | solution.py:31
  58.6 10.6 %all-to-all-start.1 = ((f32[32,1,384]{2,1,0:T(1,128)}), f32[32,1,384]{2,1,0:T(1,128)S(1)}, u32[]{:S(2)}, u32[]{:S(2)}) async-start(f32[32,1,384]{2,1,0:T(1,128)} %spread.1), calls=%async_computation.1 | async-start | bytes 98304 | tf_op jit(solution)/shard_map/all_to_all | solution.py:405
  62.2 7.8 %copy-start.6 = (bf16[256,1152]{1,0:T(8,128)(2,1)}, bf16[256,1152]{1,0:T(8,128)(2,1)S(1)}, u32[]{:S(2)}) copy-start(bf16[256,1152]{1,0:T(8,128)(2,1)S(1)} %add_convert_fusion._) | copy-start | bytes 1769476
where the time goes:
time: 70.3 us; the launch traced here: 69.9 us
  Pallas kernels  21.1 us (30%)
  waiting for transfers between devices  19.4 us (28%)
  starting transfers between devices  15.6 us (22%)
  blocking collectives  12.1 us (17%)
  between operations  1.49 us (2%)
    ppermute x6, waiting for transfers between devices, shifted(): return lax.ppermute(x, axis, pairs)  12.3 us
    ppermute x6, starting transfers between devices, shifted(): return lax.ppermute(x, axis, pairs)  12.2 us
    all_to_all x1, blocking collectives, sum_over_devices(): terms = lax.all_to_all(parts, axes, 0, 0)  12.1 us
    pallas_call x3, Pallas kernels, own_stats(): pl.pallas_call(functools.partial(own_stats_kernel, head_width, group), gr...  10 us
    all_to_all x1, waiting for transfers between devices, sum_over_devices(): every = lax.all_to_all(spread(terms, parts.shape[0]), axes, 0, 0)  7.1 us
    pallas_call x3, Pallas kernels, cross(): pl.pallas_call(functools.partial(cross_kernel, head_width, group), grid=(...  5.42 us
    pallas_call x1, Pallas kernels, own(): pl.pallas_call(functools.partial(own_kernel, groups, head_width), grid=(g...  4.4 us
    all_to_all x1, starting transfers between devices, sum_over_devices(): every = lax.all_to_all(spread(terms, parts.shape[0]), axes, 0, 0)  3.41 us
  transfers between devices with their start and end apart: 7, of which 4 were waited for; matrix products, arithmetic and copies ran while one was open for 0% of the time, Pallas kernels for 27%

commit v1 on v0

--- a/solution.py
+++ b/solution.py
@@ -14,7 +14,8 @@
 MASKED = -(2.0**30)
 GROUP_HEADS = 4
 GROUP_LANES = 384
-WINDOWS = ((0, 128), (0, 256), (128, 256), (256, 128))
+WIDTH = 256
+FIRST = (0, 0, 128, 128)
 
 NT = (((1,), (1,)), ((), ()))
 NN = (((1,), (0,)), ((), ()))
@@ -32,15 +33,9 @@
 
 
 def head_mask(j, head_width, dtype):
-    lo, width = WINDOWS[j]
-    lane = lax.broadcasted_iota(jnp.int32, (1, width), 1) + lo
+    lane = lax.broadcasted_iota(jnp.int32, (1, WIDTH), 1) + FIRST[j]
     inside = (lane >= j * head_width) & (lane < (j + 1) * head_width)
     return jnp.where(inside, 1.0, 0.0).astype(dtype)
-
-
-def live_rows(count, width, dtype):
-    row = lax.broadcasted_iota(jnp.int32, (BLOCK, width), 0)
-    return jnp.where(row < count, 1.0, 0.0).astype(dtype)
 
 
 def skew(row):
@@ -82,25 +77,14 @@
     return total
 
 
-def window(ref, j):
-    lo, width = WINDOWS[j]
-    return ref[:BLOCK, lo : lo + width]
-
-
-def add_window(ref, j, value):
-    lo, width = WINDOWS[j]
-    for tile in range(0, width, 128):
-        at = slice(lo + tile, lo + tile + 128)
-        piece = value[:, tile : tile + 128]
-        if (lo + tile) // 128 == j:
-            ref[:, at] = piece
-        else:
-            ref[:, at] += piece
-
-
-def live_tiles(count):
-    rows = live_rows(count, 128, jnp.bfloat16)
-    return {128: rows, 256: jnp.concatenate([rows, rows], axis=1)}
+def window(ref, j, group=0):
+    first = group * GROUP_LANES + FIRST[j]
+    return ref[:BLOCK, first : first + WIDTH]
+
+
+def live_rows(count):
+    row = lax.broadcasted_iota(jnp.int32, (BLOCK, WIDTH), 0)
+    return jnp.where(row < count, 1.0, 0.0).astype(HALF)
 
 
 def put_lines(ref, j, lines):
@@ -140,12 +124,21 @@
     return jnp.max(x, axis=0, keepdims=True).astype(HALF).astype(jnp.float32)
 
 
-def add_products(j, qm, gm, km, p, ds, dq_acc, dk_acc, dv_acc):
-    pb = p.astype(HALF)
-    dsb = ds.astype(HALF)
-    add_window(dv_acc, j, dot(pb, gm, NN))
-    add_window(dk_acc, j, dot(dsb, qm, NN))
-    add_window(dq_acc, j, dot(dsb, km, TN))
+def pair_products(heads, dq_acc, dk_acc, dv_acc):
+    for pair in range(2):
+        qm, gm, km, p, ds = zip(*heads[2 * pair : 2 * pair + 2])
+        ps, dss = (jnp.concatenate(x, axis=1) for x in (p, ds))
+        products = (
+            (dv_acc, dot(ps, jnp.concatenate(gm, axis=0), NN)),
+            (dk_acc, dot(dss, jnp.concatenate(qm, axis=0), NN)),
+            (dq_acc, dot(jnp.concatenate(ds, axis=0), jnp.concatenate(km, axis=0), TN)),
+        )
+        for ref, value in products:
+            if pair == 0:
+                ref[:, :WIDTH] = value
+            else:
+                ref[:, 128:WIDTH] += value[:, :128]
+                ref[:, WIDTH:] = value[:, 128:]
 
 
 def own_stats_kernel(
@@ -161,12 +154,12 @@
     scale = head_width**-0.5 * LOG2E
     live = live_ref[0]
     key_live = lax.broadcasted_iota(jnp.int32, (BLOCK, BLOCK), 0) < live
-    rows = live_tiles(live)
+    rows = live_rows(live)
     for j in range(GROUP_HEADS):
         mask = head_mask(j, head_width, HALF)
         head = group * GROUP_HEADS + j
         qm = window(q_ref, j) * mask
-        gm = window(g_ref, j) * mask * rows[WINDOWS[j][1]]
+        gm = window(g_ref, j) * mask * rows
         x = dot(window(k_ref, j), qm, NT) * scale + skew(flip_ref[head : head + 1, : 2 * BLOCK])
         x = jnp.where(key_live, x, MASKED)
         m = reference_value(x)
@@ -187,18 +180,19 @@
 ):
     out_ref, dq_ref, dk_ref, dv_ref, lines_ref, rows_ref, dq_acc, dk_acc, dv_acc = refs[-9:]
     scale = head_width**-0.5 * LOG2E
-    live = live_tiles(live_ref[0])
+    live = live_rows(live_ref[0])
     far_m, far_total, far_mixed = unpack_rows(g_ref.at[BLOCK:PACKED, :])
+    heads = []
     for j in range(GROUP_HEADS):
         mask = head_mask(j, head_width, HALF)
-        qm = window(q_ref, j) * mask
-        gm = window(g_ref, j) * mask * live[WINDOWS[j][1]]
-        km = window(k_ref, j) * mask
+        qm = window(q_ref, j, group) * mask
+        gm = window(g_ref, j) * mask * live
+        km = window(k_ref, j, group) * mask
         x = dot(km, qm, NT) * scale + skew(w_ref[group * GROUP_HEADS + j : group * GROUP_HEADS + j + 1, BLOCK:])
         m_far = far_m[j : j + 1]
         m = jnp.maximum(reference_value(x), m_far)
         e = jnp.exp2(x - m)
-        dp = dot(window(v_ref, j), gm, NT)
+        dp = dot(window(v_ref, j, group), gm, NT)
         shrink = jnp.exp2(m_far - m)
         total = jnp.sum(e, axis=0, keepdims=True) + far_total[j : j + 1] * shrink
         mixed = jnp.sum(e * dp, axis=0, keepdims=True) + far_mixed[j : j + 1] * shrink
@@ -210,7 +204,8 @@
         p = e * inverse
         ds = p * (dp - delta)
         put_lines(lines_ref, j, unskew(ds))
-        add_products(j, qm, gm, km, p, ds, dq_acc, dk_acc, dv_acc)
+        heads.append((qm, gm, km, p.astype(HALF), ds.astype(HALF)))
+    pair_products(heads, dq_acc, dk_acc, dv_acc)
     rows_ref[12:16, :] = jnp.zeros((4, BLOCK), jnp.float32)
     pack_rows(out_ref, rows_ref[...])
     scaling = head_width**-0.5
@@ -248,29 +243,38 @@
     cross_ref, dq_ref, dk_ref, dv_ref, table_ref, dq_acc, dk_acc, dv_acc, lines_ref,
 ):
     step = pl.program_id(0)
-    live = live_tiles(live_ref[0])
-    given_m, given_inverse, given_delta = unpack_rows(given_ref)
-    for j in range(GROUP_HEADS):
-        mask = head_mask(j, head_width, HALF)
-        qm = window(q_ref, j) * mask
-        gm = window(g_ref, j) * mask * live[WINDOWS[j][1]]
-        km = window(k_ref, j) * mask
-        m_near = near_ref[0, j : j + 1, :]
-        inverse_near = 1.0 / near_ref[0, 4 + j : 5 + j, :]
-        inverse = given_inverse[j : j + 1]
-        there = inverse > 0.0
-        m = jnp.where(there, given_m[j : j + 1], m_near)
-        ratio = jnp.exp2(m_near - m) * jnp.where(there, inverse, inverse_near)
-        delta = jnp.where(there, given_delta[j : j + 1], near_ref[0, 8 + j : 9 + j, :] * inverse_near)
-        p = e_ref[j] * ratio
-        ds = p * (dp_ref[j] - delta)
-        put_lines(lines_ref.at[pl.ds(step, 1)], j, unskew(ds))
-        add_products(j, qm, gm, km, p, ds, dq_acc, dk_acc, dv_acc)
-    scaling = head_width**-0.5
-    f32 = jnp.float32
-    dq_ref[...] = dq_acc[...] * scaling
-    dk_ref[...] = (dk_acc[...] * scaling + dkc_ref[...].astype(f32)).astype(HALF)
-    dv_ref[...] = (dv_acc[...] + dvc_ref[...].astype(f32)).astype(HALF)
+    live = live_rows(live_ref[0])
+
+    def one_group(group):
+        lanes = slice(group * GROUP_LANES, (group + 1) * GROUP_LANES)
+        given_m, given_inverse, given_delta = unpack_rows(given_ref.at[:, lanes])
+        heads = []
+        for j in range(GROUP_HEADS):
+            mask = head_mask(j, head_width, HALF)
+            head = group * GROUP_HEADS + j
+            qm = window(q_ref, j, group) * mask
+            gm = window(g_ref, j, group) * mask * live
+            km = window(k_ref, j, group) * mask
+            m_near = near_ref[group, j : j + 1, :]
+            inverse_near = 1.0 / near_ref[group, 4 + j : 5 + j, :]
+            inverse = given_inverse[j : j + 1]
+            there = inverse > 0.0
+            m = jnp.where(there, given_m[j : j + 1], m_near)
+            ratio = jnp.exp2(m_near - m) * jnp.where(there, inverse, inverse_near)
+            delta = jnp.where(there, given_delta[j : j + 1], near_ref[group, 8 + j : 9 + j, :] * inverse_near)
+            p = e_ref[head] * ratio
+            ds = p * (dp_ref[head] - delta)
+            put_lines(lines_ref.at[group : group + 1], j, unskew(ds))
+            heads.append((qm, gm, km, p.astype(HALF), ds.astype(HALF)))
+        pair_products(heads, dq_acc, dk_acc, dv_acc)
+        scaling = head_width**-0.5
+        f32 = jnp.float32
+        dq_ref[...] = dq_acc[...] * scaling
+        dk_ref[...] = (dk_acc[...] * scaling + dkc_ref[:, lanes].astype(f32)).astype(HALF)
+        dv_ref[...] = (dv_acc[...] + dvc_ref[:, lanes].astype(f32)).astype(HALF)
+
+    for group in range(groups):
+        pl.when(step == group)(functools.partial(one_group, group))
 
     @pl.when(step == groups - 1)
     def _():
@@ -299,6 +303,7 @@
 
 SMEM = pl.BlockSpec(memory_space=pltpu.SMEM)
 ANY = pl.BlockSpec(memory_space=pl.ANY)
+VMEM = pl.BlockSpec(memory_space=pltpu.VMEM)
 ACCS = [pltpu.VMEM((BLOCK, GROUP_LANES), jnp.float32)] * 3
 PACKED = BLOCK + 16
 LINES = (1, 4, 8 * GROUP_HEADS, 128)
@@ -357,9 +362,7 @@
     return pl.pallas_call(
         functools.partial(cross_kernel, head_width, group),
         grid=(1,),
-        in_specs=[
-            SMEM, columns(group), columns(rows=PACKED), columns(group), columns(group), whole_spec(w.shape),
-        ] + [ANY] * len(before),
+        in_specs=[SMEM] + [VMEM] * 5 + [ANY] * len(before),
         out_specs=[columns(group, 16), columns(group), columns(group), columns(group), stack(*LINES, first=group)],
         out_shape=[shape((16, q.shape[1]), HALF), half, half, half, shape((groups,) + LINES[1:])],
         scratch_shapes=[pltpu.VMEM((16, BLOCK), jnp.float32)] + ACCS,
@@ -376,11 +379,7 @@
     return pl.pallas_call(
         functools.partial(own_kernel, groups, head_width),
         grid=(groups,),
-        in_specs=[
-            SMEM, columns(), columns(), columns(),
-            stack(GROUP_HEADS, BLOCK, BLOCK), stack(GROUP_HEADS, BLOCK, BLOCK),
-            stack(1, 16, BLOCK), columns(rows=16), columns(), columns(), whole_spec(lines.shape),
-        ],
+        in_specs=[SMEM] + [VMEM] * 10,
         out_specs=[columns()] * 3 + [whole_spec(table.shape)],
         out_shape=[shape(q.shape), shape(q.shape, HALF), shape(q.shape, HALF), table],
         scratch_shapes=ACCS + [pltpu.VMEM(lines.shape, jnp.float32)],
@@ -405,7 +404,7 @@
     every = lax.all_to_all(spread(terms, parts.shape[0]), axes, 0, 0)
     return pl.pallas_call(
         gather_kernel,
-        in_specs=[pl.BlockSpec(memory_space=pltpu.VMEM), ANY],
+        in_specs=[VMEM, ANY],
         out_shape=shape((heads, 3 * BLOCK)),
         compiler_params=params(),
         cost_estimate=COST,

time: 70.3 us -> 69.9 us (level)
  Pallas kernels: 21.1 us -> 19.5 us
    pallas_call x3, Pallas kernels: 5.42 us -> 4.17 us  [cross(): pl.pallas_call(functools.partial(cross_kernel, head_width, group), grid=(...]
    ppermute x6, waiting for transfers between devices: 12.3 us -> 13 us  [shifted(): return lax.ppermute(x, axis, pairs)]
  transfers between devices with their start and end apart: 7 -> 7, of which waited for: 4 -> 4; matrix products, arithmetic and copies ran while one was open for 0% -> 0% of each run, Pallas kernels for 27% -> 25%
where the time goes in v1:
time: 69.9 us; the launch traced here: 69.6 us
  waiting for transfers between devices  20.1 us (29%)
  Pallas kernels  19.5 us (28%)
  starting transfers between devices  16.2 us (23%)
  blocking collectives  12.1 us (17%)
  between operations  1.48 us (2%)
    ppermute x6, waiting for transfers between devices, shifted(): return lax.ppermute(x, axis, pairs)  13 us
    ppermute x6, starting transfers between devices, shifted(): return lax.ppermute(x, axis, pairs)  12.2 us
    all_to_all x1, blocking collectives, sum_over_devices(): terms = lax.all_to_all(parts, axes, 0, 0)  12.1 us
    pallas_call x3, Pallas kernels, own_stats(): pl.pallas_call(functools.partial(own_stats_kernel, head_width, group), gr...  10.1 us
    all_to_all x1, waiting for transfers between devices, sum_over_devices(): every = lax.all_to_all(spread(terms, parts.shape[0]), axes, 0, 0)  7.1 us
    pallas_call x3, Pallas kernels, cross(): pl.pallas_call(functools.partial(cross_kernel, head_width, group), grid=(...  4.17 us
    all_to_all x1, starting transfers between devices, sum_over_devices(): every = lax.all_to_all(spread(terms, parts.shape[0]), axes, 0, 0)  3.94 us
    pallas_call x1, Pallas kernels, own(): pl.pallas_call(functools.partial(own_kernel, groups, head_width), grid=(g...  3.9 us
  transfers between devices with their start and end apart: 7, of which 4 were waited for; matrix products, arithmetic and copies ran while one was open for 0% of the time, Pallas kernels for 25%

profile of v1, /device:TPU:0, one launch (start us, length us, event | category | flops | bytes accessed | tf_op | source)
XLA Modules:
  0.0 69.6 jit_solution(6939712258260955833)
XLA Ops:
  0.6 1.3 %collective-permute-start = (bf16[256,1152]{1,0:T(8,128)(2,1)}, bf16[256,1152]{1,0:T(8,128)(2,1)S(1)}, u32[]{:S(2)}, u32[]{:S(2)}) collective-permute-start(bf16[256,1152]{1,0:T(8,128)(2,1)} %bitcast.21), channel_id=1, source_target_pairs={{1,0},{2,1},{3,2},{4,3},{5,4},{6,5},{7,6},{9,8},{10,9},{11,10},{12... | collective-permute-start | bytes 1769480 | tf_op jit(solution)/shard_map/ppermute | solution.py:32
  2.6 3.5 %own_stats_0.1 = (f32[3,16,256]{2,1,0:T(8,128)}, f32[12,256,256]{2,1,0:T(8,128)}, f32[12,256,256]{2,1,0:T(8,128)}, bf16[272,384]{1,0:T(8,128)(2,1)}, f32[12,768]{1,0:T(8,128)}) custom-call(s32[1]{0:T(128)S(6)} %sub.10.live_ref, bf16[256,1152]{1,0:T(8,128)(2,1)} %bitcast.22, bf16[256,1152]{1,0:T(8,128)(2,1)} %bitcast.26, bf16[256,1152]{1,0:T(8,128)(2,1)} %bitcast.14, ...), custom_call_target="tpu_custom_call" | custom-call | flops 1024 | bytes 1024 | tf_op jit(solution)/shard_map/own_stats_0/pallas_call | solution.py:346
  6.1 1.3 %collective-permute-start.3 = (bf16[272,384]{1,0:T(8,128)(2,1)}, bf16[272,384]{1,0:T(8,128)(2,1)S(1)}, u32[]{:S(2)}, u32[]{:S(2)}) collective-permute-start(bf16[272,384]{1,0:T(8,128)(2,1)} %get-tuple-element.48), channel_id=1, source_target_pairs={{1,0},{2,1},{3,2},{4,3},{5,4},{6,5},{7,6},{9,8},{10,9},{11,10},{12... | collective-permute-start | bytes 626696 | tf_op jit(solution)/shard_map/ppermute | solution.py:32
  7.3 3.3 %own_stats_1.1 = (f32[3,16,256]{2,1,0:T(8,128)}, f32[12,256,256]{2,1,0:T(8,128)}, f32[12,256,256]{2,1,0:T(8,128)}, bf16[272,384]{1,0:T(8,128)(2,1)}) custom-call(s32[1]{0:T(128)S(6)} %sub.10.live_ref, bf16[256,1152]{1,0:T(8,128)(2,1)} %bitcast.23, bf16[256,1152]{1,0:T(8,128)(2,1)} %bitcast.27, ...), custom_call_target="tpu_custom_call", output_to_operand_aliasing={{0}: (6, {}), {1}: (7, {}), {2}: (8, {})} | custom-call | flops 1024 | bytes 1024 | tf_op jit(solution)/shard_map/own_stats_1/pallas_call | solution.py:346
  10.6 1.3 %collective-permute-start.2 = (bf16[272,384]{1,0:T(8,128)(2,1)}, bf16[272,384]{1,0:T(8,128)(2,1)S(1)}, u32[]{:S(2)}, u32[]{:S(2)}) collective-permute-start(bf16[272,384]{1,0:T(8,128)(2,1)} %get-tuple-element.47), channel_id=1, source_target_pairs={{1,0},{2,1},{3,2},{4,3},{5,4},{6,5},{7,6},{9,8},{10,9},{11,10},{12... | collective-permute-start | bytes 626696 | tf_op jit(solution)/shard_map/ppermute | solution.py:32
  11.9 0.0 copy-start
  11.9 0.0 copy-start.1
  11.9 0.0 copy-start.7
  11.9 3.4 %own_stats_2.1 = (f32[3,16,256]{2,1,0:T(8,128)}, f32[12,256,256]{2,1,0:T(8,128)}, f32[12,256,256]{2,1,0:T(8,128)}, bf16[272,384]{1,0:T(8,128)(2,1)}) custom-call(s32[1]{0:T(128)S(6)} %sub.10.live_ref, bf16[256,1152]{1,0:T(8,128)(2,1)} %bitcast.24, bf16[256,1152]{1,0:T(8,128)(2,1)} %bitcast.28, ...), custom_call_target="tpu_custom_call", output_to_operand_aliasing={{0}: (6, {}), {1}: (7, {}), {2}: (8, {})} | custom-call | flops 1024 | bytes 1024 | tf_op jit(solution)/shard_map/own_stats_2/pallas_call | solution.py:346
  15.3 1.3 %collective-permute-start.1 = (bf16[272,384]{1,0:T(8,128)(2,1)}, bf16[272,384]{1,0:T(8,128)(2,1)S(1)}, u32[]{:S(2)}, u32[]{:S(2)}) collective-permute-start(bf16[272,384]{1,0:T(8,128)(2,1)} %get-tuple-element.46), channel_id=1, source_target_pairs={{1,0},{2,1},{3,2},{4,3},{5,4},{6,5},{7,6},{9,8},{10,9},{11,10},{12... | collective-permute-start | bytes 626696 | tf_op jit(solution)/shard_map/ppermute | solution.py:32
  16.6 7.7 %collective-permute-done.3.g_ref = bf16[272,384]{1,0:T(8,128)(2,1)S(1)} collective-permute-done((bf16[272,384]{1,0:T(8,128)(2,1)}, bf16[272,384]{1,0:T(8,128)(2,1)S(1)}, u32[]{:S(2)}, u32[]{:S(2)}) %collective-permute-start.3) | collective-permute-done | bytes 208928 | tf_op jit(solution)/shard_map/ppermute | solution.py:32
  24.3 0.0 collective-permute-done.q_ref
  24.3 0.0 copy-done
  24.4 0.0 copy-done.7
  24.4 1.4 %cross_0.1 = (bf16[16,1152]{1,0:T(8,128)(2,1)S(1)}, bf16[256,1152]{1,0:T(8,128)(2,1)S(1)}, bf16[256,1152]{1,0:T(8,128)(2,1)S(1)}, bf16[256,1152]{1,0:T(8,128)(2,1)S(1)}, f32[3,4,32,128]{3,2,1,0:T(8,128)S(1)}) custom-call(s32[1]{0:T(128)S(6)} %sub.11.live_ref, bf16[256,1152]{1,0:T(8,128)(2,1)S(1)} %collective-permute-done.q_ref, ...), custom_call_target="tpu_custom_call" | custom-call | flops 1024 | bytes 1024 | tf_op jit(solution)/shard_map/cross_0/pallas_call | solution.py:362
  25.8 3.1 %collective-permute-done.2.g_ref = bf16[272,384]{1,0:T(8,128)(2,1)S(1)} collective-permute-done((bf16[272,384]{1,0:T(8,128)(2,1)}, bf16[272,384]{1,0:T(8,128)(2,1)S(1)}, u32[]{:S(2)}, u32[]{:S(2)}) %collective-permute-start.2) | collective-permute-done | bytes 208928 | tf_op jit(solution)/shard_map/ppermute | solution.py:32
  28.8 0.0 copy-start.8
  28.8 1.4 %cross_1.1 = (bf16[16,1152]{1,0:T(8,128)(2,1)S(1)}, bf16[256,1152]{1,0:T(8,128)(2,1)S(1)}, bf16[256,1152]{1,0:T(8,128)(2,1)S(1)}, bf16[256,1152]{1,0:T(8,128)(2,1)S(1)}, f32[3,4,32,128]{3,2,1,0:T(8,128)S(1)}) custom-call(s32[1]{0:T(128)S(6)} %sub.11.live_ref, ...), custom_call_target="tpu_custom_call", output_to_operand_aliasing={{0}: (6, {}), {1}: (7, {}), {2}: (8, {}), {3}: (9, {}), {4}... | custom-call | flops 1024 | bytes 1024 | tf_op jit(solution)/shard_map/cross_1/pallas_call | solution.py:362
  30.2 2.2 %collective-permute-done.1.g_ref = bf16[272,384]{1,0:T(8,128)(2,1)S(1)} collective-permute-done((bf16[272,384]{1,0:T(8,128)(2,1)}, bf16[272,384]{1,0:T(8,128)(2,1)S(1)}, u32[]{:S(2)}, u32[]{:S(2)}) %collective-permute-start.1) | collective-permute-done | bytes 208928 | tf_op jit(solution)/shard_map/ppermute | solution.py:32
  32.5 1.4 %cross_2.1 = (bf16[16,1152]{1,0:T(8,128)(2,1)S(1)}, bf16[256,1152]{1,0:T(8,128)(2,1)S(1)}, bf16[256,1152]{1,0:T(8,128)(2,1)S(1)}, bf16[256,1152]{1,0:T(8,128)(2,1)S(1)}, f32[3,4,32,128]{3,2,1,0:T(8,128)S(1)}) custom-call(s32[1]{0:T(128)S(6)} %sub.11.live_ref, ...), custom_call_target="tpu_custom_call", output_to_operand_aliasing={{0}: (6, {}), {1}: (7, {}), {2}: (8, {}), {3}: (9, {}), {4}... | custom-call | flops 1024 | bytes 1024 | tf_op jit(solution)/shard_map/cross_2/pallas_call | solution.py:362
  33.9 4.5 %collective-permute-start.4 = (bf16[16,1152]{1,0:T(8,128)(2,1)S(1)}, bf16[16,1152]{1,0:T(8,128)(2,1)S(1)}, u32[]{:S(2)}, u32[]{:S(2)}) collective-permute-start(bf16[16,1152]{1,0:T(8,128)(2,1)S(1)} %get-tuple-element.59), channel_id=1, source_target_pairs={{0,1},{1,2},{2,3},{3,4},{4,5},{5,6},{6,7},{8,9},{9,10},{10,11},{11... | collective-permute-start | bytes 110600 | tf_op jit(solution)/shard_map/ppermute | solution.py:32
  38.4 2.6 %collective-permute-start.5 = (bf16[256,1152]{1,0:T(8,128)(2,1)S(1)}, bf16[256,1152]{1,0:T(8,128)(2,1)S(1)}, u32[]{:S(2)}, u32[]{:S(2)}) collective-permute-start(bf16[256,1152]{1,0:T(8,128)(2,1)S(1)} %get-tuple-element.64), channel_id=1, source_target_pairs={{0,1},{1,2},{2,3},{3,4},{4,5},{5,6},{6,7},{8,9},{9,10},{10,11},{11... | collective-permute-start | bytes 1769480 | tf_op jit(solution)/shard_map/ppermute | solution.py:32
  41.0 0.0 collective-permute-done.4.given_ref
  41.0 3.9 %own.1 = (f32[256,1152]{1,0:T(8,128)S(1)}, bf16[256,1152]{1,0:T(8,128)(2,1)}, bf16[256,1152]{1,0:T(8,128)(2,1)}, f32[32,1,384]{2,1,0:T(1,128)S(1)}) custom-call(s32[1]{0:T(128)S(6)} %sub.10.live_ref, bf16[256,1152]{1,0:T(8,128)(2,1)S(1)} %bitcast.25, bf16[256,1152]{1,0:T(8,128)(2,1)S(1)} %bitcast.29, bf16[256,1152]{1,0:T(8,128)(2,1)S(1)} %bitcast.20, ...), custom_call_target="tpu_custom_call" | custom-call | flops 99999997952 | bytes 1024 | tf_op jit(solution)/shard_map/own/pallas_call | solution.py:379
  44.9 12.1 %all_to_all.10.terms_ref = f32[32,1,384]{2,1,0:T(1,128)S(1)} all-to-all(f32[32,1,384]{2,1,0:T(1,128)S(1)} %get-tuple-element.67), channel_id=1, replica_groups=mesh['dp'=4,'tm'=8] {'dp','tm'}, dimensions={0} | all-to-all | bytes 98304 | tf_op jit(solution)/shard_map/all_to_all | solution.py:403
  57.1 0.7 spread.1
  57.7 3.9 %all-to-all-start.1 = ((f32[32,1,384]{2,1,0:T(1,128)}), f32[32,1,384]{2,1,0:T(1,128)S(1)}, u32[]{:S(2)}, u32[]{:S(2)}) async-start(f32[32,1,384]{2,1,0:T(1,128)} %spread.1), calls=%async_computation.1 | async-start | bytes 98304 | tf_op jit(solution)/shard_map/all_to_all | solution.py:404
  61.7 0.0 collective-permute-done.5
  61.7 0.1 add_convert_fusion._
  61.8 0.0 copy-start.6
  61.8 7.1 %all-to-all-done.1.parts_ref = f32[32,1,384]{2,1,0:T(1,128)S(1)} async-done(((f32[32,1,384]{2,1,0:T(1,128)}), f32[32,1,384]{2,1,0:T(1,128)S(1)}, u32[]{:S(2)}, u32[]{:S(2)}) %all-to-all-start.1) | async-done | bytes 49184 | tf_op jit(solution)/shard_map/all_to_all | solution.py:404
  68.9 0.6 gather.1
  (11 shorter events, 0.0 us)
Async XLA Ops:
  0.6 23.7 %collective-permute-start = (bf16[256,1152]{1,0:T(8,128)(2,1)}, bf16[256,1152]{1,0:T(8,128)(2,1)S(1)}, u32[]{:S(2)}, u32[]{:S(2)}) collective-permute-start(bf16[256,1152]{1,0:T(8,128)(2,1)} %bitcast.21), channel_id=1, source_target_pairs={{1,0},{2,1},{3,2},{4,3},{5,4},{6,5},{7,6},{9,8},{10,9},{11,10},{12... | collective-permute-start | bytes 1769480 | tf_op jit(solution)/shard_map/ppermute | solution.py:32
  6.1 18.3 %collective-permute-start.3 = (bf16[272,384]{1,0:T(8,128)(2,1)}, bf16[272,384]{1,0:T(8,128)(2,1)S(1)}, u32[]{:S(2)}, u32[]{:S(2)}) collective-permute-start(bf16[272,384]{1,0:T(8,128)(2,1)} %get-tuple-element.48), channel_id=1, source_target_pairs={{1,0},{2,1},{3,2},{4,3},{5,4},{6,5},{7,6},{9,8},{10,9},{11,10},{12... | collective-permute-start | bytes 626696 | tf_op jit(solution)/shard_map/ppermute | solution.py:32
  10.6 18.2 %collective-permute-start.2 = (bf16[272,384]{1,0:T(8,128)(2,1)}, bf16[272,384]{1,0:T(8,128)(2,1)S(1)}, u32[]{:S(2)}, u32[]{:S(2)}) collective-permute-start(bf16[272,384]{1,0:T(8,128)(2,1)} %get-tuple-element.47), channel_id=1, source_target_pairs={{1,0},{2,1},{3,2},{4,3},{5,4},{6,5},{7,6},{9,8},{10,9},{11,10},{12... | collective-permute-start | bytes 626696 | tf_op jit(solution)/shard_map/ppermute | solution.py:32
  11.9 12.4 %copy-start = (bf16[1,256,1152]{2,1,0:T(8,128)(2,1)S(1)}, bf16[1,256,1152]{2,1,0:T(8,128)(2,1)}, u32[]{:S(2)}) copy-start(bf16[1,256,1152]{2,1,0:T(8,128)(2,1)} %param.8) | copy-start | bytes 1769476
  11.9 12.4 %copy-start.1 = (bf16[1,256,1152]{2,1,0:T(8,128)(2,1)S(1)}, bf16[1,256,1152]{2,1,0:T(8,128)(2,1)}, u32[]{:S(2)}) copy-start(bf16[1,256,1152]{2,1,0:T(8,128)(2,1)} %param.7) | copy-start | bytes 1769476
  11.9 12.4 %copy-start.7 = (f32[12,768]{1,0:T(8,128)S(1)}, f32[12,768]{1,0:T(8,128)}, u32[]{:S(2)}) copy-start(f32[12,768]{1,0:T(8,128)} %get-tuple-element.36.bias_ref.w_ref) | copy-start | bytes 110596
  15.3 17.2 %collective-permute-start.1 = (bf16[272,384]{1,0:T(8,128)(2,1)}, bf16[272,384]{1,0:T(8,128)(2,1)S(1)}, u32[]{:S(2)}, u32[]{:S(2)}) collective-permute-start(bf16[272,384]{1,0:T(8,128)(2,1)} %get-tuple-element.46), channel_id=1, source_target_pairs={{1,0},{2,1},{3,2},{4,3},{5,4},{6,5},{7,6},{9,8},{10,9},{11,10},{12... | collective-permute-start | bytes 626696 | tf_op jit(solution)/shard_map/ppermute | solution.py:32
  28.8 12.2 %copy-start.2 = (f32[12,256,256]{2,1,0:T(8,128)S(1)}, f32[12,256,256]{2,1,0:T(8,128)}, u32[]{:S(2)}) copy-start(f32[12,256,256]{2,1,0:T(8,128)} %get-tuple-element.43.e_ref) | copy-start | bytes 9437188
  28.8 12.2 %copy-start.3 = (f32[12,256,256]{2,1,0:T(8,128)S(1)}, f32[12,256,256]{2,1,0:T(8,128)}, u32[]{:S(2)}) copy-start(f32[12,256,256]{2,1,0:T(8,128)} %get-tuple-element.44.dp_ref) | copy-start | bytes 9437188
  28.8 12.2 %copy-start.4 = (bf16[1,256,1152]{2,1,0:T(8,128)(2,1)S(1)}, bf16[1,256,1152]{2,1,0:T(8,128)(2,1)}, u32[]{:S(2)}) copy-start(bf16[1,256,1152]{2,1,0:T(8,128)(2,1)} %param.6) | copy-start | bytes 1769476
  28.8 12.2 %copy-start.5 = (bf16[1,256,1152]{2,1,0:T(8,128)(2,1)S(1)}, bf16[1,256,1152]{2,1,0:T(8,128)(2,1)}, u32[]{:S(2)}) copy-start(bf16[1,256,1152]{2,1,0:T(8,128)(2,1)} %param.9) | copy-start | bytes 1769476
  28.8 12.2 %copy-start.8 = (f32[3,16,256]{2,1,0:T(8,128)S(1)}, f32[3,16,256]{2,1,0:T(8,128)}, u32[]{:S(2)}) copy-start(f32[3,16,256]{2,1,0:T(8,128)} %get-tuple-element.45.near_ref) | copy-start | bytes 147460
  33.9 7.1 %collective-permute-start.4 = (bf16[16,1152]{1,0:T(8,128)(2,1)S(1)}, bf16[16,1152]{1,0:T(8,128)(2,1)S(1)}, u32[]{:S(2)}, u32[]{:S(2)}) collective-permute-start(bf16[16,1152]{1,0:T(8,128)(2,1)S(1)} %get-tuple-element.59), channel_id=1, source_target_pairs={{0,1},{1,2},{2,3},{3,4},{4,5},{5,6},{6,7},{8,9},{9,10},{10,11},{11... | collective-permute-start | bytes 110600 | tf_op jit(solution)/shard_map/ppermute | solution.py:32
  38.4 23.3 %collective-permute-start.5 = (bf16[256,1152]{1,0:T(8,128)(2,1)S(1)}, bf16[256,1152]{1,0:T(8,128)(2,1)S(1)}, u32[]{:S(2)}, u32[]{:S(2)}) collective-permute-start(bf16[256,1152]{1,0:T(8,128)(2,1)S(1)} %get-tuple-element.64), channel_id=1, source_target_pairs={{0,1},{1,2},{2,3},{3,4},{4,5},{5,6},{6,7},{8,9},{9,10},{10,11},{11... | collective-permute-start | bytes 1769480 | tf_op jit(solution)/shard_map/ppermute | solution.py:32
  57.7 11.2 %all-to-all-start.1 = ((f32[32,1,384]{2,1,0:T(1,128)}), f32[32,1,384]{2,1,0:T(1,128)S(1)}, u32[]{:S(2)}, u32[]{:S(2)}) async-start(f32[32,1,384]{2,1,0:T(1,128)} %spread.1), calls=%async_computation.1 | async-start | bytes 98304 | tf_op jit(solution)/shard_map/all_to_all | solution.py:404
  61.8 7.8 %copy-start.6 = (bf16[256,1152]{1,0:T(8,128)(2,1)}, bf16[256,1152]{1,0:T(8,128)(2,1)S(1)}, u32[]{:S(2)}) copy-start(bf16[256,1152]{1,0:T(8,128)(2,1)S(1)} %add_convert_fusion._) | copy-start | bytes 1769476

commit v2 on v1

--- a/solution.py
+++ b/solution.py
@@ -231,11 +231,19 @@
         out_ref[part] = total
 
 
-def gather_kernel(parts_ref, _, out_ref):
+def gather_kernel(count, every_ref, _, out_ref):
+    terms = every_ref.shape[0] // count
+    shape_of_parts = (count,) + every_ref.shape[1:]
+    totals = []
+    for part in range(count):
+        total = every_ref[part * terms]
+        for term in range(1, terms):
+            total = total + every_ref[part * terms + term]
+        totals.append(total)
     for row in range(out_ref.shape[0]):
         for tile in range(ROW_TILES):
-            part, lanes = place(row, tile, parts_ref.shape)
-            out_ref[row : row + 1, 128 * tile : 128 * tile + 128] = parts_ref[part, :, lanes]
+            part, lanes = place(row, tile, shape_of_parts)
+            out_ref[row : row + 1, 128 * tile : 128 * tile + 128] = totals[part][:, lanes]
 
 
 def own_kernel(
@@ -399,11 +407,13 @@
     )(terms)
 
 
-def sum_over_devices(parts, axes, heads, after):
-    terms = lax.all_to_all(parts, axes, 0, 0)
-    every = lax.all_to_all(spread(terms, parts.shape[0]), axes, 0, 0)
+def sum_over_devices(parts, inner, outer, heads, after):
+    count = parts.shape[0]
+    terms = lax.all_to_all(parts, inner, 0, 0)
+    sums = spread(terms, count * lax.axis_size(outer))
+    every = lax.all_to_all(sums, (inner, outer), 0, 0)
     return pl.pallas_call(
-        gather_kernel,
+        functools.partial(gather_kernel, count),
         in_specs=[VMEM, ANY],
         out_shape=shape((heads, 3 * BLOCK)),
         compiler_params=params(),
@@ -434,10 +444,10 @@
     given, dq_cross, dkc, dvc, lines = results
     given = shifted(given, "tm", 1)
     dq_cross = shifted(dq_cross, "tm", 1)
-    parts = lax.axis_size("dp") * lax.axis_size("tm")
+    parts = lax.axis_size("dp")
     dq_own, dk, dv, table = own(head_width, live_own, q, g, k, e, dp, near, given, dkc, dvc, lines, parts)
     dq = (dq_own + dq_cross.astype(jnp.float32)).astype(HALF)
-    bias_grad = sum_over_devices(table, ("dp", "tm"), head_count, dq)
+    bias_grad = sum_over_devices(table, "dp", "tm", head_count, dq)
     return tuple(a[None] for a in (dq, dk, dv)) + (bias_grad,)
 
 

time: 69.9 us -> 68.9 us (0.986)
  blocking collectives: 12.1 us -> 6.51 us
  waiting for transfers between devices: 20.1 us -> 24.4 us
    all_to_all x1, blocking collectives: 12.1 us -> 6.51 us  [sum_over_devices(): terms = lax.all_to_all(parts, inner, 0, 0)]
    all_to_all x1, waiting for transfers between devices: 7.1 us -> 11.3 us  [sum_over_devices(): every = lax.all_to_all(sums, (inner, outer), 0, 0)]
  transfers between devices with their start and end apart: 7 -> 7, of which waited for: 4 -> 4; matrix products, arithmetic and copies ran while one was open for 0% -> 0% of each run, Pallas kernels for 25% -> 26%
where the time goes in v2:
time: 68.9 us; the launch traced here: 68.5 us
  waiting for transfers between devices  24.4 us (35%)
  Pallas kernels  19.6 us (28%)
  starting transfers between devices  16.4 us (24%)
  blocking collectives  6.51 us (9%)
  between operations  1.48 us (2%)
    ppermute x6, waiting for transfers between devices, shifted(): return lax.ppermute(x, axis, pairs)  13.1 us
    ppermute x6, starting transfers between devices, shifted(): return lax.ppermute(x, axis, pairs)  12.2 us
    all_to_all x1, waiting for transfers between devices, sum_over_devices(): every = lax.all_to_all(sums, (inner, outer), 0, 0)  11.3 us
    pallas_call x3, Pallas kernels, own_stats(): pl.pallas_call(functools.partial(own_stats_kernel, head_width, group), gr...  10.1 us
    all_to_all x1, blocking collectives, sum_over_devices(): terms = lax.all_to_all(parts, inner, 0, 0)  6.51 us
    all_to_all x1, starting transfers between devices, sum_over_devices(): every = lax.all_to_all(sums, (inner, outer), 0, 0)  4.18 us
    pallas_call x3, Pallas kernels, cross(): pl.pallas_call(functools.partial(cross_kernel, head_width, group), grid=(...  4.16 us
    pallas_call x1, Pallas kernels, own(): pl.pallas_call(functools.partial(own_kernel, groups, head_width), grid=(g...  3.93 us
  transfers between devices with their start and end apart: 7, of which 4 were waited for; matrix products, arithmetic and copies ran while one was open for 0% of the time, Pallas kernels for 26%

profile of v2, /device:TPU:0, one launch (start us, length us, event | category | flops | bytes accessed | tf_op | source)
XLA Modules:
  0.0 68.5 jit_solution(11129864378134810125)
XLA Ops:
  0.6 1.3 %collective-permute-start = (bf16[256,1152]{1,0:T(8,128)(2,1)}, bf16[256,1152]{1,0:T(8,128)(2,1)S(1)}, u32[]{:S(2)}, u32[]{:S(2)}) collective-permute-start(bf16[256,1152]{1,0:T(8,128)(2,1)} %bitcast.21), channel_id=1, source_target_pairs={{1,0},{2,1},{3,2},{4,3},{5,4},{6,5},{7,6},{9,8},{10,9},{11,10},{12... | collective-permute-start | bytes 1769480 | tf_op jit(solution)/shard_map/ppermute | solution.py:32
  2.6 3.5 %own_stats_0.1 = (f32[3,16,256]{2,1,0:T(8,128)}, f32[12,256,256]{2,1,0:T(8,128)}, f32[12,256,256]{2,1,0:T(8,128)}, bf16[272,384]{1,0:T(8,128)(2,1)}, f32[12,768]{1,0:T(8,128)}) custom-call(s32[1]{0:T(128)S(6)} %sub.10.live_ref, bf16[256,1152]{1,0:T(8,128)(2,1)} %bitcast.22, bf16[256,1152]{1,0:T(8,128)(2,1)} %bitcast.26, bf16[256,1152]{1,0:T(8,128)(2,1)} %bitcast.14, ...), custom_call_target="tpu_custom_call" | custom-call | flops 1024 | bytes 1024 | tf_op jit(solution)/shard_map/own_stats_0/pallas_call | solution.py:354
  6.1 1.3 %collective-permute-start.3 = (bf16[272,384]{1,0:T(8,128)(2,1)}, bf16[272,384]{1,0:T(8,128)(2,1)S(1)}, u32[]{:S(2)}, u32[]{:S(2)}) collective-permute-start(bf16[272,384]{1,0:T(8,128)(2,1)} %get-tuple-element.48), channel_id=1, source_target_pairs={{1,0},{2,1},{3,2},{4,3},{5,4},{6,5},{7,6},{9,8},{10,9},{11,10},{12... | collective-permute-start | bytes 626696 | tf_op jit(solution)/shard_map/ppermute | solution.py:32
  7.3 3.3 %own_stats_1.1 = (f32[3,16,256]{2,1,0:T(8,128)}, f32[12,256,256]{2,1,0:T(8,128)}, f32[12,256,256]{2,1,0:T(8,128)}, bf16[272,384]{1,0:T(8,128)(2,1)}) custom-call(s32[1]{0:T(128)S(6)} %sub.10.live_ref, bf16[256,1152]{1,0:T(8,128)(2,1)} %bitcast.23, bf16[256,1152]{1,0:T(8,128)(2,1)} %bitcast.27, ...), custom_call_target="tpu_custom_call", output_to_operand_aliasing={{0}: (6, {}), {1}: (7, {}), {2}: (8, {})} | custom-call | flops 1024 | bytes 1024 | tf_op jit(solution)/shard_map/own_stats_1/pallas_call | solution.py:354
  10.6 1.3 %collective-permute-start.2 = (bf16[272,384]{1,0:T(8,128)(2,1)}, bf16[272,384]{1,0:T(8,128)(2,1)S(1)}, u32[]{:S(2)}, u32[]{:S(2)}) collective-permute-start(bf16[272,384]{1,0:T(8,128)(2,1)} %get-tuple-element.47), channel_id=1, source_target_pairs={{1,0},{2,1},{3,2},{4,3},{5,4},{6,5},{7,6},{9,8},{10,9},{11,10},{12... | collective-permute-start | bytes 626696 | tf_op jit(solution)/shard_map/ppermute | solution.py:32
  11.9 0.0 copy-start
  11.9 0.0 copy-start.1
  11.9 0.0 copy-start.7
  11.9 3.4 %own_stats_2.1 = (f32[3,16,256]{2,1,0:T(8,128)}, f32[12,256,256]{2,1,0:T(8,128)}, f32[12,256,256]{2,1,0:T(8,128)}, bf16[272,384]{1,0:T(8,128)(2,1)}) custom-call(s32[1]{0:T(128)S(6)} %sub.10.live_ref, bf16[256,1152]{1,0:T(8,128)(2,1)} %bitcast.24, bf16[256,1152]{1,0:T(8,128)(2,1)} %bitcast.28, ...), custom_call_target="tpu_custom_call", output_to_operand_aliasing={{0}: (6, {}), {1}: (7, {}), {2}: (8, {})} | custom-call | flops 1024 | bytes 1024 | tf_op jit(solution)/shard_map/own_stats_2/pallas_call | solution.py:354
  15.3 1.3 %collective-permute-start.1 = (bf16[272,384]{1,0:T(8,128)(2,1)}, bf16[272,384]{1,0:T(8,128)(2,1)S(1)}, u32[]{:S(2)}, u32[]{:S(2)}) collective-permute-start(bf16[272,384]{1,0:T(8,128)(2,1)} %get-tuple-element.46), channel_id=1, source_target_pairs={{1,0},{2,1},{3,2},{4,3},{5,4},{6,5},{7,6},{9,8},{10,9},{11,10},{12... | collective-permute-start | bytes 626696 | tf_op jit(solution)/shard_map/ppermute | solution.py:32
  16.6 7.7 %collective-permute-done.3.g_ref = bf16[272,384]{1,0:T(8,128)(2,1)S(1)} collective-permute-done((bf16[272,384]{1,0:T(8,128)(2,1)}, bf16[272,384]{1,0:T(8,128)(2,1)S(1)}, u32[]{:S(2)}, u32[]{:S(2)}) %collective-permute-start.3) | collective-permute-done | bytes 208928 | tf_op jit(solution)/shard_map/ppermute | solution.py:32
  24.3 0.0 collective-permute-done.q_ref
  24.3 0.0 copy-done
  24.4 0.0 copy-done.7
  24.4 1.4 %cross_0.1 = (bf16[16,1152]{1,0:T(8,128)(2,1)S(1)}, bf16[256,1152]{1,0:T(8,128)(2,1)S(1)}, bf16[256,1152]{1,0:T(8,128)(2,1)S(1)}, bf16[256,1152]{1,0:T(8,128)(2,1)S(1)}, f32[3,4,32,128]{3,2,1,0:T(8,128)S(1)}) custom-call(s32[1]{0:T(128)S(6)} %sub.11.live_ref, bf16[256,1152]{1,0:T(8,128)(2,1)S(1)} %collective-permute-done.q_ref, ...), custom_call_target="tpu_custom_call" | custom-call | flops 1024 | bytes 1024 | tf_op jit(solution)/shard_map/cross_0/pallas_call | solution.py:370
  25.8 3.1 %collective-permute-done.2.g_ref = bf16[272,384]{1,0:T(8,128)(2,1)S(1)} collective-permute-done((bf16[272,384]{1,0:T(8,128)(2,1)}, bf16[272,384]{1,0:T(8,128)(2,1)S(1)}, u32[]{:S(2)}, u32[]{:S(2)}) %collective-permute-start.2) | collective-permute-done | bytes 208928 | tf_op jit(solution)/shard_map/ppermute | solution.py:32
  28.8 0.0 copy-start.8
  28.8 1.4 %cross_1.1 = (bf16[16,1152]{1,0:T(8,128)(2,1)S(1)}, bf16[256,1152]{1,0:T(8,128)(2,1)S(1)}, bf16[256,1152]{1,0:T(8,128)(2,1)S(1)}, bf16[256,1152]{1,0:T(8,128)(2,1)S(1)}, f32[3,4,32,128]{3,2,1,0:T(8,128)S(1)}) custom-call(s32[1]{0:T(128)S(6)} %sub.11.live_ref, ...), custom_call_target="tpu_custom_call", output_to_operand_aliasing={{0}: (6, {}), {1}: (7, {}), {2}: (8, {}), {3}: (9, {}), {4}... | custom-call | flops 1024 | bytes 1024 | tf_op jit(solution)/shard_map/cross_1/pallas_call | solution.py:370
  30.2 2.2 %collective-permute-done.1.g_ref = bf16[272,384]{1,0:T(8,128)(2,1)S(1)} collective-permute-done((bf16[272,384]{1,0:T(8,128)(2,1)}, bf16[272,384]{1,0:T(8,128)(2,1)S(1)}, u32[]{:S(2)}, u32[]{:S(2)}) %collective-permute-start.1) | collective-permute-done | bytes 208928 | tf_op jit(solution)/shard_map/ppermute | solution.py:32
  32.5 1.4 %cross_2.1 = (bf16[16,1152]{1,0:T(8,128)(2,1)S(1)}, bf16[256,1152]{1,0:T(8,128)(2,1)S(1)}, bf16[256,1152]{1,0:T(8,128)(2,1)S(1)}, bf16[256,1152]{1,0:T(8,128)(2,1)S(1)}, f32[3,4,32,128]{3,2,1,0:T(8,128)S(1)}) custom-call(s32[1]{0:T(128)S(6)} %sub.11.live_ref, ...), custom_call_target="tpu_custom_call", output_to_operand_aliasing={{0}: (6, {}), {1}: (7, {}), {2}: (8, {}), {3}: (9, {}), {4}... | custom-call | flops 1024 | bytes 1024 | tf_op jit(solution)/shard_map/cross_2/pallas_call | solution.py:370
  33.9 4.5 %collective-permute-start.4 = (bf16[16,1152]{1,0:T(8,128)(2,1)S(1)}, bf16[16,1152]{1,0:T(8,128)(2,1)S(1)}, u32[]{:S(2)}, u32[]{:S(2)}) collective-permute-start(bf16[16,1152]{1,0:T(8,128)(2,1)S(1)} %get-tuple-element.59), channel_id=1, source_target_pairs={{0,1},{1,2},{2,3},{3,4},{4,5},{5,6},{6,7},{8,9},{9,10},{10,11},{11... | collective-permute-start | bytes 110600 | tf_op jit(solution)/shard_map/ppermute | solution.py:32
  38.4 2.6 %collective-permute-start.5 = (bf16[256,1152]{1,0:T(8,128)(2,1)S(1)}, bf16[256,1152]{1,0:T(8,128)(2,1)S(1)}, u32[]{:S(2)}, u32[]{:S(2)}) collective-permute-start(bf16[256,1152]{1,0:T(8,128)(2,1)S(1)} %get-tuple-element.64), channel_id=1, source_target_pairs={{0,1},{1,2},{2,3},{3,4},{4,5},{5,6},{6,7},{8,9},{9,10},{10,11},{11... | collective-permute-start | bytes 1769480 | tf_op jit(solution)/shard_map/ppermute | solution.py:32
  41.0 0.0 collective-permute-done.4.given_ref
  41.0 3.9 %own.1 = (f32[256,1152]{1,0:T(8,128)S(1)}, bf16[256,1152]{1,0:T(8,128)(2,1)}, bf16[256,1152]{1,0:T(8,128)(2,1)}, f32[4,1,2304]{2,1,0:T(1,128)S(1)}) custom-call(s32[1]{0:T(128)S(6)} %sub.10.live_ref, bf16[256,1152]{1,0:T(8,128)(2,1)S(1)} %bitcast.25, bf16[256,1152]{1,0:T(8,128)(2,1)S(1)} %bitcast.29, bf16[256,1152]{1,0:T(8,128)(2,1)S(1)} %bitcast.20, ...), custom_call_target="tpu_custom_call" | custom-call | flops 99999997952 | bytes 1024 | tf_op jit(solution)/shard_map/own/pallas_call | solution.py:387
  45.0 6.5 %all_to_all.10.terms_ref = f32[4,1,2304]{2,1,0:T(1,128)S(1)} all-to-all(f32[4,1,2304]{2,1,0:T(1,128)S(1)} %get-tuple-element.67), channel_id=1, replica_groups=mesh['dp'=4,'tm'=8] {'dp'}, dimensions={0} | all-to-all | bytes 73728 | tf_op jit(solution)/shard_map/all_to_all | solution.py:412
  51.5 0.7 %spread.1 = f32[32,1,2304]{2,1,0:T(1,128)} custom-call(f32[4,1,2304]{2,1,0:T(1,128)S(1)} %all_to_all.10.terms_ref), custom_call_target="tpu_custom_call" | custom-call | flops 1024 | bytes 1024 | tf_op jit(solution)/shard_map/spread/pallas_call | solution.py:401
  52.2 4.2 %all-to-all-start.1 = ((f32[32,1,2304]{2,1,0:T(1,128)}), f32[32,1,2304]{2,1,0:T(1,128)S(1)}, u32[]{:S(2)}, u32[]{:S(2)}) async-start(f32[32,1,2304]{2,1,0:T(1,128)} %spread.1), calls=%async_computation.1 | async-start | bytes 589824 | tf_op jit(solution)/shard_map/all_to_all | solution.py:414
  56.4 0.0 collective-permute-done.5
  56.4 0.1 add_convert_fusion._
  56.5 0.0 copy-start.6
  56.6 11.3 %all-to-all-done.1.every_ref = f32[32,1,2304]{2,1,0:T(1,128)S(1)} async-done(((f32[32,1,2304]{2,1,0:T(1,128)}), f32[32,1,2304]{2,1,0:T(1,128)S(1)}, u32[]{:S(2)}, u32[]{:S(2)}) %all-to-all-start.1) | async-done | bytes 294944 | tf_op jit(solution)/shard_map/all_to_all | solution.py:414
  67.9 0.7 gather.1
  (11 shorter events, 0.0 us)
Async XLA Ops:
  0.6 23.7 %collective-permute-start = (bf16[256,1152]{1,0:T(8,128)(2,1)}, bf16[256,1152]{1,0:T(8,128)(2,1)S(1)}, u32[]{:S(2)}, u32[]{:S(2)}) collective-permute-start(bf16[256,1152]{1,0:T(8,128)(2,1)} %bitcast.21), channel_id=1, source_target_pairs={{1,0},{2,1},{3,2},{4,3},{5,4},{6,5},{7,6},{9,8},{10,9},{11,10},{12... | collective-permute-start | bytes 1769480 | tf_op jit(solution)/shard_map/ppermute | solution.py:32
  6.1 18.3 %collective-permute-start.3 = (bf16[272,384]{1,0:T(8,128)(2,1)}, bf16[272,384]{1,0:T(8,128)(2,1)S(1)}, u32[]{:S(2)}, u32[]{:S(2)}) collective-permute-start(bf16[272,384]{1,0:T(8,128)(2,1)} %get-tuple-element.48), channel_id=1, source_target_pairs={{1,0},{2,1},{3,2},{4,3},{5,4},{6,5},{7,6},{9,8},{10,9},{11,10},{12... | collective-permute-start | bytes 626696 | tf_op jit(solution)/shard_map/ppermute | solution.py:32
  10.6 18.2 %collective-permute-start.2 = (bf16[272,384]{1,0:T(8,128)(2,1)}, bf16[272,384]{1,0:T(8,128)(2,1)S(1)}, u32[]{:S(2)}, u32[]{:S(2)}) collective-permute-start(bf16[272,384]{1,0:T(8,128)(2,1)} %get-tuple-element.47), channel_id=1, source_target_pairs={{1,0},{2,1},{3,2},{4,3},{5,4},{6,5},{7,6},{9,8},{10,9},{11,10},{12... | collective-permute-start | bytes 626696 | tf_op jit(solution)/shard_map/ppermute | solution.py:32
  11.9 12.4 %copy-start = (bf16[1,256,1152]{2,1,0:T(8,128)(2,1)S(1)}, bf16[1,256,1152]{2,1,0:T(8,128)(2,1)}, u32[]{:S(2)}) copy-start(bf16[1,256,1152]{2,1,0:T(8,128)(2,1)} %param.8) | copy-start | bytes 1769476
  11.9 12.4 %copy-start.1 = (bf16[1,256,1152]{2,1,0:T(8,128)(2,1)S(1)}, bf16[1,256,1152]{2,1,0:T(8,128)(2,1)}, u32[]{:S(2)}) copy-start(bf16[1,256,1152]{2,1,0:T(8,128)(2,1)} %param.7) | copy-start | bytes 1769476
  11.9 12.4 %copy-start.7 = (f32[12,768]{1,0:T(8,128)S(1)}, f32[12,768]{1,0:T(8,128)}, u32[]{:S(2)}) copy-start(f32[12,768]{1,0:T(8,128)} %get-tuple-element.36.bias_ref.w_ref) | copy-start | bytes 110596
  15.3 17.2 %collective-permute-start.1 = (bf16[272,384]{1,0:T(8,128)(2,1)}, bf16[272,384]{1,0:T(8,128)(2,1)S(1)}, u32[]{:S(2)}, u32[]{:S(2)}) collective-permute-start(bf16[272,384]{1,0:T(8,128)(2,1)} %get-tuple-element.46), channel_id=1, source_target_pairs={{1,0},{2,1},{3,2},{4,3},{5,4},{6,5},{7,6},{9,8},{10,9},{11,10},{12... | collective-permute-start | bytes 626696 | tf_op jit(solution)/shard_map/ppermute | solution.py:32
  28.8 12.2 %copy-start.2 = (f32[12,256,256]{2,1,0:T(8,128)S(1)}, f32[12,256,256]{2,1,0:T(8,128)}, u32[]{:S(2)}) copy-start(f32[12,256,256]{2,1,0:T(8,128)} %get-tuple-element.43.e_ref) | copy-start | bytes 9437188
  28.8 12.2 %copy-start.3 = (f32[12,256,256]{2,1,0:T(8,128)S(1)}, f32[12,256,256]{2,1,0:T(8,128)}, u32[]{:S(2)}) copy-start(f32[12,256,256]{2,1,0:T(8,128)} %get-tuple-element.44.dp_ref) | copy-start | bytes 9437188
  28.8 12.2 %copy-start.4 = (bf16[1,256,1152]{2,1,0:T(8,128)(2,1)S(1)}, bf16[1,256,1152]{2,1,0:T(8,128)(2,1)}, u32[]{:S(2)}) copy-start(bf16[1,256,1152]{2,1,0:T(8,128)(2,1)} %param.6) | copy-start | bytes 1769476
  28.8 12.2 %copy-start.5 = (bf16[1,256,1152]{2,1,0:T(8,128)(2,1)S(1)}, bf16[1,256,1152]{2,1,0:T(8,128)(2,1)}, u32[]{:S(2)}) copy-start(bf16[1,256,1152]{2,1,0:T(8,128)(2,1)} %param.9) | copy-start | bytes 1769476
  28.8 12.2 %copy-start.8 = (f32[3,16,256]{2,1,0:T(8,128)S(1)}, f32[3,16,256]{2,1,0:T(8,128)}, u32[]{:S(2)}) copy-start(f32[3,16,256]{2,1,0:T(8,128)} %get-tuple-element.45.near_ref) | copy-start | bytes 147460
  33.9 7.1 %collective-permute-start.4 = (bf16[16,1152]{1,0:T(8,128)(2,1)S(1)}, bf16[16,1152]{1,0:T(8,128)(2,1)S(1)}, u32[]{:S(2)}, u32[]{:S(2)}) collective-permute-start(bf16[16,1152]{1,0:T(8,128)(2,1)S(1)} %get-tuple-element.59), channel_id=1, source_target_pairs={{0,1},{1,2},{2,3},{3,4},{4,5},{5,6},{6,7},{8,9},{9,10},{10,11},{11... | collective-permute-start | bytes 110600 | tf_op jit(solution)/shard_map/ppermute | solution.py:32
  38.4 18.0 %collective-permute-start.5 = (bf16[256,1152]{1,0:T(8,128)(2,1)S(1)}, bf16[256,1152]{1,0:T(8,128)(2,1)S(1)}, u32[]{:S(2)}, u32[]{:S(2)}) collective-permute-start(bf16[256,1152]{1,0:T(8,128)(2,1)S(1)} %get-tuple-element.64), channel_id=1, source_target_pairs={{0,1},{1,2},{2,3},{3,4},{4,5},{5,6},{6,7},{8,9},{9,10},{10,11},{11... | collective-permute-start | bytes 1769480 | tf_op jit(solution)/shard_map/ppermute | solution.py:32
  52.2 15.6 %all-to-all-start.1 = ((f32[32,1,2304]{2,1,0:T(1,128)}), f32[32,1,2304]{2,1,0:T(1,128)S(1)}, u32[]{:S(2)}, u32[]{:S(2)}) async-start(f32[32,1,2304]{2,1,0:T(1,128)} %spread.1), calls=%async_computation.1 | async-start | bytes 589824 | tf_op jit(solution)/shard_map/all_to_all | solution.py:414
  56.5 12.0 %copy-start.6 = (bf16[256,1152]{1,0:T(8,128)(2,1)}, bf16[256,1152]{1,0:T(8,128)(2,1)S(1)}, u32[]{:S(2)}) copy-start(bf16[256,1152]{1,0:T(8,128)(2,1)S(1)} %add_convert_fusion._) | copy-start | bytes 1769476

commit v3 on v2

--- a/solution.py
+++ b/solution.py
@@ -246,55 +246,65 @@
             out_ref[row : row + 1, 128 * tile : 128 * tile + 128] = totals[part][:, lanes]
 
 
+def own_parts(head, group, j, e_ref, dp_ref, near_ref, given):
+    given_m, given_inverse, given_delta = given
+    m_near = near_ref[group, j : j + 1, :]
+    inverse_near = 1.0 / near_ref[group, 4 + j : 5 + j, :]
+    inverse = given_inverse[j : j + 1]
+    there = inverse > 0.0
+    m = jnp.where(there, given_m[j : j + 1], m_near)
+    ratio = jnp.exp2(m_near - m) * jnp.where(there, inverse, inverse_near)
+    delta = jnp.where(there, given_delta[j : j + 1], near_ref[group, 8 + j : 9 + j, :] * inverse_near)
+    p = e_ref[head] * ratio
+    return p, p * (dp_ref[head] - delta)
+
+
+def lanes_of(group):
+    return slice(group * GROUP_LANES, (group + 1) * GROUP_LANES)
+
+
+def table_kernel(groups, e_ref, dp_ref, near_ref, given_ref, cross_ref, table_ref, lines_ref):
+    table_ref[...] = jnp.zeros_like(table_ref)
+    for group in range(groups):
+        given = unpack_rows(given_ref.at[:, lanes_of(group)])
+        for j in range(GROUP_HEADS):
+            _, ds = own_parts(group * GROUP_HEADS + j, group, j, e_ref, dp_ref, near_ref, given)
+            put_lines(lines_ref.at[group : group + 1], j, unskew(ds))
+        a, b = lined(lines_ref, group), lined(cross_ref, group)
+        row = jnp.concatenate([a[:, :BLOCK], a[:, BLOCK:] + b[:, :BLOCK], b[:, BLOCK:]], axis=1)
+        row = flipped(row)
+        for j in range(GROUP_HEADS):
+            for tile in range(ROW_TILES):
+                part, lanes = place(group * GROUP_HEADS + j, tile, table_ref.shape)
+                table_ref[part, :, lanes] = row[j : j + 1, 128 * tile : 128 * tile + 128]
+
+
 def own_kernel(
-    groups, head_width, live_ref, q_ref, g_ref, k_ref, e_ref, dp_ref, near_ref, given_ref, dkc_ref, dvc_ref,
-    cross_ref, dq_ref, dk_ref, dv_ref, table_ref, dq_acc, dk_acc, dv_acc, lines_ref,
+    groups, head_width, live_ref, q_ref, g_ref, k_ref, e_ref, dp_ref, near_ref, given_ref, dqc_ref, dkc_ref, dvc_ref,
+    dq_ref, dk_ref, dv_ref, dq_acc, dk_acc, dv_acc,
 ):
-    step = pl.program_id(0)
     live = live_rows(live_ref[0])
 
     def one_group(group):
-        lanes = slice(group * GROUP_LANES, (group + 1) * GROUP_LANES)
-        given_m, given_inverse, given_delta = unpack_rows(given_ref.at[:, lanes])
+        lanes = lanes_of(group)
+        given = unpack_rows(given_ref.at[:, lanes])
         heads = []
         for j in range(GROUP_HEADS):
             mask = head_mask(j, head_width, HALF)
-            head = group * GROUP_HEADS + j
             qm = window(q_ref, j, group) * mask
             gm = window(g_ref, j, group) * mask * live
             km = window(k_ref, j, group) * mask
-            m_near = near_ref[group, j : j + 1, :]
-            inverse_near = 1.0 / near_ref[group, 4 + j : 5 + j, :]
-            inverse = given_inverse[j : j + 1]
-            there = inverse > 0.0
-            m = jnp.where(there, given_m[j : j + 1], m_near)
-            ratio = jnp.exp2(m_near - m) * jnp.where(there, inverse, inverse_near)
-            delta = jnp.where(there, given_delta[j : j + 1], near_ref[group, 8 + j : 9 + j, :] * inverse_near)
-            p = e_ref[head] * ratio
-            ds = p * (dp_ref[head] - delta)
-            put_lines(lines_ref.at[group : group + 1], j, unskew(ds))
+            p, ds = own_parts(group * GROUP_HEADS + j, group, j, e_ref, dp_ref, near_ref, given)
             heads.append((qm, gm, km, p.astype(HALF), ds.astype(HALF)))
         pair_products(heads, dq_acc, dk_acc, dv_acc)
         scaling = head_width**-0.5
         f32 = jnp.float32
-        dq_ref[...] = dq_acc[...] * scaling
+        dq_ref[...] = (dq_acc[...] * scaling + dqc_ref[:, lanes].astype(f32)).astype(HALF)
         dk_ref[...] = (dk_acc[...] * scaling + dkc_ref[:, lanes].astype(f32)).astype(HALF)
         dv_ref[...] = (dv_acc[...] + dvc_ref[:, lanes].astype(f32)).astype(HALF)
 
     for group in range(groups):
-        pl.when(step == group)(functools.partial(one_group, group))
-
-    @pl.when(step == groups - 1)
-    def _():
-        table_ref[...] = jnp.zeros_like(table_ref)
-        for i in range(groups):
-            a, b = lined(lines_ref, i), lined(cross_ref, i)
-            row = jnp.concatenate([a[:, :BLOCK], a[:, BLOCK:] + b[:, :BLOCK], b[:, BLOCK:]], axis=1)
-            row = flipped(row)
-            for j in range(GROUP_HEADS):
-                for tile in range(ROW_TILES):
-                    part, lanes = place(i * GROUP_HEADS + j, tile, table_ref.shape)
-                    table_ref[part, :, lanes] = row[j : j + 1, 128 * tile : 128 * tile + 128]
+        pl.when(pl.program_id(0) == group)(functools.partial(one_group, group))
 
 
 def params(mebibytes=32):
@@ -381,20 +391,32 @@
     )(live, q, g, k, v, w, *before)
 
 
-def own(head_width, live, q, g, k, e, dp, near, given, dkc, dvc, lines, parts):
+def table_sums(e, dp, near, given, lines, parts):
     groups = near.shape[0]
-    table = shape((parts, 1, -(-groups * GROUP_HEADS * ROW_TILES // parts) * 128))
+    return pl.pallas_call(
+        functools.partial(table_kernel, groups),
+        in_specs=[VMEM] * 5,
+        out_shape=shape((parts, 1, -(-groups * GROUP_HEADS * ROW_TILES // parts) * 128)),
+        scratch_shapes=[pltpu.VMEM(lines.shape, jnp.float32)],
+        compiler_params=params(),
+        cost_estimate=LONG,
+        name="table_sums",
+    )(e, dp, near, given, lines)
+
+
+def own(head_width, live, q, g, k, e, dp, near, given, dqc, dkc, dvc):
+    groups = near.shape[0]
     return pl.pallas_call(
         functools.partial(own_kernel, groups, head_width),
         grid=(groups,),
         in_specs=[SMEM] + [VMEM] * 10,
-        out_specs=[columns()] * 3 + [whole_spec(table.shape)],
-        out_shape=[shape(q.shape), shape(q.shape, HALF), shape(q.shape, HALF), table],
-        scratch_shapes=ACCS + [pltpu.VMEM(lines.shape, jnp.float32)],
+        out_specs=[columns()] * 3,
+        out_shape=[shape(q.shape, HALF)] * 3,
+        scratch_shapes=ACCS,
         compiler_params=params(),
         cost_estimate=LONG,
         name="own",
-    )(live, q, g, k, e, dp, near, given, dkc, dvc, lines)
+    )(live, q, g, k, e, dp, near, given, dqc, dkc, dvc)
 
 
 def spread(terms, count):
@@ -445,8 +467,8 @@
     given = shifted(given, "tm", 1)
     dq_cross = shifted(dq_cross, "tm", 1)
     parts = lax.axis_size("dp")
-    dq_own, dk, dv, table = own(head_width, live_own, q, g, k, e, dp, near, given, dkc, dvc, lines, parts)
-    dq = (dq_own + dq_cross.astype(jnp.float32)).astype(HALF)
+    table = table_sums(e, dp, near, given, lines, parts)
+    dq, dk, dv = own(head_width, live_own, q, g, k, e, dp, near, given, dq_cross, dkc, dvc)
     bias_grad = sum_over_devices(table, "dp", "tm", head_count, dq)
     return tuple(a[None] for a in (dq, dk, dv)) + (bias_grad,)
 

time: 68.9 us -> 68.7 us (level)
  waiting for transfers between devices: 24.4 us -> 14.1 us
  local copies, waits for them, and re-layouts: 0.04 us -> 7.14 us
  Pallas kernels: 19.6 us -> 22.3 us
    all_to_all x1, waiting for transfers between devices: 11.3 us -> 2.06 us  [sum_over_devices(): every = lax.all_to_all(sums, (inner, outer), 0, 0)]
    unnamed x18 -> x30, local copies, waits for them, and re-layouts: 0.04 us -> 7.14 us
    pallas_call x0 -> x1, Pallas kernels: none -> 1.3 us  [table_sums(): pl.pallas_call(functools.partial(table_kernel, groups), in_specs=[VMEM] *...]
    pallas_call x3, Pallas kernels: 4.16 us -> 5.21 us  [cross(): pl.pallas_call(functools.partial(cross_kernel, head_width, group), grid=(...]
    ppermute x6, waiting for transfers between devices: 13.1 us -> 12 us  [shifted(): return lax.ppermute(x, axis, pairs)]
    pallas_call x1, Pallas kernels: 0.66 us -> 1.62 us  [sum_over_devices(): pl.pallas_call(functools.partial(gather_kernel, count), in_specs=[VMEM, A...]
    ppermute x6, starting transfers between devices: 12.2 us -> 13 us  [shifted(): return lax.ppermute(x, axis, pairs)]
    pallas_call x1, Pallas kernels: 0.75 us -> 0.03 us  [spread(): pl.pallas_call(spread_kernel, out_shape=shape((count,) + terms.shape[1:])...]
  transfers between devices with their start and end apart: 7 -> 7, of which waited for: 4 -> 4; matrix products, arithmetic and copies ran while one was open for 0% -> 0% of each run, Pallas kernels for 26% -> 28%
where the time goes in v3:
time: 68.7 us; the launch traced here: 68 us
  Pallas kernels  22.3 us (32%)
  starting transfers between devices  16.5 us (24%)
  waiting for transfers between devices  14.1 us (21%)
  local copies, waits for them, and re-layouts  7.14 us (10%)
  blocking collectives  6.53 us (10%)
  between operations  1.47 us (2%)
    ppermute x6, starting transfers between devices, shifted(): return lax.ppermute(x, axis, pairs)  13 us
    ppermute x6, waiting for transfers between devices, shifted(): return lax.ppermute(x, axis, pairs)  12 us
    pallas_call x3, Pallas kernels, own_stats(): pl.pallas_call(functools.partial(own_stats_kernel, head_width, group), gr...  10.1 us
    unnamed x30, local copies, waits for them, and re-layouts  7.14 us
    all_to_all x1, blocking collectives, sum_over_devices(): terms = lax.all_to_all(parts, inner, 0, 0)  6.53 us
    pallas_call x3, Pallas kernels, cross(): pl.pallas_call(functools.partial(cross_kernel, head_width, group), grid=(...  5.21 us
    pallas_call x1, Pallas kernels, own(): pl.pallas_call(functools.partial(own_kernel, groups, head_width), grid=(g...  3.99 us
    all_to_all x1, starting transfers between devices, sum_over_devices(): every = lax.all_to_all(sums, (inner, outer), 0, 0)  3.51 us
  transfers between devices with their start and end apart: 7, of which 4 were waited for; matrix products, arithmetic and copies ran while one was open for 0% of the time, Pallas kernels for 28%

profile of v3, /device:TPU:0, one launch (start us, length us, event | category | flops | bytes accessed | tf_op | source)
XLA Modules:
  0.0 68.0 jit_solution(11861340369259708783)
XLA Ops:
  0.6 1.3 %collective-permute-start = (bf16[256,1152]{1,0:T(8,128)(2,1)}, bf16[256,1152]{1,0:T(8,128)(2,1)S(1)}, u32[]{:S(2)}, u32[]{:S(2)}) collective-permute-start(bf16[256,1152]{1,0:T(8,128)(2,1)} %bitcast.21), channel_id=1, source_target_pairs={{1,0},{2,1},{3,2},{4,3},{5,4},{6,5},{7,6},{9,8},{10,9},{11,10},{12... | collective-permute-start | bytes 1769480 | tf_op jit(solution)/shard_map/ppermute | solution.py:32
  2.6 3.5 %own_stats_0.1 = (f32[3,16,256]{2,1,0:T(8,128)}, f32[12,256,256]{2,1,0:T(8,128)}, f32[12,256,256]{2,1,0:T(8,128)}, bf16[272,384]{1,0:T(8,128)(2,1)}, f32[12,768]{1,0:T(8,128)}) custom-call(s32[1]{0:T(128)S(6)} %sub.10.live_ref, bf16[256,1152]{1,0:T(8,128)(2,1)} %bitcast.22, bf16[256,1152]{1,0:T(8,128)(2,1)} %bitcast.26, bf16[256,1152]{1,0:T(8,128)(2,1)} %bitcast.14, ...), custom_call_target="tpu_custom_call" | custom-call | flops 1024 | bytes 1024 | tf_op jit(solution)/shard_map/own_stats_0/pallas_call | solution.py:364
  6.1 1.3 %collective-permute-start.3 = (bf16[272,384]{1,0:T(8,128)(2,1)}, bf16[272,384]{1,0:T(8,128)(2,1)S(1)}, u32[]{:S(2)}, u32[]{:S(2)}) collective-permute-start(bf16[272,384]{1,0:T(8,128)(2,1)} %get-tuple-element.47), channel_id=1, source_target_pairs={{1,0},{2,1},{3,2},{4,3},{5,4},{6,5},{7,6},{9,8},{10,9},{11,10},{12... | collective-permute-start | bytes 626696 | tf_op jit(solution)/shard_map/ppermute | solution.py:32
  7.3 3.3 %own_stats_1.1 = (f32[3,16,256]{2,1,0:T(8,128)}, f32[12,256,256]{2,1,0:T(8,128)}, f32[12,256,256]{2,1,0:T(8,128)}, bf16[272,384]{1,0:T(8,128)(2,1)}) custom-call(s32[1]{0:T(128)S(6)} %sub.10.live_ref, bf16[256,1152]{1,0:T(8,128)(2,1)} %bitcast.23, bf16[256,1152]{1,0:T(8,128)(2,1)} %bitcast.27, ...), custom_call_target="tpu_custom_call", output_to_operand_aliasing={{0}: (6, {}), {1}: (7, {}), {2}: (8, {})} | custom-call | flops 1024 | bytes 1024 | tf_op jit(solution)/shard_map/own_stats_1/pallas_call | solution.py:364
  10.6 1.3 %collective-permute-start.2 = (bf16[272,384]{1,0:T(8,128)(2,1)}, bf16[272,384]{1,0:T(8,128)(2,1)}, u32[]{:S(2)}, u32[]{:S(2)}) collective-permute-start(bf16[272,384]{1,0:T(8,128)(2,1)} %get-tuple-element.46), channel_id=1, source_target_pairs={{1,0},{2,1},{3,2},{4,3},{5,4},{6,5},{7,6},{9,8},{10,9},{11,10},{12... | collective-permute-start | bytes 626696 | tf_op jit(solution)/shard_map/ppermute | solution.py:32
  11.9 0.0 copy-start
  11.9 0.0 copy-start.1
  11.9 3.4 %own_stats_2.1 = (f32[3,16,256]{2,1,0:T(8,128)}, f32[12,256,256]{2,1,0:T(8,128)}, f32[12,256,256]{2,1,0:T(8,128)}, bf16[272,384]{1,0:T(8,128)(2,1)}) custom-call(s32[1]{0:T(128)S(6)} %sub.10.live_ref, bf16[256,1152]{1,0:T(8,128)(2,1)} %bitcast.24, bf16[256,1152]{1,0:T(8,128)(2,1)} %bitcast.28, ...), custom_call_target="tpu_custom_call", output_to_operand_aliasing={{0}: (6, {}), {1}: (7, {}), {2}: (8, {})} | custom-call | flops 1024 | bytes 1024 | tf_op jit(solution)/shard_map/own_stats_2/pallas_call | solution.py:364
  15.3 1.3 %collective-permute-start.1 = (bf16[272,384]{1,0:T(8,128)(2,1)}, bf16[272,384]{1,0:T(8,128)(2,1)S(1)}, u32[]{:S(2)}, u32[]{:S(2)}) collective-permute-start(bf16[272,384]{1,0:T(8,128)(2,1)} %get-tuple-element.45), channel_id=1, source_target_pairs={{1,0},{2,1},{3,2},{4,3},{5,4},{6,5},{7,6},{9,8},{10,9},{11,10},{12... | collective-permute-start | bytes 626696 | tf_op jit(solution)/shard_map/ppermute | solution.py:32
  16.6 7.7 %collective-permute-done.3.g_ref = bf16[272,384]{1,0:T(8,128)(2,1)S(1)} collective-permute-done((bf16[272,384]{1,0:T(8,128)(2,1)}, bf16[272,384]{1,0:T(8,128)(2,1)S(1)}, u32[]{:S(2)}, u32[]{:S(2)}) %collective-permute-start.3) | collective-permute-done | bytes 208928 | tf_op jit(solution)/shard_map/ppermute | solution.py:32
  24.4 1.4 %cross_0.1 = (bf16[16,1152]{1,0:T(8,128)(2,1)S(1)}, bf16[256,1152]{1,0:T(8,128)(2,1)S(1)}, bf16[256,1152]{1,0:T(8,128)(2,1)S(1)}, bf16[256,1152]{1,0:T(8,128)(2,1)S(1)}, f32[3,4,32,128]{3,2,1,0:T(8,128)S(1)}) custom-call(s32[1]{0:T(128)S(6)} %sub.11.live_ref, bf16[256,1152]{1,0:T(8,128)(2,1)S(1)} %collective-permute-done.q_ref, ...), custom_call_target="tpu_custom_call" | custom-call | flops 1024 | bytes 1024 | tf_op jit(solution)/shard_map/cross_0/pallas_call | solution.py:380
  25.8 3.2 %collective-permute-done.2.g_ref = bf16[272,384]{1,0:T(8,128)(2,1)} collective-permute-done((bf16[272,384]{1,0:T(8,128)(2,1)}, bf16[272,384]{1,0:T(8,128)(2,1)}, u32[]{:S(2)}, u32[]{:S(2)}) %collective-permute-start.2) | collective-permute-done | bytes 208928 | tf_op jit(solution)/shard_map/ppermute | solution.py:32
  28.9 2.5 %cross_1.1 = (bf16[16,1152]{1,0:T(8,128)(2,1)S(1)}, bf16[256,1152]{1,0:T(8,128)(2,1)S(1)}, bf16[256,1152]{1,0:T(8,128)(2,1)S(1)}, bf16[256,1152]{1,0:T(8,128)(2,1)S(1)}, f32[3,4,32,128]{3,2,1,0:T(8,128)S(1)}) custom-call(s32[1]{0:T(128)S(6)} %sub.11.live_ref, ...), custom_call_target="tpu_custom_call", output_to_operand_aliasing={{0}: (6, {}), {1}: (7, {}), {2}: (8, {}), {3}: (9, {}), {4}... | custom-call | flops 1024 | bytes 1024 | tf_op jit(solution)/shard_map/cross_1/pallas_call | solution.py:380
  31.4 1.1 %collective-permute-done.1.g_ref = bf16[272,384]{1,0:T(8,128)(2,1)S(1)} collective-permute-done((bf16[272,384]{1,0:T(8,128)(2,1)}, bf16[272,384]{1,0:T(8,128)(2,1)S(1)}, u32[]{:S(2)}, u32[]{:S(2)}) %collective-permute-start.1) | collective-permute-done | bytes 208928 | tf_op jit(solution)/shard_map/ppermute | solution.py:32
  32.5 1.4 %cross_2.1 = (bf16[16,1152]{1,0:T(8,128)(2,1)S(1)}, bf16[256,1152]{1,0:T(8,128)(2,1)S(1)}, bf16[256,1152]{1,0:T(8,128)(2,1)S(1)}, bf16[256,1152]{1,0:T(8,128)(2,1)S(1)}, f32[3,4,32,128]{3,2,1,0:T(8,128)S(1)}) custom-call(s32[1]{0:T(128)S(6)} %sub.11.live_ref, ...), custom_call_target="tpu_custom_call", output_to_operand_aliasing={{0}: (6, {}), {1}: (7, {}), {2}: (8, {}), {3}: (9, {}), {4}... | custom-call | flops 1024 | bytes 1024 | tf_op jit(solution)/shard_map/cross_2/pallas_call | solution.py:380
  33.9 4.5 %collective-permute-start.4 = (bf16[16,1152]{1,0:T(8,128)(2,1)S(1)}, bf16[16,1152]{1,0:T(8,128)(2,1)S(1)}, u32[]{:S(2)}, u32[]{:S(2)}) collective-permute-start(bf16[16,1152]{1,0:T(8,128)(2,1)S(1)} %get-tuple-element.58), channel_id=1, source_target_pairs={{0,1},{1,2},{2,3},{3,4},{4,5},{5,6},{6,7},{8,9},{9,10},{10,11},{11... | collective-permute-start | bytes 110600 | tf_op jit(solution)/shard_map/ppermute | solution.py:32
  38.4 3.4 %collective-permute-start.5 = (bf16[256,1152]{1,0:T(8,128)(2,1)S(1)}, bf16[256,1152]{1,0:T(8,128)(2,1)}, u32[]{:S(2)}, u32[]{:S(2)}) collective-permute-start(bf16[256,1152]{1,0:T(8,128)(2,1)S(1)} %get-tuple-element.59), channel_id=1, source_target_pairs={{0,1},{1,2},{2,3},{3,4},{4,5},{5,6},{6,7},{8,9},{9,10},{10,11},{11... | collective-permute-start | bytes 1769480 | tf_op jit(solution)/shard_map/ppermute | solution.py:32
  41.8 0.0 copy-start.6
  41.8 0.0 copy-start.7
  41.8 1.3 %table_sums.1 = f32[4,1,2304]{2,1,0:T(1,128)S(1)} custom-call(f32[12,256,256]{2,1,0:T(8,128)S(1)} %copy-done.2, f32[12,256,256]{2,1,0:T(8,128)S(1)} %copy-done.4, f32[3,16,256]{2,1,0:T(8,128)S(1)} %copy-done.11, bf16[16,1152]{1,0:T(8,128)(2,1)S(1)} %collective-permute-done.4.given_ref, f32[3,4,32,128]{3,2,1,0:T(8,128)S(1)} %get-tuple-element.65.cross_ref), custom_call_target="tpu_custom_call" | custom-call | flops 99999997952 | bytes 1024 | tf_op jit(solution)/shard_map/table_sums/pallas_call | solution.py:396
  43.1 6.5 %all_to_all.10.terms_ref = f32[4,1,2304]{2,1,0:T(1,128)S(1)} all-to-all(f32[4,1,2304]{2,1,0:T(1,128)S(1)} %table_sums.1), channel_id=1, replica_groups=mesh['dp'=4,'tm'=8] {'dp'}, dimensions={0} | all-to-all | bytes 73728 | tf_op jit(solution)/shard_map/all_to_all | solution.py:434
  49.7 0.7 %copy-done.9 = f32[32,1,2304]{2,1,0:T(1,128)} copy-done((f32[32,1,2304]{2,1,0:T(1,128)}, f32[32,1,2304]{2,1,0:T(1,128)S(1)}, u32[]{:S(2)}) %copy-start.9) | copy-done | bytes 294936
  50.4 3.5 %all-to-all-start.1 = ((f32[32,1,2304]{2,1,0:T(1,128)}), f32[32,1,2304]{2,1,0:T(1,128)}, u32[]{:S(2)}, u32[]{:S(2)}) async-start(f32[32,1,2304]{2,1,0:T(1,128)} %copy-done.9), calls=%async_computation.1 | async-start | bytes 589824 | tf_op jit(solution)/shard_map/all_to_all | solution.py:436
  53.9 0.0 collective-permute-done.5.dqc_ref
  53.9 1.9 %copy-done.3 = f32[12,256,256]{2,1,0:T(8,128)S(1)} copy-done((f32[12,256,256]{2,1,0:T(8,128)S(1)}, f32[12,256,256]{2,1,0:T(8,128)}, u32[]{:S(2)}) %copy-start.3) | copy-done | bytes 3145752
  55.8 1.9 %copy-done.5 = f32[12,256,256]{2,1,0:T(8,128)S(1)} copy-done((f32[12,256,256]{2,1,0:T(8,128)S(1)}, f32[12,256,256]{2,1,0:T(8,128)}, u32[]{:S(2)}) %copy-start.5) | copy-done | bytes 3145752
  57.7 0.8 %copy-done.12 = f32[3,16,256]{2,1,0:T(8,128)S(1)} copy-done((f32[3,16,256]{2,1,0:T(8,128)S(1)}, f32[3,16,256]{2,1,0:T(8,128)}, u32[]{:S(2)}) %copy-start.12) | copy-done | bytes 49176
  58.5 0.8 %copy-done.14 = bf16[16,1152]{1,0:T(8,128)(2,1)S(1)} copy-done((bf16[16,1152]{1,0:T(8,128)(2,1)S(1)}, bf16[16,1152]{1,0:T(8,128)(2,1)}, u32[]{:S(2)}) %copy-start.14) | copy-done | bytes 36888
  59.3 4.0 %own.1 = (bf16[256,1152]{1,0:T(8,128)(2,1)}, bf16[256,1152]{1,0:T(8,128)(2,1)}, bf16[256,1152]{1,0:T(8,128)(2,1)}) custom-call(s32[1]{0:T(128)S(6)} %sub.10.live_ref, bf16[256,1152]{1,0:T(8,128)(2,1)S(1)} %bitcast.25, bf16[256,1152]{1,0:T(8,128)(2,1)S(1)} %bitcast.29, bf16[256,1152]{1,0:T(8,128)(2,1)S(1)} %bitcast.20, f32[12,256,256]{2,1,0:T(8,128)S(1)} %copy-done.3, ...), custom_call_target="tpu_custom_call" | custom-call | flops 99999997952 | bytes 1024 | tf_op jit(solution)/shard_map/own/pallas_call | solution.py:409
  63.3 2.1 %all-to-all-done.1.every_ref = f32[32,1,2304]{2,1,0:T(1,128)} async-done(((f32[32,1,2304]{2,1,0:T(1,128)}), f32[32,1,2304]{2,1,0:T(1,128)}, u32[]{:S(2)}, u32[]{:S(2)}) %all-to-all-start.1) | async-done | bytes 294944 | tf_op jit(solution)/shard_map/all_to_all | solution.py:436
  65.3 1.1 %copy-done.10 = bf16[256,1152]{1,0:T(8,128)(2,1)S(1)} copy-done((bf16[256,1152]{1,0:T(8,128)(2,1)S(1)}, bf16[256,1152]{1,0:T(8,128)(2,1)}, u32[]{:S(2)}) %copy-start.10) | copy-done | bytes 589848
  66.4 1.6 %gather.1 = f32[12,768]{1,0:T(8,128)} custom-call(f32[32,1,2304]{2,1,0:T(1,128)} %all-to-all-done.1.every_ref, bf16[256,1152]{1,0:T(8,128)(2,1)S(1)} %copy-done.10), custom_call_target="tpu_custom_call" | custom-call | flops 1024 | bytes 1024 | tf_op jit(solution)/shard_map/gather/pallas_call | solution.py:437
  (23 shorter events, 0.1 us)
Async XLA Ops:
  0.6 23.7 %collective-permute-start = (bf16[256,1152]{1,0:T(8,128)(2,1)}, bf16[256,1152]{1,0:T(8,128)(2,1)S(1)}, u32[]{:S(2)}, u32[]{:S(2)}) collective-permute-start(bf16[256,1152]{1,0:T(8,128)(2,1)} %bitcast.21), channel_id=1, source_target_pairs={{1,0},{2,1},{3,2},{4,3},{5,4},{6,5},{7,6},{9,8},{10,9},{11,10},{12... | collective-permute-start | bytes 1769480 | tf_op jit(solution)/shard_map/ppermute | solution.py:32
  6.1 18.3 %collective-permute-start.3 = (bf16[272,384]{1,0:T(8,128)(2,1)}, bf16[272,384]{1,0:T(8,128)(2,1)S(1)}, u32[]{:S(2)}, u32[]{:S(2)}) collective-permute-start(bf16[272,384]{1,0:T(8,128)(2,1)} %get-tuple-element.47), channel_id=1, source_target_pairs={{1,0},{2,1},{3,2},{4,3},{5,4},{6,5},{7,6},{9,8},{10,9},{11,10},{12... | collective-permute-start | bytes 626696 | tf_op jit(solution)/shard_map/ppermute | solution.py:32
  10.6 18.3 %collective-permute-start.2 = (bf16[272,384]{1,0:T(8,128)(2,1)}, bf16[272,384]{1,0:T(8,128)(2,1)}, u32[]{:S(2)}, u32[]{:S(2)}) collective-permute-start(bf16[272,384]{1,0:T(8,128)(2,1)} %get-tuple-element.46), channel_id=1, source_target_pairs={{1,0},{2,1},{3,2},{4,3},{5,4},{6,5},{7,6},{9,8},{10,9},{11,10},{12... | collective-permute-start | bytes 626696 | tf_op jit(solution)/shard_map/ppermute | solution.py:32
  11.9 12.4 %copy-start = (bf16[1,256,1152]{2,1,0:T(8,128)(2,1)S(1)}, bf16[1,256,1152]{2,1,0:T(8,128)(2,1)}, u32[]{:S(2)}) copy-start(bf16[1,256,1152]{2,1,0:T(8,128)(2,1)} %param.8) | copy-start | bytes 1769476
  11.9 12.4 %copy-start.1 = (bf16[1,256,1152]{2,1,0:T(8,128)(2,1)S(1)}, bf16[1,256,1152]{2,1,0:T(8,128)(2,1)}, u32[]{:S(2)}) copy-start(bf16[1,256,1152]{2,1,0:T(8,128)(2,1)} %param.7) | copy-start | bytes 1769476
  11.9 12.4 %copy-start.8 = (f32[12,768]{1,0:T(8,128)S(1)}, f32[12,768]{1,0:T(8,128)}, u32[]{:S(2)}) copy-start(f32[12,768]{1,0:T(8,128)} %get-tuple-element.35.bias_ref.w_ref) | copy-start | bytes 110596
  15.3 17.2 %collective-permute-start.1 = (bf16[272,384]{1,0:T(8,128)(2,1)}, bf16[272,384]{1,0:T(8,128)(2,1)S(1)}, u32[]{:S(2)}, u32[]{:S(2)}) collective-permute-start(bf16[272,384]{1,0:T(8,128)(2,1)} %get-tuple-element.45), channel_id=1, source_target_pairs={{1,0},{2,1},{3,2},{4,3},{5,4},{6,5},{7,6},{9,8},{10,9},{11,10},{12... | collective-permute-start | bytes 626696 | tf_op jit(solution)/shard_map/ppermute | solution.py:32
  28.9 12.8 %copy-start.2 = (f32[12,256,256]{2,1,0:T(8,128)S(1)}, f32[12,256,256]{2,1,0:T(8,128)}, u32[]{:S(2)}) copy-start(f32[12,256,256]{2,1,0:T(8,128)} %get-tuple-element.42.e_ref) | copy-start | bytes 9437188
  28.9 12.8 %copy-start.4 = (f32[12,256,256]{2,1,0:T(8,128)S(1)}, f32[12,256,256]{2,1,0:T(8,128)}, u32[]{:S(2)}) copy-start(f32[12,256,256]{2,1,0:T(8,128)} %get-tuple-element.43.dp_ref) | copy-start | bytes 9437188
  28.9 12.9 %copy-start.11 = (f32[3,16,256]{2,1,0:T(8,128)S(1)}, f32[3,16,256]{2,1,0:T(8,128)}, u32[]{:S(2)}) copy-start(f32[3,16,256]{2,1,0:T(8,128)} %get-tuple-element.44.near_ref) | copy-start | bytes 147460
  33.9 7.9 %collective-permute-start.4 = (bf16[16,1152]{1,0:T(8,128)(2,1)S(1)}, bf16[16,1152]{1,0:T(8,128)(2,1)S(1)}, u32[]{:S(2)}, u32[]{:S(2)}) collective-permute-start(bf16[16,1152]{1,0:T(8,128)(2,1)S(1)} %get-tuple-element.58), channel_id=1, source_target_pairs={{0,1},{1,2},{2,3},{3,4},{4,5},{5,6},{6,7},{8,9},{9,10},{10,11},{11... | collective-permute-start | bytes 110600 | tf_op jit(solution)/shard_map/ppermute | solution.py:32
  38.4 15.5 %collective-permute-start.5 = (bf16[256,1152]{1,0:T(8,128)(2,1)S(1)}, bf16[256,1152]{1,0:T(8,128)(2,1)}, u32[]{:S(2)}, u32[]{:S(2)}) collective-permute-start(bf16[256,1152]{1,0:T(8,128)(2,1)S(1)} %get-tuple-element.59), channel_id=1, source_target_pairs={{0,1},{1,2},{2,3},{3,4},{4,5},{5,6},{6,7},{8,9},{9,10},{10,11},{11... | collective-permute-start | bytes 1769480 | tf_op jit(solution)/shard_map/ppermute | solution.py:32
  41.8 1.3 %copy-start.13 = (bf16[16,1152]{1,0:T(8,128)(2,1)}, bf16[16,1152]{1,0:T(8,128)(2,1)S(1)}, u32[]{:S(2)}) copy-start(bf16[16,1152]{1,0:T(8,128)(2,1)S(1)} %collective-permute-done.4.given_ref) | copy-start | bytes 110596
  41.8 12.1 %copy-start.6 = (bf16[1,256,1152]{2,1,0:T(8,128)(2,1)S(1)}, bf16[1,256,1152]{2,1,0:T(8,128)(2,1)}, u32[]{:S(2)}) copy-start(bf16[1,256,1152]{2,1,0:T(8,128)(2,1)} %param.6) | copy-start | bytes 1769476
  41.8 12.1 %copy-start.7 = (bf16[1,256,1152]{2,1,0:T(8,128)(2,1)S(1)}, bf16[1,256,1152]{2,1,0:T(8,128)(2,1)}, u32[]{:S(2)}) copy-start(bf16[1,256,1152]{2,1,0:T(8,128)(2,1)} %param.9) | copy-start | bytes 1769476
  49.7 0.7 %copy-start.9 = (f32[32,1,2304]{2,1,0:T(1,128)}, f32[32,1,2304]{2,1,0:T(1,128)S(1)}, u32[]{:S(2)}) copy-start(f32[32,1,2304]{2,1,0:T(1,128)S(1)} %spread.1) | copy-start | bytes 884740
  50.4 14.9 %all-to-all-start.1 = ((f32[32,1,2304]{2,1,0:T(1,128)}), f32[32,1,2304]{2,1,0:T(1,128)}, u32[]{:S(2)}, u32[]{:S(2)}) async-start(f32[32,1,2304]{2,1,0:T(1,128)} %copy-done.9), calls=%async_computation.1 | async-start | bytes 589824 | tf_op jit(solution)/shard_map/all_to_all | solution.py:436
  53.9 1.9 %copy-start.3 = (f32[12,256,256]{2,1,0:T(8,128)S(1)}, f32[12,256,256]{2,1,0:T(8,128)}, u32[]{:S(2)}) copy-start(f32[12,256,256]{2,1,0:T(8,128)} %get-tuple-element.42.e_ref) | copy-start | bytes 9437188
  55.8 1.9 %copy-start.5 = (f32[12,256,256]{2,1,0:T(8,128)S(1)}, f32[12,256,256]{2,1,0:T(8,128)}, u32[]{:S(2)}) copy-start(f32[12,256,256]{2,1,0:T(8,128)} %get-tuple-element.43.dp_ref) | copy-start | bytes 9437188
  57.7 0.8 %copy-start.12 = (f32[3,16,256]{2,1,0:T(8,128)S(1)}, f32[3,16,256]{2,1,0:T(8,128)}, u32[]{:S(2)}) copy-start(f32[3,16,256]{2,1,0:T(8,128)} %get-tuple-element.44.near_ref) | copy-start | bytes 147460
  58.5 0.8 %copy-start.14 = (bf16[16,1152]{1,0:T(8,128)(2,1)S(1)}, bf16[16,1152]{1,0:T(8,128)(2,1)}, u32[]{:S(2)}) copy-start(bf16[16,1152]{1,0:T(8,128)(2,1)} %copy-done.13) | copy-start | bytes 110596
  65.3 1.1 %copy-start.10 = (bf16[256,1152]{1,0:T(8,128)(2,1)S(1)}, bf16[256,1152]{1,0:T(8,128)(2,1)}, u32[]{:S(2)}) copy-start(bf16[256,1152]{1,0:T(8,128)(2,1)} %get-tuple-element.62._) | copy-start | bytes 1769476

commit v4 on v3

--- a/solution.py
+++ b/solution.py
@@ -422,7 +422,8 @@
 def spread(terms, count):
     return pl.pallas_call(
         spread_kernel,
-        out_shape=shape((count,) + terms.shape[1:]),
+        out_shape=pltpu.HBM((count,) + terms.shape[1:], jnp.float32),
+        out_specs=VMEM,
         compiler_params=params(),
         cost_estimate=COST,
         name="spread",
@@ -441,7 +442,7 @@
         compiler_params=params(),
         cost_estimate=COST,
         name="gather",
-    )(every, after)
+    )(every, pltpu.with_memory_space_constraint(after, pltpu.HBM))
 
 
 def per_device(queries, keys, values, out_grad, lengths, rel_bias):
@@ -468,7 +469,8 @@
     dq_cross = shifted(dq_cross, "tm", 1)
     parts = lax.axis_size("dp")
     table = table_sums(e, dp, near, given, lines, parts)
-    dq, dk, dv = own(head_width, live_own, q, g, k, e, dp, near, given, dq_cross, dkc, dvc)
+    late = (pltpu.with_memory_space_constraint(a, pltpu.HBM) for a in (e, dp, near, given))
+    dq, dk, dv = own(head_width, live_own, q, g, k, *late, dq_cross, dkc, dvc)
     bias_grad = sum_over_devices(table, "dp", "tm", head_count, dq)
     return tuple(a[None] for a in (dq, dk, dv)) + (bias_grad,)
 

time: 68.7 us -> 68 us (0.990)
  local copies, waits for them, and re-layouts: 7.14 us -> 0.66 us
  waiting for transfers between devices: 14.1 us -> 17.5 us
  Pallas kernels: 22.3 us -> 24.9 us
    unnamed x30 -> x18, local copies, waits for them, and re-layouts: 7.14 us -> 0.66 us
    all_to_all x1, waiting for transfers between devices: 2.06 us -> 5.47 us  [sum_over_devices(): every = lax.all_to_all(sums, (inner, outer), 0, 0)]
    pallas_call x1, Pallas kernels: 3.99 us -> 5.92 us  [own(): pl.pallas_call(functools.partial(own_kernel, groups, head_width), grid=(g...]
    pallas_call x1, Pallas kernels: 0.03 us -> 0.74 us  [spread(): pl.pallas_call(spread_kernel, out_shape=pltpu.HBM((count,) + terms.shape[...]
  transfers between devices with their start and end apart: 7 -> 7, of which waited for: 4 -> 4; matrix products, arithmetic and copies ran while one was open for 0% -> 0% of each run, Pallas kernels for 28% -> 32%
where the time goes in v4:
time: 68 us; the launch traced here: 67.6 us
  Pallas kernels  24.9 us (37%)
  waiting for transfers between devices  17.5 us (26%)
  starting transfers between devices  16.6 us (24%)
  blocking collectives  6.51 us (10%)
  between operations  1.44 us (2%)
    ppermute x6, starting transfers between devices, shifted(): return lax.ppermute(x, axis, pairs)  13 us
    ppermute x6, waiting for transfers between devices, shifted(): return lax.ppermute(x, axis, pairs)  12 us
    pallas_call x3, Pallas kernels, own_stats(): pl.pallas_call(functools.partial(own_stats_kernel, head_width, group), gr...  10.1 us
    all_to_all x1, blocking collectives, sum_over_devices(): terms = lax.all_to_all(parts, inner, 0, 0)  6.51 us
    pallas_call x1, Pallas kernels, own(): pl.pallas_call(functools.partial(own_kernel, groups, head_width), grid=(g...  5.92 us
    all_to_all x1, waiting for transfers between devices, sum_over_devices(): every = lax.all_to_all(sums, (inner, outer), 0, 0)  5.47 us
    pallas_call x3, Pallas kernels, cross(): pl.pallas_call(functools.partial(cross_kernel, head_width, group), grid=(...  5.22 us
    all_to_all x1, starting transfers between devices, sum_over_devices(): every = lax.all_to_all(sums, (inner, outer), 0, 0)  3.52 us
  transfers between devices with their start and end apart: 7, of which 4 were waited for; matrix products, arithmetic and copies ran while one was open for 0% of the time, Pallas kernels for 32%

profile of v4, /device:TPU:0, one launch (start us, length us, event | category | flops | bytes accessed | tf_op | source)
XLA Modules:
  0.0 67.6 jit_solution(10453270647886553747)
XLA Ops:
  0.6 1.3 %collective-permute-start = (bf16[256,1152]{1,0:T(8,128)(2,1)}, bf16[256,1152]{1,0:T(8,128)(2,1)S(1)}, u32[]{:S(2)}, u32[]{:S(2)}) collective-permute-start(bf16[256,1152]{1,0:T(8,128)(2,1)} %bitcast.21), channel_id=1, source_target_pairs={{1,0},{2,1},{3,2},{4,3},{5,4},{6,5},{7,6},{9,8},{10,9},{11,10},{12... | collective-permute-start | bytes 1769480 | tf_op jit(solution)/shard_map/ppermute | solution.py:32
  2.6 3.5 %own_stats_0.1 = (f32[3,16,256]{2,1,0:T(8,128)}, f32[12,256,256]{2,1,0:T(8,128)}, f32[12,256,256]{2,1,0:T(8,128)}, bf16[272,384]{1,0:T(8,128)(2,1)}, f32[12,768]{1,0:T(8,128)}) custom-call(s32[1]{0:T(128)S(6)} %sub.10.live_ref, bf16[256,1152]{1,0:T(8,128)(2,1)} %bitcast.22, bf16[256,1152]{1,0:T(8,128)(2,1)} %bitcast.26, bf16[256,1152]{1,0:T(8,128)(2,1)} %bitcast.14, ...), custom_call_target="tpu_custom_call" | custom-call | flops 1024 | bytes 1024 | tf_op jit(solution)/shard_map/own_stats_0/pallas_call | solution.py:364
  6.1 1.3 %collective-permute-start.3 = (bf16[272,384]{1,0:T(8,128)(2,1)}, bf16[272,384]{1,0:T(8,128)(2,1)S(1)}, u32[]{:S(2)}, u32[]{:S(2)}) collective-permute-start(bf16[272,384]{1,0:T(8,128)(2,1)} %get-tuple-element.47), channel_id=1, source_target_pairs={{1,0},{2,1},{3,2},{4,3},{5,4},{6,5},{7,6},{9,8},{10,9},{11,10},{12... | collective-permute-start | bytes 626696 | tf_op jit(solution)/shard_map/ppermute | solution.py:32
  7.3 3.3 %own_stats_1.1 = (f32[3,16,256]{2,1,0:T(8,128)}, f32[12,256,256]{2,1,0:T(8,128)}, f32[12,256,256]{2,1,0:T(8,128)}, bf16[272,384]{1,0:T(8,128)(2,1)}) custom-call(s32[1]{0:T(128)S(6)} %sub.10.live_ref, bf16[256,1152]{1,0:T(8,128)(2,1)} %bitcast.23, bf16[256,1152]{1,0:T(8,128)(2,1)} %bitcast.27, ...), custom_call_target="tpu_custom_call", output_to_operand_aliasing={{0}: (6, {}), {1}: (7, {}), {2}: (8, {})} | custom-call | flops 1024 | bytes 1024 | tf_op jit(solution)/shard_map/own_stats_1/pallas_call | solution.py:364
  10.6 1.3 %collective-permute-start.2 = (bf16[272,384]{1,0:T(8,128)(2,1)}, bf16[272,384]{1,0:T(8,128)(2,1)}, u32[]{:S(2)}, u32[]{:S(2)}) collective-permute-start(bf16[272,384]{1,0:T(8,128)(2,1)} %get-tuple-element.46), channel_id=1, source_target_pairs={{1,0},{2,1},{3,2},{4,3},{5,4},{6,5},{7,6},{9,8},{10,9},{11,10},{12... | collective-permute-start | bytes 626696 | tf_op jit(solution)/shard_map/ppermute | solution.py:32
  11.9 0.0 copy-start
  11.9 0.0 copy-start.1
  11.9 3.4 %own_stats_2.1 = (f32[3,16,256]{2,1,0:T(8,128)}, f32[12,256,256]{2,1,0:T(8,128)}, f32[12,256,256]{2,1,0:T(8,128)}, bf16[272,384]{1,0:T(8,128)(2,1)}) custom-call(s32[1]{0:T(128)S(6)} %sub.10.live_ref, bf16[256,1152]{1,0:T(8,128)(2,1)} %bitcast.24, bf16[256,1152]{1,0:T(8,128)(2,1)} %bitcast.28, ...), custom_call_target="tpu_custom_call", output_to_operand_aliasing={{0}: (6, {}), {1}: (7, {}), {2}: (8, {})} | custom-call | flops 1024 | bytes 1024 | tf_op jit(solution)/shard_map/own_stats_2/pallas_call | solution.py:364
  15.3 1.3 %collective-permute-start.1 = (bf16[272,384]{1,0:T(8,128)(2,1)}, bf16[272,384]{1,0:T(8,128)(2,1)S(1)}, u32[]{:S(2)}, u32[]{:S(2)}) collective-permute-start(bf16[272,384]{1,0:T(8,128)(2,1)} %get-tuple-element.45), channel_id=1, source_target_pairs={{1,0},{2,1},{3,2},{4,3},{5,4},{6,5},{7,6},{9,8},{10,9},{11,10},{12... | collective-permute-start | bytes 626696 | tf_op jit(solution)/shard_map/ppermute | solution.py:32
  16.6 7.7 %collective-permute-done.3.g_ref = bf16[272,384]{1,0:T(8,128)(2,1)S(1)} collective-permute-done((bf16[272,384]{1,0:T(8,128)(2,1)}, bf16[272,384]{1,0:T(8,128)(2,1)S(1)}, u32[]{:S(2)}, u32[]{:S(2)}) %collective-permute-start.3) | collective-permute-done | bytes 208928 | tf_op jit(solution)/shard_map/ppermute | solution.py:32
  24.3 0.0 collective-permute-done.q_ref
  24.3 0.0 copy-done
  24.4 1.4 %cross_0.1 = (bf16[16,1152]{1,0:T(8,128)(2,1)S(1)}, bf16[256,1152]{1,0:T(8,128)(2,1)S(1)}, bf16[256,1152]{1,0:T(8,128)(2,1)S(1)}, bf16[256,1152]{1,0:T(8,128)(2,1)S(1)}, f32[3,4,32,128]{3,2,1,0:T(8,128)S(1)}) custom-call(s32[1]{0:T(128)S(6)} %sub.11.live_ref, bf16[256,1152]{1,0:T(8,128)(2,1)S(1)} %collective-permute-done.q_ref, ...), custom_call_target="tpu_custom_call" | custom-call | flops 1024 | bytes 1024 | tf_op jit(solution)/shard_map/cross_0/pallas_call | solution.py:380
  25.8 3.2 %collective-permute-done.2.g_ref = bf16[272,384]{1,0:T(8,128)(2,1)} collective-permute-done((bf16[272,384]{1,0:T(8,128)(2,1)}, bf16[272,384]{1,0:T(8,128)(2,1)}, u32[]{:S(2)}, u32[]{:S(2)}) %collective-permute-start.2) | collective-permute-done | bytes 208928 | tf_op jit(solution)/shard_map/ppermute | solution.py:32
  28.9 2.5 %cross_1.1 = (bf16[16,1152]{1,0:T(8,128)(2,1)S(1)}, bf16[256,1152]{1,0:T(8,128)(2,1)S(1)}, bf16[256,1152]{1,0:T(8,128)(2,1)S(1)}, bf16[256,1152]{1,0:T(8,128)(2,1)S(1)}, f32[3,4,32,128]{3,2,1,0:T(8,128)S(1)}) custom-call(s32[1]{0:T(128)S(6)} %sub.11.live_ref, ...), custom_call_target="tpu_custom_call", output_to_operand_aliasing={{0}: (6, {}), {1}: (7, {}), {2}: (8, {}), {3}: (9, {}), {4}... | custom-call | flops 1024 | bytes 1024 | tf_op jit(solution)/shard_map/cross_1/pallas_call | solution.py:380
  31.4 1.1 %collective-permute-done.1.g_ref = bf16[272,384]{1,0:T(8,128)(2,1)S(1)} collective-permute-done((bf16[272,384]{1,0:T(8,128)(2,1)}, bf16[272,384]{1,0:T(8,128)(2,1)S(1)}, u32[]{:S(2)}, u32[]{:S(2)}) %collective-permute-start.1) | collective-permute-done | bytes 208928 | tf_op jit(solution)/shard_map/ppermute | solution.py:32
  32.5 1.4 %cross_2.1 = (bf16[16,1152]{1,0:T(8,128)(2,1)S(1)}, bf16[256,1152]{1,0:T(8,128)(2,1)S(1)}, bf16[256,1152]{1,0:T(8,128)(2,1)S(1)}, bf16[256,1152]{1,0:T(8,128)(2,1)S(1)}, f32[3,4,32,128]{3,2,1,0:T(8,128)S(1)}) custom-call(s32[1]{0:T(128)S(6)} %sub.11.live_ref, ...), custom_call_target="tpu_custom_call", output_to_operand_aliasing={{0}: (6, {}), {1}: (7, {}), {2}: (8, {}), {3}: (9, {}), {4}... | custom-call | flops 1024 | bytes 1024 | tf_op jit(solution)/shard_map/cross_2/pallas_call | solution.py:380
  33.9 4.5 %collective-permute-start.4 = (bf16[16,1152]{1,0:T(8,128)(2,1)S(1)}, bf16[16,1152]{1,0:T(8,128)(2,1)S(1)}, u32[]{:S(2)}, u32[]{:S(2)}) collective-permute-start(bf16[16,1152]{1,0:T(8,128)(2,1)S(1)} %get-tuple-element.58), channel_id=1, source_target_pairs={{0,1},{1,2},{2,3},{3,4},{4,5},{5,6},{6,7},{8,9},{9,10},{10,11},{11... | collective-permute-start | bytes 110600 | tf_op jit(solution)/shard_map/ppermute | solution.py:32
  38.4 3.4 %collective-permute-start.5 = (bf16[256,1152]{1,0:T(8,128)(2,1)S(1)}, bf16[256,1152]{1,0:T(8,128)(2,1)}, u32[]{:S(2)}, u32[]{:S(2)}) collective-permute-start(bf16[256,1152]{1,0:T(8,128)(2,1)S(1)} %get-tuple-element.59), channel_id=1, source_target_pairs={{0,1},{1,2},{2,3},{3,4},{4,5},{5,6},{6,7},{8,9},{9,10},{10,11},{11... | collective-permute-start | bytes 1769480 | tf_op jit(solution)/shard_map/ppermute | solution.py:32
  41.8 0.0 collective-permute-done.4.given_ref
  41.8 0.0 copy-done.2
  41.8 0.0 copy-start.4
  41.8 0.0 copy-start.5
  41.8 1.3 %table_sums.1 = f32[4,1,2304]{2,1,0:T(1,128)S(1)} custom-call(f32[12,256,256]{2,1,0:T(8,128)S(1)} %copy-done.2, f32[12,256,256]{2,1,0:T(8,128)S(1)} %copy-done.3, f32[3,16,256]{2,1,0:T(8,128)S(1)} %copy-done.7, bf16[16,1152]{1,0:T(8,128)(2,1)S(1)} %collective-permute-done.4.given_ref, f32[3,4,32,128]{3,2,1,0:T(8,128)S(1)} %get-tuple-element.65.cross_ref), custom_call_target="tpu_custom_call" | custom-call | flops 99999997952 | bytes 1024 | tf_op jit(solution)/shard_map/table_sums/pallas_call | solution.py:396
  43.1 0.6 copy-done.8
  43.7 6.5 %all_to_all.10.terms_ref = f32[4,1,2304]{2,1,0:T(1,128)S(1)} all-to-all(f32[4,1,2304]{2,1,0:T(1,128)S(1)} %table_sums.1), channel_id=1, replica_groups=mesh['dp'=4,'tm'=8] {'dp'}, dimensions={0} | all-to-all | bytes 73728 | tf_op jit(solution)/shard_map/all_to_all | solution.py:435
  50.3 0.7 %spread.1 = f32[32,1,2304]{2,1,0:T(1,128)} custom-call(f32[4,1,2304]{2,1,0:T(1,128)S(1)} %all_to_all.10.terms_ref), custom_call_target="tpu_custom_call" | custom-call | flops 1024 | bytes 1024 | tf_op jit(solution)/shard_map/spread/pallas_call | solution.py:423
  51.0 3.5 %all-to-all-start.1 = ((f32[32,1,2304]{2,1,0:T(1,128)}), f32[32,1,2304]{2,1,0:T(1,128)}, u32[]{:S(2)}, u32[]{:S(2)}) async-start(f32[32,1,2304]{2,1,0:T(1,128)} %spread.1), calls=%async_computation.1 | async-start | bytes 589824 | tf_op jit(solution)/shard_map/all_to_all | solution.py:437
  54.5 0.0 collective-permute-done.5.dqc_ref
  54.6 5.9 %own.1 = (bf16[256,1152]{1,0:T(8,128)(2,1)}, bf16[256,1152]{1,0:T(8,128)(2,1)}, bf16[256,1152]{1,0:T(8,128)(2,1)}) custom-call(s32[1]{0:T(128)S(6)} %sub.10.live_ref, bf16[256,1152]{1,0:T(8,128)(2,1)S(1)} %bitcast.25, bf16[256,1152]{1,0:T(8,128)(2,1)S(1)} %bitcast.29, bf16[256,1152]{1,0:T(8,128)(2,1)S(1)} %bitcast.20, ...), custom_call_target="tpu_custom_call" | custom-call | flops 99999997952 | bytes 1024 | tf_op jit(solution)/shard_map/own/pallas_call | solution.py:409
  60.5 5.5 %all-to-all-done.1.every_ref = f32[32,1,2304]{2,1,0:T(1,128)} async-done(((f32[32,1,2304]{2,1,0:T(1,128)}), f32[32,1,2304]{2,1,0:T(1,128)}, u32[]{:S(2)}, u32[]{:S(2)}) %all-to-all-start.1) | async-done | bytes 294944 | tf_op jit(solution)/shard_map/all_to_all | solution.py:437
  65.9 1.6 %gather.1 = f32[12,768]{1,0:T(8,128)} custom-call(f32[32,1,2304]{2,1,0:T(1,128)} %all-to-all-done.1.every_ref, bf16[256,1152]{1,0:T(8,128)(2,1)} %get-tuple-element.62._), custom_call_target="tpu_custom_call" | custom-call | flops 1024 | bytes 1024 | tf_op jit(solution)/shard_map/gather/pallas_call | solution.py:438
  (11 shorter events, 0.0 us)
Async XLA Ops:
  0.6 23.7 %collective-permute-start = (bf16[256,1152]{1,0:T(8,128)(2,1)}, bf16[256,1152]{1,0:T(8,128)(2,1)S(1)}, u32[]{:S(2)}, u32[]{:S(2)}) collective-permute-start(bf16[256,1152]{1,0:T(8,128)(2,1)} %bitcast.21), channel_id=1, source_target_pairs={{1,0},{2,1},{3,2},{4,3},{5,4},{6,5},{7,6},{9,8},{10,9},{11,10},{12... | collective-permute-start | bytes 1769480 | tf_op jit(solution)/shard_map/ppermute | solution.py:32
  6.1 18.3 %collective-permute-start.3 = (bf16[272,384]{1,0:T(8,128)(2,1)}, bf16[272,384]{1,0:T(8,128)(2,1)S(1)}, u32[]{:S(2)}, u32[]{:S(2)}) collective-permute-start(bf16[272,384]{1,0:T(8,128)(2,1)} %get-tuple-element.47), channel_id=1, source_target_pairs={{1,0},{2,1},{3,2},{4,3},{5,4},{6,5},{7,6},{9,8},{10,9},{11,10},{12... | collective-permute-start | bytes 626696 | tf_op jit(solution)/shard_map/ppermute | solution.py:32
  10.6 18.3 %collective-permute-start.2 = (bf16[272,384]{1,0:T(8,128)(2,1)}, bf16[272,384]{1,0:T(8,128)(2,1)}, u32[]{:S(2)}, u32[]{:S(2)}) collective-permute-start(bf16[272,384]{1,0:T(8,128)(2,1)} %get-tuple-element.46), channel_id=1, source_target_pairs={{1,0},{2,1},{3,2},{4,3},{5,4},{6,5},{7,6},{9,8},{10,9},{11,10},{12... | collective-permute-start | bytes 626696 | tf_op jit(solution)/shard_map/ppermute | solution.py:32
  11.9 12.4 %copy-start = (bf16[1,256,1152]{2,1,0:T(8,128)(2,1)S(1)}, bf16[1,256,1152]{2,1,0:T(8,128)(2,1)}, u32[]{:S(2)}) copy-start(bf16[1,256,1152]{2,1,0:T(8,128)(2,1)} %param.8) | copy-start | bytes 1769476
  11.9 12.4 %copy-start.1 = (bf16[1,256,1152]{2,1,0:T(8,128)(2,1)S(1)}, bf16[1,256,1152]{2,1,0:T(8,128)(2,1)}, u32[]{:S(2)}) copy-start(bf16[1,256,1152]{2,1,0:T(8,128)(2,1)} %param.7) | copy-start | bytes 1769476
  11.9 12.4 %copy-start.6 = (f32[12,768]{1,0:T(8,128)S(1)}, f32[12,768]{1,0:T(8,128)}, u32[]{:S(2)}) copy-start(f32[12,768]{1,0:T(8,128)} %get-tuple-element.35.bias_ref.w_ref) | copy-start | bytes 110596
  15.3 17.2 %collective-permute-start.1 = (bf16[272,384]{1,0:T(8,128)(2,1)}, bf16[272,384]{1,0:T(8,128)(2,1)S(1)}, u32[]{:S(2)}, u32[]{:S(2)}) collective-permute-start(bf16[272,384]{1,0:T(8,128)(2,1)} %get-tuple-element.45), channel_id=1, source_target_pairs={{1,0},{2,1},{3,2},{4,3},{5,4},{6,5},{7,6},{9,8},{10,9},{11,10},{12... | collective-permute-start | bytes 626696 | tf_op jit(solution)/shard_map/ppermute | solution.py:32
  28.9 12.9 %copy-start.2 = (f32[12,256,256]{2,1,0:T(8,128)S(1)}, f32[12,256,256]{2,1,0:T(8,128)}, u32[]{:S(2)}) copy-start(f32[12,256,256]{2,1,0:T(8,128)} %get-tuple-element.42.e_ref) | copy-start | bytes 9437188
  28.9 12.9 %copy-start.3 = (f32[12,256,256]{2,1,0:T(8,128)S(1)}, f32[12,256,256]{2,1,0:T(8,128)}, u32[]{:S(2)}) copy-start(f32[12,256,256]{2,1,0:T(8,128)} %get-tuple-element.43.dp_ref) | copy-start | bytes 9437188
  28.9 12.9 %copy-start.7 = (f32[3,16,256]{2,1,0:T(8,128)S(1)}, f32[3,16,256]{2,1,0:T(8,128)}, u32[]{:S(2)}) copy-start(f32[3,16,256]{2,1,0:T(8,128)} %get-tuple-element.44.near_ref) | copy-start | bytes 147460
  33.9 7.9 %collective-permute-start.4 = (bf16[16,1152]{1,0:T(8,128)(2,1)S(1)}, bf16[16,1152]{1,0:T(8,128)(2,1)S(1)}, u32[]{:S(2)}, u32[]{:S(2)}) collective-permute-start(bf16[16,1152]{1,0:T(8,128)(2,1)S(1)} %get-tuple-element.58), channel_id=1, source_target_pairs={{0,1},{1,2},{2,3},{3,4},{4,5},{5,6},{6,7},{8,9},{9,10},{10,11},{11... | collective-permute-start | bytes 110600 | tf_op jit(solution)/shard_map/ppermute | solution.py:32
  38.4 16.1 %collective-permute-start.5 = (bf16[256,1152]{1,0:T(8,128)(2,1)S(1)}, bf16[256,1152]{1,0:T(8,128)(2,1)}, u32[]{:S(2)}, u32[]{:S(2)}) collective-permute-start(bf16[256,1152]{1,0:T(8,128)(2,1)S(1)} %get-tuple-element.59), channel_id=1, source_target_pairs={{0,1},{1,2},{2,3},{3,4},{4,5},{5,6},{6,7},{8,9},{9,10},{10,11},{11... | collective-permute-start | bytes 1769480 | tf_op jit(solution)/shard_map/ppermute | solution.py:32
  41.8 12.7 %copy-start.4 = (bf16[1,256,1152]{2,1,0:T(8,128)(2,1)S(1)}, bf16[1,256,1152]{2,1,0:T(8,128)(2,1)}, u32[]{:S(2)}) copy-start(bf16[1,256,1152]{2,1,0:T(8,128)(2,1)} %param.6) | copy-start | bytes 1769476
  41.8 12.7 %copy-start.5 = (bf16[1,256,1152]{2,1,0:T(8,128)(2,1)S(1)}, bf16[1,256,1152]{2,1,0:T(8,128)(2,1)}, u32[]{:S(2)}) copy-start(bf16[1,256,1152]{2,1,0:T(8,128)(2,1)} %param.9) | copy-start | bytes 1769476
  43.1 0.6 copy-start.8
  51.0 15.0 %all-to-all-start.1 = ((f32[32,1,2304]{2,1,0:T(1,128)}), f32[32,1,2304]{2,1,0:T(1,128)}, u32[]{:S(2)}, u32[]{:S(2)}) async-start(f32[32,1,2304]{2,1,0:T(1,128)} %spread.1), calls=%async_computation.1 | async-start | bytes 589824 | tf_op jit(solution)/shard_map/all_to_all | solution.py:437

commit v5 on v4

--- a/solution.py
+++ b/solution.py
@@ -232,21 +232,21 @@
 
 
 def gather_kernel(count, every_ref, _, out_ref):
-    terms = every_ref.shape[0] // count
-    shape_of_parts = (count,) + every_ref.shape[1:]
-    totals = []
+    each = every_ref.shape[2] // 128
+
+    def one_part(part):
+        total = every_ref[0]
+        for term in range(1, every_ref.shape[0]):
+            total = total + every_ref[term]
+        for tile in range(min(each, out_ref.shape[0] * ROW_TILES - part * each)):
+            row, lane = divmod(part * each + tile, ROW_TILES)
+            out_ref[row : row + 1, 128 * lane : 128 * lane + 128] = total[:, 128 * tile : 128 * tile + 128]
+
     for part in range(count):
-        total = every_ref[part * terms]
-        for term in range(1, terms):
-            total = total + every_ref[part * terms + term]
-        totals.append(total)
-    for row in range(out_ref.shape[0]):
-        for tile in range(ROW_TILES):
-            part, lanes = place(row, tile, shape_of_parts)
-            out_ref[row : row + 1, 128 * tile : 128 * tile + 128] = totals[part][:, lanes]
-
-
-def own_parts(head, group, j, e_ref, dp_ref, near_ref, given):
+        pl.when(pl.program_id(0) == part)(functools.partial(one_part, part))
+
+
+def final_factors(group, j, near_ref, given):
     given_m, given_inverse, given_delta = given
     m_near = near_ref[group, j : j + 1, :]
     inverse_near = 1.0 / near_ref[group, 4 + j : 5 + j, :]
@@ -255,20 +255,23 @@
     m = jnp.where(there, given_m[j : j + 1], m_near)
     ratio = jnp.exp2(m_near - m) * jnp.where(there, inverse, inverse_near)
     delta = jnp.where(there, given_delta[j : j + 1], near_ref[group, 8 + j : 9 + j, :] * inverse_near)
-    p = e_ref[head] * ratio
-    return p, p * (dp_ref[head] - delta)
+    return ratio, delta
 
 
 def lanes_of(group):
     return slice(group * GROUP_LANES, (group + 1) * GROUP_LANES)
 
 
-def table_kernel(groups, e_ref, dp_ref, near_ref, given_ref, cross_ref, table_ref, lines_ref):
+def table_kernel(groups, e_ref, dp_ref, near_ref, given_ref, cross_ref, table_ref, factors_ref, lines_ref):
     table_ref[...] = jnp.zeros_like(table_ref)
     for group in range(groups):
         given = unpack_rows(given_ref.at[:, lanes_of(group)])
         for j in range(GROUP_HEADS):
-            _, ds = own_parts(group * GROUP_HEADS + j, group, j, e_ref, dp_ref, near_ref, given)
+            head = group * GROUP_HEADS + j
+            ratio, delta = final_factors(group, j, near_ref, given)
+            factors_ref[group, j : j + 1, :] = ratio
+            factors_ref[group, 4 + j : 5 + j, :] = delta
+            ds = e_ref[head] * ratio * (dp_ref[head] - delta)
             put_lines(lines_ref.at[group : group + 1], j, unskew(ds))
         a, b = lined(lines_ref, group), lined(cross_ref, group)
         row = jnp.concatenate([a[:, :BLOCK], a[:, BLOCK:] + b[:, :BLOCK], b[:, BLOCK:]], axis=1)
@@ -280,21 +283,22 @@
 
 
 def own_kernel(
-    groups, head_width, live_ref, q_ref, g_ref, k_ref, e_ref, dp_ref, near_ref, given_ref, dqc_ref, dkc_ref, dvc_ref,
+    groups, head_width, live_ref, q_ref, g_ref, k_ref, e_ref, dp_ref, factors_ref, dqc_ref, dkc_ref, dvc_ref,
     dq_ref, dk_ref, dv_ref, dq_acc, dk_acc, dv_acc,
 ):
     live = live_rows(live_ref[0])
 
     def one_group(group):
         lanes = lanes_of(group)
-        given = unpack_rows(given_ref.at[:, lanes])
         heads = []
         for j in range(GROUP_HEADS):
             mask = head_mask(j, head_width, HALF)
             qm = window(q_ref, j, group) * mask
             gm = window(g_ref, j, group) * mask * live
             km = window(k_ref, j, group) * mask
-            p, ds = own_parts(group * GROUP_HEADS + j, group, j, e_ref, dp_ref, near_ref, given)
+            head = group * GROUP_HEADS + j
+            p = e_ref[head] * factors_ref[group, j : j + 1, :]
+            ds = p * (dp_ref[head] - factors_ref[group, 4 + j : 5 + j, :])
             heads.append((qm, gm, km, p.astype(HALF), ds.astype(HALF)))
         pair_products(heads, dq_acc, dk_acc, dv_acc)
         scaling = head_width**-0.5
@@ -396,7 +400,11 @@
     return pl.pallas_call(
         functools.partial(table_kernel, groups),
         in_specs=[VMEM] * 5,
-        out_shape=shape((parts, 1, -(-groups * GROUP_HEADS * ROW_TILES // parts) * 128)),
+        out_specs=[VMEM, VMEM],
+        out_shape=[
+            shape((parts, 1, -(-groups * GROUP_HEADS * ROW_TILES // parts) * 128)),
+            pltpu.HBM((groups, 2 * GROUP_HEADS, BLOCK), jnp.float32),
+        ],
         scratch_shapes=[pltpu.VMEM(lines.shape, jnp.float32)],
         compiler_params=params(),
         cost_estimate=LONG,
@@ -404,19 +412,19 @@
     )(e, dp, near, given, lines)
 
 
-def own(head_width, live, q, g, k, e, dp, near, given, dqc, dkc, dvc):
-    groups = near.shape[0]
+def own(head_width, live, q, g, k, e, dp, factors, dqc, dkc, dvc):
+    groups = factors.shape[0]
     return pl.pallas_call(
         functools.partial(own_kernel, groups, head_width),
         grid=(groups,),
-        in_specs=[SMEM] + [VMEM] * 10,
+        in_specs=[SMEM] + [VMEM] * 9,
         out_specs=[columns()] * 3,
         out_shape=[shape(q.shape, HALF)] * 3,
         scratch_shapes=ACCS,
         compiler_params=params(),
         cost_estimate=LONG,
         name="own",
-    )(live, q, g, k, e, dp, near, given, dqc, dkc, dvc)
+    )(live, q, g, k, e, dp, factors, dqc, dkc, dvc)
 
 
 def spread(terms, count):
@@ -437,7 +445,9 @@
     every = lax.all_to_all(sums, (inner, outer), 0, 0)
     return pl.pallas_call(
         functools.partial(gather_kernel, count),
-        in_specs=[VMEM, ANY],
+        grid=(count,),
+        in_specs=[stack(every.shape[0] // count, *every.shape[1:]), ANY],
+        out_specs=whole_spec((heads, 3 * BLOCK)),
         out_shape=shape((heads, 3 * BLOCK)),
         compiler_params=params(),
         cost_estimate=COST,
@@ -468,8 +478,8 @@
     given = shifted(given, "tm", 1)
     dq_cross = shifted(dq_cross, "tm", 1)
     parts = lax.axis_size("dp")
-    table = table_sums(e, dp, near, given, lines, parts)
-    late = (pltpu.with_memory_space_constraint(a, pltpu.HBM) for a in (e, dp, near, given))
+    table, factors = table_sums(e, dp, near, given, lines, parts)
+    late = (pltpu.with_memory_space_constraint(a, pltpu.HBM) for a in (e, dp, factors))
     dq, dk, dv = own(head_width, live_own, q, g, k, *late, dq_cross, dkc, dvc)
     bias_grad = sum_over_devices(table, "dp", "tm", head_count, dq)
     return tuple(a[None] for a in (dq, dk, dv)) + (bias_grad,)

time: 68 us -> 68.8 us (1.012)
  Pallas kernels: 24.9 us -> 26.3 us
    pallas_call x1, Pallas kernels: 1.62 us -> 2.49 us  [sum_over_devices(): pl.pallas_call(functools.partial(gather_kernel, count), grid=(count,), in...]
  transfers between devices with their start and end apart: 7 -> 7, of which waited for: 4 -> 4; matrix products, arithmetic and copies ran while one was open for 0% -> 0% of each run, Pallas kernels for 32% -> 33%
where the time goes in v5:
time: 68.8 us; the launch traced here: 68.3 us
  Pallas kernels  26.3 us (38%)
  waiting for transfers between devices  17.5 us (25%)
  starting transfers between devices  16.6 us (24%)
  blocking collectives  6.51 us (9%)
  between operations  1.44 us (2%)
    ppermute x6, starting transfers between devices, shifted(): return lax.ppermute(x, axis, pairs)  13 us
    ppermute x6, waiting for transfers between devices, shifted(): return lax.ppermute(x, axis, pairs)  12 us
    pallas_call x3, Pallas kernels, own_stats(): pl.pallas_call(functools.partial(own_stats_kernel, head_width, group), gr...  10.1 us
    all_to_all x1, blocking collectives, sum_over_devices(): terms = lax.all_to_all(parts, inner, 0, 0)  6.51 us
    pallas_call x1, Pallas kernels, own(): pl.pallas_call(functools.partial(own_kernel, groups, head_width), grid=(g...  5.88 us
    all_to_all x1, waiting for transfers between devices, sum_over_devices(): every = lax.all_to_all(sums, (inner, outer), 0, 0)  5.51 us
    pallas_call x3, Pallas kernels, cross(): pl.pallas_call(functools.partial(cross_kernel, head_width, group), grid=(...  5.22 us
    all_to_all x1, starting transfers between devices, sum_over_devices(): every = lax.all_to_all(sums, (inner, outer), 0, 0)  3.52 us
  transfers between devices with their start and end apart: 7, of which 4 were waited for; matrix products, arithmetic and copies ran while one was open for 0% of the time, Pallas kernels for 33%

profile of v5, /device:TPU:0, one launch (start us, length us, event | category | flops | bytes accessed | tf_op | source)
XLA Modules:
  0.0 68.3 jit_solution(6652352434857330939)
XLA Ops:
  0.6 1.3 %collective-permute-start = (bf16[256,1152]{1,0:T(8,128)(2,1)}, bf16[256,1152]{1,0:T(8,128)(2,1)S(1)}, u32[]{:S(2)}, u32[]{:S(2)}) collective-permute-start(bf16[256,1152]{1,0:T(8,128)(2,1)} %bitcast.21), channel_id=1, source_target_pairs={{1,0},{2,1},{3,2},{4,3},{5,4},{6,5},{7,6},{9,8},{10,9},{11,10},{12... | collective-permute-start | bytes 1769480 | tf_op jit(solution)/shard_map/ppermute | solution.py:32
  2.6 3.5 %own_stats_0.1 = (f32[3,16,256]{2,1,0:T(8,128)}, f32[12,256,256]{2,1,0:T(8,128)}, f32[12,256,256]{2,1,0:T(8,128)}, bf16[272,384]{1,0:T(8,128)(2,1)}, f32[12,768]{1,0:T(8,128)}) custom-call(s32[1]{0:T(128)S(6)} %sub.10.live_ref, bf16[256,1152]{1,0:T(8,128)(2,1)} %bitcast.22, bf16[256,1152]{1,0:T(8,128)(2,1)} %bitcast.26, bf16[256,1152]{1,0:T(8,128)(2,1)} %bitcast.14, ...), custom_call_target="tpu_custom_call" | custom-call | flops 1024 | bytes 1024 | tf_op jit(solution)/shard_map/own_stats_0/pallas_call | solution.py:368
  6.1 1.3 %collective-permute-start.3 = (bf16[272,384]{1,0:T(8,128)(2,1)}, bf16[272,384]{1,0:T(8,128)(2,1)S(1)}, u32[]{:S(2)}, u32[]{:S(2)}) collective-permute-start(bf16[272,384]{1,0:T(8,128)(2,1)} %get-tuple-element.49), channel_id=1, source_target_pairs={{1,0},{2,1},{3,2},{4,3},{5,4},{6,5},{7,6},{9,8},{10,9},{11,10},{12... | collective-permute-start | bytes 626696 | tf_op jit(solution)/shard_map/ppermute | solution.py:32
  7.3 3.3 %own_stats_1.1 = (f32[3,16,256]{2,1,0:T(8,128)}, f32[12,256,256]{2,1,0:T(8,128)}, f32[12,256,256]{2,1,0:T(8,128)}, bf16[272,384]{1,0:T(8,128)(2,1)}) custom-call(s32[1]{0:T(128)S(6)} %sub.10.live_ref, bf16[256,1152]{1,0:T(8,128)(2,1)} %bitcast.23, bf16[256,1152]{1,0:T(8,128)(2,1)} %bitcast.27, ...), custom_call_target="tpu_custom_call", output_to_operand_aliasing={{0}: (6, {}), {1}: (7, {}), {2}: (8, {})} | custom-call | flops 1024 | bytes 1024 | tf_op jit(solution)/shard_map/own_stats_1/pallas_call | solution.py:368
  10.6 1.3 %collective-permute-start.2 = (bf16[272,384]{1,0:T(8,128)(2,1)}, bf16[272,384]{1,0:T(8,128)(2,1)}, u32[]{:S(2)}, u32[]{:S(2)}) collective-permute-start(bf16[272,384]{1,0:T(8,128)(2,1)} %get-tuple-element.48), channel_id=1, source_target_pairs={{1,0},{2,1},{3,2},{4,3},{5,4},{6,5},{7,6},{9,8},{10,9},{11,10},{12... | collective-permute-start | bytes 626696 | tf_op jit(solution)/shard_map/ppermute | solution.py:32
  11.9 0.0 copy-start
  11.9 0.0 copy-start.1
  11.9 3.4 %own_stats_2.1 = (f32[3,16,256]{2,1,0:T(8,128)}, f32[12,256,256]{2,1,0:T(8,128)}, f32[12,256,256]{2,1,0:T(8,128)}, bf16[272,384]{1,0:T(8,128)(2,1)}) custom-call(s32[1]{0:T(128)S(6)} %sub.10.live_ref, bf16[256,1152]{1,0:T(8,128)(2,1)} %bitcast.24, bf16[256,1152]{1,0:T(8,128)(2,1)} %bitcast.28, ...), custom_call_target="tpu_custom_call", output_to_operand_aliasing={{0}: (6, {}), {1}: (7, {}), {2}: (8, {})} | custom-call | flops 1024 | bytes 1024 | tf_op jit(solution)/shard_map/own_stats_2/pallas_call | solution.py:368
  15.3 1.3 %collective-permute-start.1 = (bf16[272,384]{1,0:T(8,128)(2,1)}, bf16[272,384]{1,0:T(8,128)(2,1)S(1)}, u32[]{:S(2)}, u32[]{:S(2)}) collective-permute-start(bf16[272,384]{1,0:T(8,128)(2,1)} %get-tuple-element.47), channel_id=1, source_target_pairs={{1,0},{2,1},{3,2},{4,3},{5,4},{6,5},{7,6},{9,8},{10,9},{11,10},{12... | collective-permute-start | bytes 626696 | tf_op jit(solution)/shard_map/ppermute | solution.py:32
  16.6 7.7 %collective-permute-done.3.g_ref = bf16[272,384]{1,0:T(8,128)(2,1)S(1)} collective-permute-done((bf16[272,384]{1,0:T(8,128)(2,1)}, bf16[272,384]{1,0:T(8,128)(2,1)S(1)}, u32[]{:S(2)}, u32[]{:S(2)}) %collective-permute-start.3) | collective-permute-done | bytes 208928 | tf_op jit(solution)/shard_map/ppermute | solution.py:32
  24.3 0.0 collective-permute-done.q_ref
  24.3 0.0 copy-done
  24.4 1.4 %cross_0.1 = (bf16[16,1152]{1,0:T(8,128)(2,1)S(1)}, bf16[256,1152]{1,0:T(8,128)(2,1)S(1)}, bf16[256,1152]{1,0:T(8,128)(2,1)S(1)}, bf16[256,1152]{1,0:T(8,128)(2,1)S(1)}, f32[3,4,32,128]{3,2,1,0:T(8,128)S(1)}) custom-call(s32[1]{0:T(128)S(6)} %sub.11.live_ref, bf16[256,1152]{1,0:T(8,128)(2,1)S(1)} %collective-permute-done.q_ref, ...), custom_call_target="tpu_custom_call" | custom-call | flops 1024 | bytes 1024 | tf_op jit(solution)/shard_map/cross_0/pallas_call | solution.py:384
  25.8 3.2 %collective-permute-done.2.g_ref = bf16[272,384]{1,0:T(8,128)(2,1)} collective-permute-done((bf16[272,384]{1,0:T(8,128)(2,1)}, bf16[272,384]{1,0:T(8,128)(2,1)}, u32[]{:S(2)}, u32[]{:S(2)}) %collective-permute-start.2) | collective-permute-done | bytes 208928 | tf_op jit(solution)/shard_map/ppermute | solution.py:32
  28.9 2.5 %cross_1.1 = (bf16[16,1152]{1,0:T(8,128)(2,1)S(1)}, bf16[256,1152]{1,0:T(8,128)(2,1)S(1)}, bf16[256,1152]{1,0:T(8,128)(2,1)S(1)}, bf16[256,1152]{1,0:T(8,128)(2,1)S(1)}, f32[3,4,32,128]{3,2,1,0:T(8,128)S(1)}) custom-call(s32[1]{0:T(128)S(6)} %sub.11.live_ref, ...), custom_call_target="tpu_custom_call", output_to_operand_aliasing={{0}: (6, {}), {1}: (7, {}), {2}: (8, {}), {3}: (9, {}), {4}... | custom-call | flops 1024 | bytes 1024 | tf_op jit(solution)/shard_map/cross_1/pallas_call | solution.py:384
  31.4 1.1 %collective-permute-done.1.g_ref = bf16[272,384]{1,0:T(8,128)(2,1)S(1)} collective-permute-done((bf16[272,384]{1,0:T(8,128)(2,1)}, bf16[272,384]{1,0:T(8,128)(2,1)S(1)}, u32[]{:S(2)}, u32[]{:S(2)}) %collective-permute-start.1) | collective-permute-done | bytes 208928 | tf_op jit(solution)/shard_map/ppermute | solution.py:32
  32.5 1.4 %cross_2.1 = (bf16[16,1152]{1,0:T(8,128)(2,1)S(1)}, bf16[256,1152]{1,0:T(8,128)(2,1)S(1)}, bf16[256,1152]{1,0:T(8,128)(2,1)S(1)}, bf16[256,1152]{1,0:T(8,128)(2,1)S(1)}, f32[3,4,32,128]{3,2,1,0:T(8,128)S(1)}) custom-call(s32[1]{0:T(128)S(6)} %sub.11.live_ref, ...), custom_call_target="tpu_custom_call", output_to_operand_aliasing={{0}: (6, {}), {1}: (7, {}), {2}: (8, {}), {3}: (9, {}), {4}... | custom-call | flops 1024 | bytes 1024 | tf_op jit(solution)/shard_map/cross_2/pallas_call | solution.py:384
  33.9 4.5 %collective-permute-start.4 = (bf16[16,1152]{1,0:T(8,128)(2,1)S(1)}, bf16[16,1152]{1,0:T(8,128)(2,1)S(1)}, u32[]{:S(2)}, u32[]{:S(2)}) collective-permute-start(bf16[16,1152]{1,0:T(8,128)(2,1)S(1)} %get-tuple-element.60), channel_id=1, source_target_pairs={{0,1},{1,2},{2,3},{3,4},{4,5},{5,6},{6,7},{8,9},{9,10},{10,11},{11... | collective-permute-start | bytes 110600 | tf_op jit(solution)/shard_map/ppermute | solution.py:32
  38.4 3.4 %collective-permute-start.5 = (bf16[256,1152]{1,0:T(8,128)(2,1)S(1)}, bf16[256,1152]{1,0:T(8,128)(2,1)}, u32[]{:S(2)}, u32[]{:S(2)}) collective-permute-start(bf16[256,1152]{1,0:T(8,128)(2,1)S(1)} %get-tuple-element.63), channel_id=1, source_target_pairs={{0,1},{1,2},{2,3},{3,4},{4,5},{5,6},{6,7},{8,9},{9,10},{10,11},{11... | collective-permute-start | bytes 1769480 | tf_op jit(solution)/shard_map/ppermute | solution.py:32
  41.8 0.0 collective-permute-done.4.given_ref
  41.8 0.0 copy-done.2
  41.8 0.0 copy-start.4
  41.8 0.0 copy-start.5
  41.8 1.8 %table_sums.1 = (f32[4,1,2304]{2,1,0:T(1,128)S(1)}, f32[3,8,256]{2,1,0:T(8,128)}) custom-call(f32[12,256,256]{2,1,0:T(8,128)S(1)} %copy-done.2, f32[12,256,256]{2,1,0:T(8,128)S(1)} %copy-done.3, f32[3,16,256]{2,1,0:T(8,128)S(1)} %copy-done.7, bf16[16,1152]{1,0:T(8,128)(2,1)S(1)} %collective-permute-done.4.given_ref, ...), custom_call_target="tpu_custom_call" | custom-call | flops 99999997952 | bytes 1024 | tf_op jit(solution)/shard_map/table_sums/pallas_call | solution.py:400
  43.6 6.5 %all_to_all.10.terms_ref = f32[4,1,2304]{2,1,0:T(1,128)S(1)} all-to-all(f32[4,1,2304]{2,1,0:T(1,128)S(1)} %get-tuple-element.69), channel_id=1, replica_groups=mesh['dp'=4,'tm'=8] {'dp'}, dimensions={0} | all-to-all | bytes 73728 | tf_op jit(solution)/shard_map/all_to_all | solution.py:443
  50.1 0.7 %spread.1 = f32[32,1,2304]{2,1,0:T(1,128)} custom-call(f32[4,1,2304]{2,1,0:T(1,128)S(1)} %all_to_all.10.terms_ref), custom_call_target="tpu_custom_call" | custom-call | flops 1024 | bytes 1024 | tf_op jit(solution)/shard_map/spread/pallas_call | solution.py:431
  50.9 3.5 %all-to-all-start.1 = ((f32[32,1,2304]{2,1,0:T(1,128)}), f32[32,1,2304]{2,1,0:T(1,128)}, u32[]{:S(2)}, u32[]{:S(2)}) async-start(f32[32,1,2304]{2,1,0:T(1,128)} %spread.1), calls=%async_computation.1 | async-start | bytes 589824 | tf_op jit(solution)/shard_map/all_to_all | solution.py:445
  54.4 0.0 collective-permute-done.5.dqc_ref
  54.4 0.0 copy-done.4
  54.4 5.9 %own.1 = (bf16[256,1152]{1,0:T(8,128)(2,1)}, bf16[256,1152]{1,0:T(8,128)(2,1)}, bf16[256,1152]{1,0:T(8,128)(2,1)}) custom-call(s32[1]{0:T(128)S(6)} %sub.10.live_ref, bf16[256,1152]{1,0:T(8,128)(2,1)S(1)} %bitcast.25, bf16[256,1152]{1,0:T(8,128)(2,1)S(1)} %bitcast.29, bf16[256,1152]{1,0:T(8,128)(2,1)S(1)} %bitcast.20, ...), custom_call_target="tpu_custom_call" | custom-call | flops 99999997952 | bytes 1024 | tf_op jit(solution)/shard_map/own/pallas_call | solution.py:417
  60.3 5.5 %all-to-all-done.1.every_ref = f32[32,1,2304]{2,1,0:T(1,128)} async-done(((f32[32,1,2304]{2,1,0:T(1,128)}), f32[32,1,2304]{2,1,0:T(1,128)}, u32[]{:S(2)}, u32[]{:S(2)}) %all-to-all-start.1) | async-done | bytes 294944 | tf_op jit(solution)/shard_map/all_to_all | solution.py:445
  65.8 2.5 %gather.1 = f32[12,768]{1,0:T(8,128)} custom-call(f32[32,1,2304]{2,1,0:T(1,128)} %all-to-all-done.1.every_ref, bf16[256,1152]{1,0:T(8,128)(2,1)} %get-tuple-element.66._), custom_call_target="tpu_custom_call" | custom-call | flops 1024 | bytes 1024 | tf_op jit(solution)/shard_map/gather/pallas_call | solution.py:446
  (9 shorter events, 0.0 us)
Async XLA Ops:
  0.6 23.7 %collective-permute-start = (bf16[256,1152]{1,0:T(8,128)(2,1)}, bf16[256,1152]{1,0:T(8,128)(2,1)S(1)}, u32[]{:S(2)}, u32[]{:S(2)}) collective-permute-start(bf16[256,1152]{1,0:T(8,128)(2,1)} %bitcast.21), channel_id=1, source_target_pairs={{1,0},{2,1},{3,2},{4,3},{5,4},{6,5},{7,6},{9,8},{10,9},{11,10},{12... | collective-permute-start | bytes 1769480 | tf_op jit(solution)/shard_map/ppermute | solution.py:32
  6.1 18.3 %collective-permute-start.3 = (bf16[272,384]{1,0:T(8,128)(2,1)}, bf16[272,384]{1,0:T(8,128)(2,1)S(1)}, u32[]{:S(2)}, u32[]{:S(2)}) collective-permute-start(bf16[272,384]{1,0:T(8,128)(2,1)} %get-tuple-element.49), channel_id=1, source_target_pairs={{1,0},{2,1},{3,2},{4,3},{5,4},{6,5},{7,6},{9,8},{10,9},{11,10},{12... | collective-permute-start | bytes 626696 | tf_op jit(solution)/shard_map/ppermute | solution.py:32
  10.6 18.3 %collective-permute-start.2 = (bf16[272,384]{1,0:T(8,128)(2,1)}, bf16[272,384]{1,0:T(8,128)(2,1)}, u32[]{:S(2)}, u32[]{:S(2)}) collective-permute-start(bf16[272,384]{1,0:T(8,128)(2,1)} %get-tuple-element.48), channel_id=1, source_target_pairs={{1,0},{2,1},{3,2},{4,3},{5,4},{6,5},{7,6},{9,8},{10,9},{11,10},{12... | collective-permute-start | bytes 626696 | tf_op jit(solution)/shard_map/ppermute | solution.py:32
  11.9 12.4 %copy-start = (bf16[1,256,1152]{2,1,0:T(8,128)(2,1)S(1)}, bf16[1,256,1152]{2,1,0:T(8,128)(2,1)}, u32[]{:S(2)}) copy-start(bf16[1,256,1152]{2,1,0:T(8,128)(2,1)} %param.8) | copy-start | bytes 1769476
  11.9 12.4 %copy-start.1 = (bf16[1,256,1152]{2,1,0:T(8,128)(2,1)S(1)}, bf16[1,256,1152]{2,1,0:T(8,128)(2,1)}, u32[]{:S(2)}) copy-start(bf16[1,256,1152]{2,1,0:T(8,128)(2,1)} %param.7) | copy-start | bytes 1769476
  11.9 12.4 %copy-start.6 = (f32[12,768]{1,0:T(8,128)S(1)}, f32[12,768]{1,0:T(8,128)}, u32[]{:S(2)}) copy-start(f32[12,768]{1,0:T(8,128)} %get-tuple-element.37.bias_ref.w_ref) | copy-start | bytes 110596
  15.3 17.2 %collective-permute-start.1 = (bf16[272,384]{1,0:T(8,128)(2,1)}, bf16[272,384]{1,0:T(8,128)(2,1)S(1)}, u32[]{:S(2)}, u32[]{:S(2)}) collective-permute-start(bf16[272,384]{1,0:T(8,128)(2,1)} %get-tuple-element.47), channel_id=1, source_target_pairs={{1,0},{2,1},{3,2},{4,3},{5,4},{6,5},{7,6},{9,8},{10,9},{11,10},{12... | collective-permute-start | bytes 626696 | tf_op jit(solution)/shard_map/ppermute | solution.py:32
  28.9 12.9 %copy-start.2 = (f32[12,256,256]{2,1,0:T(8,128)S(1)}, f32[12,256,256]{2,1,0:T(8,128)}, u32[]{:S(2)}) copy-start(f32[12,256,256]{2,1,0:T(8,128)} %get-tuple-element.44.e_ref) | copy-start | bytes 9437188
  28.9 12.9 %copy-start.3 = (f32[12,256,256]{2,1,0:T(8,128)S(1)}, f32[12,256,256]{2,1,0:T(8,128)}, u32[]{:S(2)}) copy-start(f32[12,256,256]{2,1,0:T(8,128)} %get-tuple-element.45.dp_ref) | copy-start | bytes 9437188
  28.9 12.9 %copy-start.7 = (f32[3,16,256]{2,1,0:T(8,128)S(1)}, f32[3,16,256]{2,1,0:T(8,128)}, u32[]{:S(2)}) copy-start(f32[3,16,256]{2,1,0:T(8,128)} %get-tuple-element.46.near_ref) | copy-start | bytes 147460
  33.9 7.9 %collective-permute-start.4 = (bf16[16,1152]{1,0:T(8,128)(2,1)S(1)}, bf16[16,1152]{1,0:T(8,128)(2,1)S(1)}, u32[]{:S(2)}, u32[]{:S(2)}) collective-permute-start(bf16[16,1152]{1,0:T(8,128)(2,1)S(1)} %get-tuple-element.60), channel_id=1, source_target_pairs={{0,1},{1,2},{2,3},{3,4},{4,5},{5,6},{6,7},{8,9},{9,10},{10,11},{11... | collective-permute-start | bytes 110600 | tf_op jit(solution)/shard_map/ppermute | solution.py:32
  38.4 16.0 %collective-permute-start.5 = (bf16[256,1152]{1,0:T(8,128)(2,1)S(1)}, bf16[256,1152]{1,0:T(8,128)(2,1)}, u32[]{:S(2)}, u32[]{:S(2)}) collective-permute-start(bf16[256,1152]{1,0:T(8,128)(2,1)S(1)} %get-tuple-element.63), channel_id=1, source_target_pairs={{0,1},{1,2},{2,3},{3,4},{4,5},{5,6},{6,7},{8,9},{9,10},{10,11},{11... | collective-permute-start | bytes 1769480 | tf_op jit(solution)/shard_map/ppermute | solution.py:32
  41.8 12.6 %copy-start.4 = (bf16[1,256,1152]{2,1,0:T(8,128)(2,1)S(1)}, bf16[1,256,1152]{2,1,0:T(8,128)(2,1)}, u32[]{:S(2)}) copy-start(bf16[1,256,1152]{2,1,0:T(8,128)(2,1)} %param.6) | copy-start | bytes 1769476
  41.8 12.6 %copy-start.5 = (bf16[1,256,1152]{2,1,0:T(8,128)(2,1)S(1)}, bf16[1,256,1152]{2,1,0:T(8,128)(2,1)}, u32[]{:S(2)}) copy-start(bf16[1,256,1152]{2,1,0:T(8,128)(2,1)} %param.9) | copy-start | bytes 1769476
  50.9 15.0 %all-to-all-start.1 = ((f32[32,1,2304]{2,1,0:T(1,128)}), f32[32,1,2304]{2,1,0:T(1,128)}, u32[]{:S(2)}, u32[]{:S(2)}) async-start(f32[32,1,2304]{2,1,0:T(1,128)} %spread.1), calls=%async_computation.1 | async-start | bytes 589824 | tf_op jit(solution)/shard_map/all_to_all | solution.py:445

commit v6 on v4

--- a/solution.py
+++ b/solution.py
@@ -324,7 +324,7 @@
 VMEM = pl.BlockSpec(memory_space=pltpu.VMEM)
 ACCS = [pltpu.VMEM((BLOCK, GROUP_LANES), jnp.float32)] * 3
 PACKED = BLOCK + 16
-LINES = (1, 4, 8 * GROUP_HEADS, 128)
+LINES = (1, 4, 64, 128)
 
 
 def whole_spec(s):

time: 68 us -> 68 us (level)
  no operation moved by 1% of the time
where the time goes in v6:
time: 68 us; the launch traced here: 67.6 us
  Pallas kernels  24.9 us (37%)
  waiting for transfers between devices  17.5 us (26%)
  starting transfers between devices  16.6 us (24%)
  blocking collectives  6.51 us (10%)
  between operations  1.46 us (2%)
    ppermute x6, starting transfers between devices, shifted(): return lax.ppermute(x, axis, pairs)  13 us
    ppermute x6, waiting for transfers between devices, shifted(): return lax.ppermute(x, axis, pairs)  12 us
    pallas_call x3, Pallas kernels, own_stats(): pl.pallas_call(functools.partial(own_stats_kernel, head_width, group), gr...  10.1 us
    all_to_all x1, blocking collectives, sum_over_devices(): terms = lax.all_to_all(parts, inner, 0, 0)  6.51 us
    pallas_call x1, Pallas kernels, own(): pl.pallas_call(functools.partial(own_kernel, groups, head_width), grid=(g...  5.92 us
    all_to_all x1, waiting for transfers between devices, sum_over_devices(): every = lax.all_to_all(sums, (inner, outer), 0, 0)  5.47 us
    pallas_call x3, Pallas kernels, cross(): pl.pallas_call(functools.partial(cross_kernel, head_width, group), grid=(...  5.23 us
    all_to_all x1, starting transfers between devices, sum_over_devices(): every = lax.all_to_all(sums, (inner, outer), 0, 0)  3.52 us
  transfers between devices with their start and end apart: 7, of which 4 were waited for; matrix products, arithmetic and copies ran while one was open for 0% of the time, Pallas kernels for 32%

profile of v6, /device:TPU:0, one launch (start us, length us, event | category | flops | bytes accessed | tf_op | source)
XLA Modules:
  0.0 67.6 jit_solution(17565718017826264480)
XLA Ops:
  0.6 1.3 %collective-permute-start = (bf16[256,1152]{1,0:T(8,128)(2,1)}, bf16[256,1152]{1,0:T(8,128)(2,1)S(1)}, u32[]{:S(2)}, u32[]{:S(2)}) collective-permute-start(bf16[256,1152]{1,0:T(8,128)(2,1)} %bitcast.21), channel_id=1, source_target_pairs={{1,0},{2,1},{3,2},{4,3},{5,4},{6,5},{7,6},{9,8},{10,9},{11,10},{12... | collective-permute-start | bytes 1769480 | tf_op jit(solution)/shard_map/ppermute | solution.py:32
  2.6 3.5 %own_stats_0.1 = (f32[3,16,256]{2,1,0:T(8,128)}, f32[12,256,256]{2,1,0:T(8,128)}, f32[12,256,256]{2,1,0:T(8,128)}, bf16[272,384]{1,0:T(8,128)(2,1)}, f32[12,768]{1,0:T(8,128)}) custom-call(s32[1]{0:T(128)S(6)} %sub.10.live_ref, bf16[256,1152]{1,0:T(8,128)(2,1)} %bitcast.22, bf16[256,1152]{1,0:T(8,128)(2,1)} %bitcast.26, bf16[256,1152]{1,0:T(8,128)(2,1)} %bitcast.14, ...), custom_call_target="tpu_custom_call" | custom-call | flops 1024 | bytes 1024 | tf_op jit(solution)/shard_map/own_stats_0/pallas_call | solution.py:364
  6.1 1.3 %collective-permute-start.3 = (bf16[272,384]{1,0:T(8,128)(2,1)}, bf16[272,384]{1,0:T(8,128)(2,1)S(1)}, u32[]{:S(2)}, u32[]{:S(2)}) collective-permute-start(bf16[272,384]{1,0:T(8,128)(2,1)} %get-tuple-element.47), channel_id=1, source_target_pairs={{1,0},{2,1},{3,2},{4,3},{5,4},{6,5},{7,6},{9,8},{10,9},{11,10},{12... | collective-permute-start | bytes 626696 | tf_op jit(solution)/shard_map/ppermute | solution.py:32
  7.3 3.3 %own_stats_1.1 = (f32[3,16,256]{2,1,0:T(8,128)}, f32[12,256,256]{2,1,0:T(8,128)}, f32[12,256,256]{2,1,0:T(8,128)}, bf16[272,384]{1,0:T(8,128)(2,1)}) custom-call(s32[1]{0:T(128)S(6)} %sub.10.live_ref, bf16[256,1152]{1,0:T(8,128)(2,1)} %bitcast.23, bf16[256,1152]{1,0:T(8,128)(2,1)} %bitcast.27, ...), custom_call_target="tpu_custom_call", output_to_operand_aliasing={{0}: (6, {}), {1}: (7, {}), {2}: (8, {})} | custom-call | flops 1024 | bytes 1024 | tf_op jit(solution)/shard_map/own_stats_1/pallas_call | solution.py:364
  10.6 1.3 %collective-permute-start.2 = (bf16[272,384]{1,0:T(8,128)(2,1)}, bf16[272,384]{1,0:T(8,128)(2,1)}, u32[]{:S(2)}, u32[]{:S(2)}) collective-permute-start(bf16[272,384]{1,0:T(8,128)(2,1)} %get-tuple-element.46), channel_id=1, source_target_pairs={{1,0},{2,1},{3,2},{4,3},{5,4},{6,5},{7,6},{9,8},{10,9},{11,10},{12... | collective-permute-start | bytes 626696 | tf_op jit(solution)/shard_map/ppermute | solution.py:32
  11.9 0.0 copy-start
  11.9 0.0 copy-start.1
  11.9 3.4 %own_stats_2.1 = (f32[3,16,256]{2,1,0:T(8,128)}, f32[12,256,256]{2,1,0:T(8,128)}, f32[12,256,256]{2,1,0:T(8,128)}, bf16[272,384]{1,0:T(8,128)(2,1)}) custom-call(s32[1]{0:T(128)S(6)} %sub.10.live_ref, bf16[256,1152]{1,0:T(8,128)(2,1)} %bitcast.24, bf16[256,1152]{1,0:T(8,128)(2,1)} %bitcast.28, ...), custom_call_target="tpu_custom_call", output_to_operand_aliasing={{0}: (6, {}), {1}: (7, {}), {2}: (8, {})} | custom-call | flops 1024 | bytes 1024 | tf_op jit(solution)/shard_map/own_stats_2/pallas_call | solution.py:364
  15.3 1.3 %collective-permute-start.1 = (bf16[272,384]{1,0:T(8,128)(2,1)}, bf16[272,384]{1,0:T(8,128)(2,1)S(1)}, u32[]{:S(2)}, u32[]{:S(2)}) collective-permute-start(bf16[272,384]{1,0:T(8,128)(2,1)} %get-tuple-element.45), channel_id=1, source_target_pairs={{1,0},{2,1},{3,2},{4,3},{5,4},{6,5},{7,6},{9,8},{10,9},{11,10},{12... | collective-permute-start | bytes 626696 | tf_op jit(solution)/shard_map/ppermute | solution.py:32
  16.6 7.7 %collective-permute-done.3.g_ref = bf16[272,384]{1,0:T(8,128)(2,1)S(1)} collective-permute-done((bf16[272,384]{1,0:T(8,128)(2,1)}, bf16[272,384]{1,0:T(8,128)(2,1)S(1)}, u32[]{:S(2)}, u32[]{:S(2)}) %collective-permute-start.3) | collective-permute-done | bytes 208928 | tf_op jit(solution)/shard_map/ppermute | solution.py:32
  24.3 0.0 collective-permute-done.q_ref
  24.3 0.0 copy-done
  24.4 1.4 %cross_0.1 = (bf16[16,1152]{1,0:T(8,128)(2,1)S(1)}, bf16[256,1152]{1,0:T(8,128)(2,1)S(1)}, bf16[256,1152]{1,0:T(8,128)(2,1)S(1)}, bf16[256,1152]{1,0:T(8,128)(2,1)S(1)}, f32[3,4,64,128]{3,2,1,0:T(8,128)S(1)}) custom-call(s32[1]{0:T(128)S(6)} %sub.11.live_ref, bf16[256,1152]{1,0:T(8,128)(2,1)S(1)} %collective-permute-done.q_ref, ...), custom_call_target="tpu_custom_call" | custom-call | flops 1024 | bytes 1024 | tf_op jit(solution)/shard_map/cross_0/pallas_call | solution.py:380
  25.8 3.2 %collective-permute-done.2.g_ref = bf16[272,384]{1,0:T(8,128)(2,1)} collective-permute-done((bf16[272,384]{1,0:T(8,128)(2,1)}, bf16[272,384]{1,0:T(8,128)(2,1)}, u32[]{:S(2)}, u32[]{:S(2)}) %collective-permute-start.2) | collective-permute-done | bytes 208928 | tf_op jit(solution)/shard_map/ppermute | solution.py:32
  28.9 2.5 %cross_1.1 = (bf16[16,1152]{1,0:T(8,128)(2,1)S(1)}, bf16[256,1152]{1,0:T(8,128)(2,1)S(1)}, bf16[256,1152]{1,0:T(8,128)(2,1)S(1)}, bf16[256,1152]{1,0:T(8,128)(2,1)S(1)}, f32[3,4,64,128]{3,2,1,0:T(8,128)S(1)}) custom-call(s32[1]{0:T(128)S(6)} %sub.11.live_ref, ...), custom_call_target="tpu_custom_call", output_to_operand_aliasing={{0}: (6, {}), {1}: (7, {}), {2}: (8, {}), {3}: (9, {}), {4}... | custom-call | flops 1024 | bytes 1024 | tf_op jit(solution)/shard_map/cross_1/pallas_call | solution.py:380
  31.4 0.0 copy-start.7
  31.4 1.1 %collective-permute-done.1.g_ref = bf16[272,384]{1,0:T(8,128)(2,1)S(1)} collective-permute-done((bf16[272,384]{1,0:T(8,128)(2,1)}, bf16[272,384]{1,0:T(8,128)(2,1)S(1)}, u32[]{:S(2)}, u32[]{:S(2)}) %collective-permute-start.1) | collective-permute-done | bytes 208928 | tf_op jit(solution)/shard_map/ppermute | solution.py:32
  32.5 1.4 %cross_2.1 = (bf16[16,1152]{1,0:T(8,128)(2,1)S(1)}, bf16[256,1152]{1,0:T(8,128)(2,1)S(1)}, bf16[256,1152]{1,0:T(8,128)(2,1)S(1)}, bf16[256,1152]{1,0:T(8,128)(2,1)S(1)}, f32[3,4,64,128]{3,2,1,0:T(8,128)S(1)}) custom-call(s32[1]{0:T(128)S(6)} %sub.11.live_ref, ...), custom_call_target="tpu_custom_call", output_to_operand_aliasing={{0}: (6, {}), {1}: (7, {}), {2}: (8, {}), {3}: (9, {}), {4}... | custom-call | flops 1024 | bytes 1024 | tf_op jit(solution)/shard_map/cross_2/pallas_call | solution.py:380
  33.9 4.5 %collective-permute-start.4 = (bf16[16,1152]{1,0:T(8,128)(2,1)S(1)}, bf16[16,1152]{1,0:T(8,128)(2,1)S(1)}, u32[]{:S(2)}, u32[]{:S(2)}) collective-permute-start(bf16[16,1152]{1,0:T(8,128)(2,1)S(1)} %get-tuple-element.58), channel_id=1, source_target_pairs={{0,1},{1,2},{2,3},{3,4},{4,5},{5,6},{6,7},{8,9},{9,10},{10,11},{11... | collective-permute-start | bytes 110600 | tf_op jit(solution)/shard_map/ppermute | solution.py:32
  38.4 3.4 %collective-permute-start.5 = (bf16[256,1152]{1,0:T(8,128)(2,1)S(1)}, bf16[256,1152]{1,0:T(8,128)(2,1)}, u32[]{:S(2)}, u32[]{:S(2)}) collective-permute-start(bf16[256,1152]{1,0:T(8,128)(2,1)S(1)} %get-tuple-element.59), channel_id=1, source_target_pairs={{0,1},{1,2},{2,3},{3,4},{4,5},{5,6},{6,7},{8,9},{9,10},{10,11},{11... | collective-permute-start | bytes 1769480 | tf_op jit(solution)/shard_map/ppermute | solution.py:32
  41.8 0.0 collective-permute-done.4.given_ref
  41.8 0.0 copy-start.4
  41.8 0.0 copy-start.5
  41.8 1.3 %table_sums.1 = f32[4,1,2304]{2,1,0:T(1,128)S(1)} custom-call(f32[12,256,256]{2,1,0:T(8,128)S(1)} %copy-done.2, f32[12,256,256]{2,1,0:T(8,128)S(1)} %copy-done.3, f32[3,16,256]{2,1,0:T(8,128)S(1)} %copy-done.7, bf16[16,1152]{1,0:T(8,128)(2,1)S(1)} %collective-permute-done.4.given_ref, f32[3,4,64,128]{3,2,1,0:T(8,128)S(1)} %get-tuple-element.65.cross_ref), custom_call_target="tpu_custom_call" | custom-call | flops 99999997952 | bytes 1024 | tf_op jit(solution)/shard_map/table_sums/pallas_call | solution.py:396
  43.1 0.6 copy-done.8
  43.7 6.5 %all_to_all.10.terms_ref = f32[4,1,2304]{2,1,0:T(1,128)S(1)} all-to-all(f32[4,1,2304]{2,1,0:T(1,128)S(1)} %table_sums.1), channel_id=1, replica_groups=mesh['dp'=4,'tm'=8] {'dp'}, dimensions={0} | all-to-all | bytes 73728 | tf_op jit(solution)/shard_map/all_to_all | solution.py:435
  50.3 0.7 %spread.1 = f32[32,1,2304]{2,1,0:T(1,128)} custom-call(f32[4,1,2304]{2,1,0:T(1,128)S(1)} %all_to_all.10.terms_ref), custom_call_target="tpu_custom_call" | custom-call | flops 1024 | bytes 1024 | tf_op jit(solution)/shard_map/spread/pallas_call | solution.py:423
  51.0 3.5 %all-to-all-start.1 = ((f32[32,1,2304]{2,1,0:T(1,128)}), f32[32,1,2304]{2,1,0:T(1,128)}, u32[]{:S(2)}, u32[]{:S(2)}) async-start(f32[32,1,2304]{2,1,0:T(1,128)} %spread.1), calls=%async_computation.1 | async-start | bytes 589824 | tf_op jit(solution)/shard_map/all_to_all | solution.py:437
  54.5 0.0 collective-permute-done.5.dqc_ref
  54.6 5.9 %own.1 = (bf16[256,1152]{1,0:T(8,128)(2,1)}, bf16[256,1152]{1,0:T(8,128)(2,1)}, bf16[256,1152]{1,0:T(8,128)(2,1)}) custom-call(s32[1]{0:T(128)S(6)} %sub.10.live_ref, bf16[256,1152]{1,0:T(8,128)(2,1)S(1)} %bitcast.25, bf16[256,1152]{1,0:T(8,128)(2,1)S(1)} %bitcast.29, bf16[256,1152]{1,0:T(8,128)(2,1)S(1)} %bitcast.20, ...), custom_call_target="tpu_custom_call" | custom-call | flops 99999997952 | bytes 1024 | tf_op jit(solution)/shard_map/own/pallas_call | solution.py:409
  60.5 5.5 %all-to-all-done.1.every_ref = f32[32,1,2304]{2,1,0:T(1,128)} async-done(((f32[32,1,2304]{2,1,0:T(1,128)}), f32[32,1,2304]{2,1,0:T(1,128)}, u32[]{:S(2)}, u32[]{:S(2)}) %all-to-all-start.1) | async-done | bytes 294944 | tf_op jit(solution)/shard_map/all_to_all | solution.py:437
  65.9 1.6 %gather.1 = f32[12,768]{1,0:T(8,128)} custom-call(f32[32,1,2304]{2,1,0:T(1,128)} %all-to-all-done.1.every_ref, bf16[256,1152]{1,0:T(8,128)(2,1)} %get-tuple-element.62._), custom_call_target="tpu_custom_call" | custom-call | flops 1024 | bytes 1024 | tf_op jit(solution)/shard_map/gather/pallas_call | solution.py:438
  (11 shorter events, 0.0 us)
Async XLA Ops:
  0.6 23.7 %collective-permute-start = (bf16[256,1152]{1,0:T(8,128)(2,1)}, bf16[256,1152]{1,0:T(8,128)(2,1)S(1)}, u32[]{:S(2)}, u32[]{:S(2)}) collective-permute-start(bf16[256,1152]{1,0:T(8,128)(2,1)} %bitcast.21), channel_id=1, source_target_pairs={{1,0},{2,1},{3,2},{4,3},{5,4},{6,5},{7,6},{9,8},{10,9},{11,10},{12... | collective-permute-start | bytes 1769480 | tf_op jit(solution)/shard_map/ppermute | solution.py:32
  6.1 18.3 %collective-permute-start.3 = (bf16[272,384]{1,0:T(8,128)(2,1)}, bf16[272,384]{1,0:T(8,128)(2,1)S(1)}, u32[]{:S(2)}, u32[]{:S(2)}) collective-permute-start(bf16[272,384]{1,0:T(8,128)(2,1)} %get-tuple-element.47), channel_id=1, source_target_pairs={{1,0},{2,1},{3,2},{4,3},{5,4},{6,5},{7,6},{9,8},{10,9},{11,10},{12... | collective-permute-start | bytes 626696 | tf_op jit(solution)/shard_map/ppermute | solution.py:32
  10.6 18.3 %collective-permute-start.2 = (bf16[272,384]{1,0:T(8,128)(2,1)}, bf16[272,384]{1,0:T(8,128)(2,1)}, u32[]{:S(2)}, u32[]{:S(2)}) collective-permute-start(bf16[272,384]{1,0:T(8,128)(2,1)} %get-tuple-element.46), channel_id=1, source_target_pairs={{1,0},{2,1},{3,2},{4,3},{5,4},{6,5},{7,6},{9,8},{10,9},{11,10},{12... | collective-permute-start | bytes 626696 | tf_op jit(solution)/shard_map/ppermute | solution.py:32
  11.9 12.4 %copy-start = (bf16[1,256,1152]{2,1,0:T(8,128)(2,1)S(1)}, bf16[1,256,1152]{2,1,0:T(8,128)(2,1)}, u32[]{:S(2)}) copy-start(bf16[1,256,1152]{2,1,0:T(8,128)(2,1)} %param.8) | copy-start | bytes 1769476
  11.9 12.4 %copy-start.1 = (bf16[1,256,1152]{2,1,0:T(8,128)(2,1)S(1)}, bf16[1,256,1152]{2,1,0:T(8,128)(2,1)}, u32[]{:S(2)}) copy-start(bf16[1,256,1152]{2,1,0:T(8,128)(2,1)} %param.7) | copy-start | bytes 1769476
  11.9 12.4 %copy-start.6 = (f32[12,768]{1,0:T(8,128)S(1)}, f32[12,768]{1,0:T(8,128)}, u32[]{:S(2)}) copy-start(f32[12,768]{1,0:T(8,128)} %get-tuple-element.35.bias_ref.w_ref) | copy-start | bytes 110596
  15.3 17.2 %collective-permute-start.1 = (bf16[272,384]{1,0:T(8,128)(2,1)}, bf16[272,384]{1,0:T(8,128)(2,1)S(1)}, u32[]{:S(2)}, u32[]{:S(2)}) collective-permute-start(bf16[272,384]{1,0:T(8,128)(2,1)} %get-tuple-element.45), channel_id=1, source_target_pairs={{1,0},{2,1},{3,2},{4,3},{5,4},{6,5},{7,6},{9,8},{10,9},{11,10},{12... | collective-permute-start | bytes 626696 | tf_op jit(solution)/shard_map/ppermute | solution.py:32
  28.9 12.9 %copy-start.3 = (f32[12,256,256]{2,1,0:T(8,128)S(1)}, f32[12,256,256]{2,1,0:T(8,128)}, u32[]{:S(2)}) copy-start(f32[12,256,256]{2,1,0:T(8,128)} %get-tuple-element.43.dp_ref) | copy-start | bytes 9437188
  31.4 10.4 %copy-start.2 = (f32[12,256,256]{2,1,0:T(8,128)S(1)}, f32[12,256,256]{2,1,0:T(8,128)}, u32[]{:S(2)}) copy-start(f32[12,256,256]{2,1,0:T(8,128)} %get-tuple-element.42.e_ref) | copy-start | bytes 9437188
  31.4 10.4 %copy-start.7 = (f32[3,16,256]{2,1,0:T(8,128)S(1)}, f32[3,16,256]{2,1,0:T(8,128)}, u32[]{:S(2)}) copy-start(f32[3,16,256]{2,1,0:T(8,128)} %get-tuple-element.44.near_ref) | copy-start | bytes 147460
  33.9 7.9 %collective-permute-start.4 = (bf16[16,1152]{1,0:T(8,128)(2,1)S(1)}, bf16[16,1152]{1,0:T(8,128)(2,1)S(1)}, u32[]{:S(2)}, u32[]{:S(2)}) collective-permute-start(bf16[16,1152]{1,0:T(8,128)(2,1)S(1)} %get-tuple-element.58), channel_id=1, source_target_pairs={{0,1},{1,2},{2,3},{3,4},{4,5},{5,6},{6,7},{8,9},{9,10},{10,11},{11... | collective-permute-start | bytes 110600 | tf_op jit(solution)/shard_map/ppermute | solution.py:32
  38.4 16.1 %collective-permute-start.5 = (bf16[256,1152]{1,0:T(8,128)(2,1)S(1)}, bf16[256,1152]{1,0:T(8,128)(2,1)}, u32[]{:S(2)}, u32[]{:S(2)}) collective-permute-start(bf16[256,1152]{1,0:T(8,128)(2,1)S(1)} %get-tuple-element.59), channel_id=1, source_target_pairs={{0,1},{1,2},{2,3},{3,4},{4,5},{5,6},{6,7},{8,9},{9,10},{10,11},{11... | collective-permute-start | bytes 1769480 | tf_op jit(solution)/shard_map/ppermute | solution.py:32
  41.8 12.7 %copy-start.4 = (bf16[1,256,1152]{2,1,0:T(8,128)(2,1)S(1)}, bf16[1,256,1152]{2,1,0:T(8,128)(2,1)}, u32[]{:S(2)}) copy-start(bf16[1,256,1152]{2,1,0:T(8,128)(2,1)} %param.6) | copy-start | bytes 1769476
  41.8 12.7 %copy-start.5 = (bf16[1,256,1152]{2,1,0:T(8,128)(2,1)S(1)}, bf16[1,256,1152]{2,1,0:T(8,128)(2,1)}, u32[]{:S(2)}) copy-start(bf16[1,256,1152]{2,1,0:T(8,128)(2,1)} %param.9) | copy-start | bytes 1769476
  43.1 0.6 copy-start.8
  51.0 15.0 %all-to-all-start.1 = ((f32[32,1,2304]{2,1,0:T(1,128)}), f32[32,1,2304]{2,1,0:T(1,128)}, u32[]{:S(2)}, u32[]{:S(2)}) async-start(f32[32,1,2304]{2,1,0:T(1,128)} %spread.1), calls=%async_computation.1 | async-start | bytes 589824 | tf_op jit(solution)/shard_map/all_to_all | solution.py:437
